TPU v7x, 128 devices: a whole 4x4x4 slice. The times are simulated.
128 devices in a mesh: pair: 8 (over y, x_hi), mat: 16 (over x_lo, z, core).
Axes of the slice: x: 4 (x_hi: 2, x_lo: 2; x = x_hi * 2 + x_lo), y: 4, z: 4, core: 2. Of those that a mesh axis runs over, the one named last changes fastest.
Arguments:
- operators: bfloat16 [32, 2048, 2048], P('pair', 'mat'), may hold values from -6 to 6
- left_rot: bfloat16 [2048, 2048], P('mat'), may hold values from -0.125 to 0.125
- right_rot: bfloat16 [2048, 2048], P('mat'), may hold values from -0.125 to 0.125
- integrals: float32 [1024, 1024], replicated, may hold values from -1.0606601 to 1.0606601
- pair_index: int32 [32], replicated, may hold values from 0 to 1023
- target_index: int32 [32], replicated, may hold values from 0 to 1023
Outputs:
- complement: bfloat16 [32, 2048, 2048], P('pair', None, 'mat')
All inputs are finite; a program needn't handle non-finite values.
Results may differ from a plain program's by a relative error of at most 0.0063.
Values may be sent and summed in bfloat16 or wider, within the bound.
No kernel may reach another device: no remote copies, remote signals or barrier semaphores. Data moves between devices by JAX's collectives and lax.ppermute only.
A program may use at most 192 MiB of HBM per device.

v0:
```python
import jax
import jax.numpy as jnp
from jax import lax
from jax.sharding import PartitionSpec as P


def selector(indices, count):
    return (indices[:, None] == jnp.arange(count, dtype=jnp.int32)[None, :]).astype(jnp.float32)


def shards(operators, left_rot, right_rot, integrals, pair_index, target_index):
    half_sum = jnp.einsum(
        "krj,jm->krm",
        operators,
        lax.all_gather(right_rot, "mat", axis=0, tiled=True),
        preferred_element_type=jnp.float32,
    )
    half_rot = half_sum.astype(jnp.bfloat16)
    columns = lax.all_to_all(half_rot, "mat", split_axis=2, concat_axis=1, tiled=True)
    rot_sum = jnp.einsum(
        "rm,krc->kmc",
        lax.all_gather(left_rot, "mat", axis=0, tiled=True),
        columns,
        preferred_element_type=jnp.float32,
    )
    rotated = rot_sum.astype(jnp.bfloat16)
    npairs = integrals.shape[0]
    ntgt = target_index.shape[0]
    tdev = ntgt // lax.axis_size("pair")
    owned = lax.dynamic_slice_in_dim(target_index, lax.axis_index("pair") * tdev, tdev, 0)
    rowsel = jnp.dot(selector(owned, npairs), integrals, precision=lax.Precision.HIGHEST)
    coupling = jnp.dot(
        rowsel, selector(pair_index, npairs).T, precision=lax.Precision.HIGHEST
    ).astype(jnp.bfloat16)
    summed = jnp.einsum(
        "tk,kmc->tmc",
        coupling,
        lax.all_gather(rotated, "pair", axis=0, tiled=True),
        preferred_element_type=jnp.float32,
    )
    return summed.astype(jnp.bfloat16)


def solution(mesh):
    in_specs = (P("pair", "mat", None), P("mat", None), P("mat", None), P(), P(), P())
    out_specs = P("pair", None, "mat")
    return jax.shard_map(shards, mesh=mesh, in_specs=in_specs, out_specs=out_specs, check_vma=False)
```

profile of v0, /device:TPU:1, one launch (start us, length us, event | category | flops | bytes accessed | tf_op | source)
XLA Modules:
  0.0 362.5 jit_solution(6267949380609808709)
XLA Ops:
  6.5 0.0 copy-start
  6.5 0.0 all-gather.4.cloned.1.call-start
  6.5 0.7 all-gather.4.cloned.1.call-update
  7.3 0.0 all-gather.6.cloned.1.call-start
  7.3 0.7 all-gather.6.cloned.1.call-update
  8.0 0.0 all-gather.8.cloned.1.call-start
  8.1 56.8 %all-gather.4.cloned.1.call-done = bf16[2048,2048]{1,0:T(8,128)(2,1)} async-done(((bf16[128,2048]{1,0:T(8,128)(2,1)}), bf16[2048,2048]{1,0:T(8,128)(2,1)}) %all-gather.4.cloned.1.call-update) | async-done | bytes 8388624 | tf_op jit(solution)/shard_map/all_gather | solution.py:15
  64.9 0.0 copy-done
  64.9 9.0 %fusion.6 = bf16[4,128,2048]{2,1,0:T(8,128)(2,1)} fusion(bf16[4,128,2048]{2,1,0:T(8,128)(2,1)S(1)} %copy-done, bf16[2048,2048]{1,0:T(8,128)(2,1)} %all-gather.4.cloned.1.call-done), kind=kOutput, calls=%fused_computation.6 | convolution fusion | flops 4296015872 | bytes 12582912 | tf_op jit(solution)/shard_map/krj,jm->krm/dot_general | solution.py:12
  73.9 4.4 %copy.15 = bf16[4,128,2048]{1,0,2:T(4,128)(2,1)} copy(bf16[4,128,2048]{2,1,0:T(8,128)(2,1)} %fusion.6) | data formatting | bytes 4194304 | tf_op jit(solution)/shard_map/convert_element_type | solution.py:18
  78.3 49.8 %all_to_all.18 = bf16[4,128,2048]{1,0,2:T(4,128)(2,1)S(1)} all-to-all(bf16[4,128,2048]{1,0,2:T(4,128)(2,1)} %copy.15), channel_id=1, replica_groups=mesh['pair'=8,'mat'=16] {'mat'}, dimensions={2} | all-to-all | bytes 4194304 | tf_op jit(solution)/shard_map/all_to_all | solution.py:19
  128.1 1.6 copy.16
  129.6 4.0 %copy.17 = bf16[4,16,128,128]{3,2,1,0:T(8,128)(2,1)} copy(bf16[4,16,128,128]{2,3,1,0:T(8,128)(2,1)} %bitcast.25) | data formatting | bytes 4194304 | tf_op jit(solution)/shard_map/all_to_all | solution.py:19
  133.6 8.6 %all-gather.6.cloned.1.call-done = bf16[2048,2048]{1,0:T(8,128)(2,1)} async-done(((bf16[128,2048]{1,0:T(8,128)(2,1)}), bf16[2048,2048]{1,0:T(8,128)(2,1)}) %all-gather.6.cloned.1.call-update) | async-done | bytes 8388624 | tf_op jit(solution)/shard_map/all_gather | solution.py:22
  142.2 9.9 %fusion.12 = bf16[4,2048,128]{1,2,0:T(8,128)(2,1)} fusion(bf16[4,2048,128]{2,1,0:T(8,128)(2,1)} %bitcast.26, bf16[2048,2048]{1,0:T(8,128)(2,1)} %all-gather.6.cloned.1.call-done), kind=kOutput, calls=%fused_computation.8 | convolution fusion | flops 4296015872 | bytes 12582912 | tf_op jit(solution)/shard_map/rm,krc->kmc/dot_general | solution.py:20
  152.1 3.9 %copy.19 = bf16[4,2048,128]{2,1,0:T(8,128)(2,1)} copy(bf16[4,2048,128]{1,2,0:T(8,128)(2,1)} %fusion.12) | data formatting | bytes 4194304 | tf_op jit(solution)/shard_map/convert_element_type | solution.py:26
  156.1 0.0 all-gather.8.cloned.1.call-update
  156.1 0.0 copy-done.1
  156.1 0.1 dynamic_slice.3
  156.2 3.6 fusion.20
  159.8 0.2 fusion.18
  160.0 179.1 %all-gather.8.cloned.1.call-done = bf16[32,2048,128]{2,1,0:T(8,128)(2,1)} async-done(((bf16[4,2048,128]{2,1,0:T(8,128)(2,1)}), bf16[32,2048,128]{2,1,0:T(8,128)(2,1)}) %all-gather.8.cloned.1.call-update) | async-done | bytes 16777232 | tf_op jit(solution)/shard_map/all_gather | solution.py:38
  339.1 15.3 %fusion.15 = bf16[4,2048,128]{2,0,1:T(4,128)(2,1)S(1)} fusion(bf16[4,32,1]{1,0,2:T(4,128)(2,1)S(1)} %fusion.18, bf16[32,2048,128]{2,1,0:T(8,128)(2,1)} %all-gather.8.cloned.1.call-done), kind=kOutput, calls=%fused_computation.9 | convolution fusion | flops 68157440 | bytes 18874624 | tf_op jit(solution)/shard_map/tk,kmc->tmc/dot_general | solution.py:35
  354.3 1.6 copy.21
  (3 shorter events, 0.0 us)
Async XLA Ops:
  6.5 58.4 %copy-start = (bf16[4,128,2048]{2,1,0:T(8,128)(2,1)S(1)}, bf16[4,128,2048]{2,1,0:T(8,128)(2,1)}, u32[]{:S(2)}) copy-start(bf16[4,128,2048]{2,1,0:T(8,128)(2,1)} %param.6) | copy-start | bytes 6291460
  6.5 58.4 %all-gather.4.cloned.1.call-start = ((), (), s32[]{:S(2)}) async-start(), calls=%async_computation.1 | async-start | bytes 8912896 | tf_op jit(solution)/shard_map/all_gather | solution.py:15
  7.3 135.0 %all-gather.6.cloned.1.call-start = ((), (), s32[]{:S(2)}) async-start(), calls=%async_computation.2 | async-start | bytes 8912896 | tf_op jit(solution)/shard_map/all_gather | solution.py:22
  8.0 331.1 %all-gather.8.cloned.1.call-start = ((), (), s32[]{:S(2)}) async-start(), calls=%async_computation.3 | async-start | bytes 18874368 | tf_op jit(solution)/shard_map/all_gather | solution.py:38
  152.1 4.0 %copy-start.1 = (s32[32]{0:T(128)S(1)}, s32[32]{0:T(128)}, u32[]{:S(2)}) copy-start(s32[32]{0:T(128)} %param.11) | copy-start | bytes 388
  156.1 3.7 %copy-start.2 = (s32[32]{0:T(128)S(1)}, s32[32]{0:T(128)}, u32[]{:S(2)}) copy-start(s32[32]{0:T(128)} %param.10) | copy-start | bytes 388
Sparse Core Ops, SparseCore 0:
  9.1 55.7 all-gather.3
  66.6 75.5 all-gather.5
  156.2 182.7 all-gather.7
where the time goes:
time: 363 us; the launch traced here: 362 us
  waiting for transfers between devices  246 us (68%)
  blocking collectives  49.8 us (14%)
  matrix products  38 us (10%)
  local copies, waits for them, and re-layouts  15.5 us (4%)
  between operations  13.1 us (4%)
    all_gather x1, waiting for transfers between devices, shards(): lax.all_gather(rotated, 'pair', axis=0, tiled=True)  179 us
    all_gather x1, waiting for transfers between devices, shards(): lax.all_gather(right_rot, 'mat', axis=0, tiled=True)  56.8 us
    all_to_all x1, blocking collectives, shards(): lax.all_to_all(half_rot, 'mat', split_axis=2, concat_axis=1, tiled=True)  49.8 us
    dot_general x1, matrix products, shards(): jnp.einsum('tk,kmc->tmc', coupling, lax.all_gather(rotated, 'pair', axis=...  15.3 us
    dot_general x1, matrix products, shards(): jnp.einsum('rm,krc->kmc', lax.all_gather(left_rot, 'mat', axis=0, tiled=T...  9.9 us
    dot_general x1, matrix products, shards(): jnp.einsum('krj,jm->krm', operators, lax.all_gather(right_rot, 'mat', axi...  9.03 us
    all_gather x1, waiting for transfers between devices, shards(): lax.all_gather(left_rot, 'mat', axis=0, tiled=True)  8.62 us
  transfers between devices with their start and end apart: 3, of which 3 were waited for; matrix products, arithmetic and copies ran while one was open for 6% of the time, Pallas kernels for 0%

commit v1 on v0

v1 whole, which is shorter than its diff:
```python
import jax
import jax.numpy as jnp
from jax import lax
from jax.sharding import Mesh, PartitionSpec as P

AXES = ("y", "xh", "xl", "z", "core")
PAIR = ("y", "xh")
MAT = ("xl", "z", "core")


def selector(indices, count):
    return (indices[:, None] == jnp.arange(count, dtype=jnp.int32)[None, :]).astype(jnp.float32)


def shards(operators, left_rot, right_rot, integrals, pair_index, target_index):
    right = lax.all_gather(right_rot, MAT, axis=0, tiled=True)
    left = lax.all_gather(left_rot, MAT, axis=0, tiled=True)
    pieces = operators.reshape(4, 8, 16, 2048).transpose(1, 0, 2, 3)
    pieces = lax.all_to_all(pieces, PAIR, 0, 0, tiled=True).reshape(512, 2048)
    npairs = integrals.shape[0]
    rowsel = jnp.dot(selector(target_index, npairs), integrals, precision=lax.Precision.HIGHEST)
    coupling = jnp.dot(
        rowsel, selector(pair_index, npairs).T, precision=lax.Precision.HIGHEST
    ).astype(jnp.bfloat16)
    spread = (coupling[:, None, :, None] * jnp.eye(16, dtype=jnp.bfloat16)[None, :, None, :]).reshape(512, 512)
    mixed = jnp.dot(spread, pieces, preferred_element_type=jnp.float32).astype(jnp.bfloat16)
    half = jnp.dot(mixed, right, preferred_element_type=jnp.float32).astype(jnp.bfloat16)
    blocks = half.reshape(8, 64, 16, 128).transpose(0, 2, 1, 3).reshape(128, 64, 128)
    columns = lax.all_to_all(blocks, AXES, 0, 0, tiled=True)
    columns = columns.reshape(8, 16, 4, 16, 128).transpose(2, 1, 0, 3, 4).reshape(4, 2048, 128)
    out = jnp.einsum("rm,trc->tmc", left, columns, preferred_element_type=jnp.float32)
    return out.astype(jnp.bfloat16)


def solution(mesh):
    fine = Mesh(mesh.devices.reshape(4, 2, 2, 4, 2), AXES)
    in_specs = (P(PAIR, MAT, None), P(MAT, None), P(MAT, None), P(), P(), P())
    out_specs = P(PAIR, None, MAT)
    return jax.shard_map(shards, mesh=fine, in_specs=in_specs, out_specs=out_specs, check_vma=False)
```

time: 363 us -> 184 us (0.51)
  waiting for transfers between devices: 246 us -> 69.9 us
  matrix products: 38 us -> 23.5 us
  starting transfers between devices: 0.08 us -> 7.65 us
    all_gather x3 -> x2, waiting for transfers between devices: 245 us -> 36.2 us  [the longest x1 18.8 us: shards(): right = lax.all_gather(right_rot, MAT, axis=0, tiled=True)]
    all_to_all x0 -> x1, waiting for transfers between devices: none -> 32.3 us  [shards(): pieces = lax.all_to_all(pieces, PAIR, 0, 0, tiled=True).reshape(512, 2048)]
    dot_general x4 -> x3, matrix products: 37.8 us -> 23.2 us  [the longest x1 10.3 us: shards(): jnp.dot(mixed, right, preferred_element_type=jnp.float32)]
    mul x0 -> x1, local copies, waits for them, and re-layouts: none -> 7.81 us  [shards(): coupling[:, None, :, None]]
    all_to_all x0 -> x1, starting transfers between devices: none -> 7.61 us  [shards(): pieces = lax.all_to_all(pieces, PAIR, 0, 0, tiled=True).reshape(512, 2048)]
    convert_element_type x3 -> x1, local copies, waits for them, and re-layouts: 9.88 us -> 3.93 us  [shards(): return out.astype(jnp.bfloat16)]
    all_to_all x2 -> x0, local copies, waits for them, and re-layouts: 5.55 us -> none  [shards(): lax.all_to_all(half_rot, 'mat', split_axis=2, concat_axis=1, tiled=True)]
    transpose x0 -> x2, local copies, waits for them, and re-layouts: none -> 3.76 us  [the longest x1 3.16 us: shards(): pieces = operators.reshape(4, 8, 16, 2048).transpose(1, 0, 2, 3)]
  transfers between devices with their start and end apart: 3 -> 3, of which waited for: 3 -> 3; matrix products, arithmetic and copies ran while one was open for 6% -> 17% of each run, Pallas kernels for 0% -> 0%
where the time goes in v1:
time: 184 us
  waiting for transfers between devices  69.9 us (38%)
  blocking collectives  48.5 us (26%)
  matrix products  23.5 us (13%)
  local copies, waits for them, and re-layouts  18.3 us (10%)
  between operations  13.5 us (7%)
  starting transfers between devices  7.65 us (4%)
  other arithmetic  2.29 us (1%)
    all_to_all x1, blocking collectives, shards(): columns = lax.all_to_all(blocks, AXES, 0, 0, tiled=True)  48.5 us
    all_to_all x1, waiting for transfers between devices, shards(): pieces = lax.all_to_all(pieces, PAIR, 0, 0, tiled=True).reshape(512, 2048)  32.3 us
    all_gather x1, waiting for transfers between devices, shards(): right = lax.all_gather(right_rot, MAT, axis=0, tiled=True)  18.8 us
    all_gather x1, waiting for transfers between devices, shards(): left = lax.all_gather(left_rot, MAT, axis=0, tiled=True)  17.4 us
    dot_general x1, matrix products, shards(): jnp.dot(mixed, right, preferred_element_type=jnp.float32)  10.3 us
    dot_general x1, matrix products, shards(): jnp.einsum('rm,trc->tmc', left, columns, preferred_element_type=jnp.float32)  9.05 us
    mul x1, local copies, waits for them, and re-layouts, shards(): coupling[:, None, :, None]  7.81 us
    all_to_all x1, starting transfers between devices, shards(): pieces = lax.all_to_all(pieces, PAIR, 0, 0, tiled=True).reshape(512, 2048)  7.61 us
  transfers between devices with their start and end apart: 3, of which 3 were waited for; matrix products, arithmetic and copies ran while one was open for 17% of the time, Pallas kernels for 0%

profile of v1, /device:TPU:1, one launch (start us, length us, event | category | flops | bytes accessed | tf_op | source)
XLA Modules:
  0.0 183.6 jit_solution(2122832208758578268)
XLA Ops:
  6.5 0.0 all-gather.3.cloned.1.call-start
  6.5 0.7 all-gather.3.cloned.1.call-update
  7.3 0.0 all-gather.5.cloned.1.call-start
  7.3 0.7 all-gather.5.cloned.1.call-update
  8.0 3.2 %copy.17 = bf16[8,4,16,2048]{3,2,1,0:T(8,128)(2,1)} copy(bf16[8,4,16,2048]{3,2,0,1:T(8,128)(2,1)} %bitcast.35) | data formatting | bytes 4194304 | tf_op jit(solution)/shard_map/transpose | solution.py:18
  11.2 0.0 copy-start
  11.2 7.6 %all-to-all-start = ((bf16[8,4,16,2048]{3,2,1,0:T(8,128)(2,1)}), bf16[8,4,16,2048]{3,2,1,0:T(8,128)(2,1)S(1)}, u32[]{:S(2)}, u32[]{:S(2)}) async-start(bf16[8,4,16,2048]{3,2,1,0:T(8,128)(2,1)} %copy.17), calls=%async_computation | async-start | bytes 4194304 | tf_op jit(solution)/shard_map/all_to_all | solution.py:19
  18.8 0.0 copy-done
  18.8 0.0 copy-start.1
  18.8 3.8 %fusion.9 = f32[32,1024]{1,0:T(8,128)S(1)} fusion(f32[1024,1024]{1,0:T(8,128)} %param.9, s32[32]{0:T(128)S(1)} %copy-done), kind=kOutput, calls=%fused_computation.11 | convolution fusion | flops 402685952 | bytes 4325504 | tf_op jit(solution)/shard_map/dot_general | solution.py:21
  22.7 0.0 copy-done.1
  22.7 0.3 convolution_convert_fusion.2
  22.9 2.3 %broadcast_multiply_fusion = bf16[32,16,32,16]{3,2,1,0:T(8,128)(2,1)} fusion(bf16[16,16]{1,0:T(8,128)(2,1)S(1)} %fusion.12, bf16[32,32]{1,0:T(8,128)(2,1)S(1)} %convolution_convert_fusion.2), kind=kLoop, calls=%fused_computation.6 | loop fusion | flops 262144 | bytes 526848 | tf_op jit(solution)/shard_map/mul | solution.py:25
  25.2 7.8 %mul.26 = bf16[512,512]{1,0:T(8,128)(2,1)S(1)} reshape(bf16[32,16,32,16]{3,2,1,0:T(8,128)(2,1)} %broadcast_multiply_fusion) | data formatting | bytes 1048576 | tf_op jit(solution)/shard_map/mul | solution.py:25
  33.0 32.3 %all-to-all-done = bf16[8,4,16,2048]{3,2,1,0:T(8,128)(2,1)S(1)} async-done(((bf16[8,4,16,2048]{3,2,1,0:T(8,128)(2,1)}), bf16[8,4,16,2048]{3,2,1,0:T(8,128)(2,1)S(1)}, u32[]{:S(2)}, u32[]{:S(2)}) %all-to-all-start) | async-done | bytes 2097184 | tf_op jit(solution)/shard_map/all_to_all | solution.py:19
  65.3 18.8 %all-gather.3.cloned.1.call-done = bf16[2048,2048]{1,0:T(8,128)(2,1)} async-done(((bf16[128,2048]{1,0:T(8,128)(2,1)}), bf16[2048,2048]{1,0:T(8,128)(2,1)}) %all-gather.3.cloned.1.call-update) | async-done | bytes 8388624 | tf_op jit(solution)/shard_map/all_gather | solution.py:16
  84.1 10.3 %fusion.8 = bf16[64,8,16,128]{3,1,2,0:T(8,128)(2,1)} fusion(bf16[2048,2048]{1,0:T(8,128)(2,1)} %all-gather.3.cloned.1.call-done, bf16[512,512]{1,0:T(8,128)(2,1)S(1)} %mul.26, bf16[512,2048]{1,0:T(8,128)(2,1)S(1)} %bitcast.36), kind=kOutput, calls=%fused_computation.7 | convolution fusion | flops 5370806272 | bytes 13107200 | tf_op jit(solution)/shard_map/dot_general | solution.py:27
  94.4 2.2 %copy.23 = bf16[64,8,16,128]{3,2,1,0:T(8,128)(2,1)S(1)} copy(bf16[64,8,16,128]{3,1,2,0:T(8,128)(2,1)} %fusion.8) | data formatting | bytes 4194304
  96.6 0.5 copy.18
  97.1 48.5 %all_to_all.10 = bf16[128,64,128]{2,1,0:T(8,128)(2,1)S(1)} all-to-all(bf16[128,64,128]{2,1,0:T(8,128)(2,1)S(1)} %bitcast.33), channel_id=1, replica_groups=mesh['y'=4,'xh'=2,'xl'=2,'z'=4,'core'=2] {'y','xh','xl','z','core'}, dimensions={0} | all-to-all | bytes 4194304 | tf_op jit(solution)/shard_map/all_to_all | solution.py:29
  145.7 0.6 copy.19
  146.3 17.4 %all-gather.5.cloned.1.call-done = bf16[2048,2048]{1,0:T(8,128)(2,1)} async-done(((bf16[128,2048]{1,0:T(8,128)(2,1)}), bf16[2048,2048]{1,0:T(8,128)(2,1)}) %all-gather.5.cloned.1.call-update) | async-done | bytes 8388624 | tf_op jit(solution)/shard_map/all_gather | solution.py:17
  163.7 9.0 %fusion.5 = bf16[4,2048,128]{1,2,0:T(8,128)(2,1)} fusion(bf16[4,2048,128]{2,1,0:T(8,128)(2,1)S(1)} %bitcast.37, bf16[2048,2048]{1,0:T(8,128)(2,1)} %all-gather.5.cloned.1.call-done), kind=kOutput, calls=%fused_computation.5 | convolution fusion | flops 4296015872 | bytes 12582912 | tf_op jit(solution)/shard_map/rm,trc->tmc/dot_general | solution.py:31
  172.8 3.9 %copy.21 = bf16[4,2048,128]{2,1,0:T(8,128)(2,1)} copy(bf16[4,2048,128]{1,2,0:T(8,128)(2,1)} %fusion.5) | data formatting | bytes 4194304 | tf_op jit(solution)/shard_map/convert_element_type | solution.py:32
  (1 shorter events, 0.0 us)
Async XLA Ops:
  6.5 77.6 %all-gather.3.cloned.1.call-start = ((), (), s32[]{:S(2)}) async-start(), calls=%async_computation.2 | async-start | bytes 8912896 | tf_op jit(solution)/shard_map/all_gather | solution.py:16
  7.3 156.5 %all-gather.5.cloned.1.call-start = ((), (), s32[]{:S(2)}) async-start(), calls=%async_computation.3 | async-start | bytes 8912896 | tf_op jit(solution)/shard_map/all_gather | solution.py:17
  11.2 7.6 %copy-start = (s32[32]{0:T(128)S(1)}, s32[32]{0:T(128)}, u32[]{:S(2)}) copy-start(s32[32]{0:T(128)} %param.11) | copy-start | bytes 388
  11.2 54.1 %all-to-all-start = ((bf16[8,4,16,2048]{3,2,1,0:T(8,128)(2,1)}), bf16[8,4,16,2048]{3,2,1,0:T(8,128)(2,1)S(1)}, u32[]{:S(2)}, u32[]{:S(2)}) async-start(bf16[8,4,16,2048]{3,2,1,0:T(8,128)(2,1)} %copy.17), calls=%async_computation | async-start | bytes 4194304 | tf_op jit(solution)/shard_map/all_to_all | solution.py:19
  18.8 3.9 %copy-start.1 = (s32[32]{0:T(128)S(1)}, s32[32]{0:T(128)}, u32[]{:S(2)}) copy-start(s32[32]{0:T(128)} %param.10) | copy-start | bytes 388
Sparse Core Ops, SparseCore 0:
  9.1 74.9 all-gather.2
  85.8 77.8 all-gather.4

commit v2 on v1

v2 whole, which is shorter than its diff:
```python
import jax
import jax.numpy as jnp
from jax import lax
from jax.experimental import pallas as pl
from jax.experimental.pallas import tpu as pltpu
from jax.sharding import Mesh, PartitionSpec as P

AXES = ("y", "xh", "xl", "z", "core")
PAIR = ("y", "xh")
MAT = ("xl", "z", "core")
BF = jnp.bfloat16
F32 = jnp.float32
HALF, FINAL = 56, 56


def place(x, y, z, core):
    x, y, z = x % 4, y % 4, z % 4
    return (y * 2 + x // 2) * 16 + ((x % 2) * 4 + z) * 2 + core


def send(value, move):
    moves = [
        (place(x, y, z, core), place(*move(x, y, z, core)))
        for x in range(4)
        for y in range(4)
        for z in range(4)
        for core in range(2)
    ]
    return lax.ppermute(value, AXES, moves)


def swap_core(value):
    return send(value, lambda x, y, z, core: (x, y, z, 1 - core))


def shift(value, dx=0, dy=0, dz=0):
    def move(x, y, z, core):
        way = 1 - 2 * core
        return x + way * dx, y + way * dy, z + way * dz, core

    return send(value, move)


def selector(indices, count):
    return (indices[:, None] == jnp.arange(count, dtype=jnp.int32)[None, :]).astype(F32)


def spread_coupling(integrals, pair_index, target_index):
    npairs = integrals.shape[0]
    rowsel = jnp.dot(selector(target_index, npairs), integrals, precision=lax.Precision.HIGHEST)
    coupling = jnp.dot(rowsel, selector(pair_index, npairs).T, precision=lax.Precision.HIGHEST).astype(BF)
    wide = selector(jnp.arange(512, dtype=jnp.int32) // 16, 32).astype(BF)
    rows = jnp.dot(wide, coupling, preferred_element_type=F32).astype(BF)
    full = jnp.dot(rows, wide.T, preferred_element_type=F32).astype(BF)
    i = lax.broadcasted_iota(jnp.int32, (512, 512), 0) % 16
    j = lax.broadcasted_iota(jnp.int32, (512, 512), 1) % 16
    return jnp.where(i == j, full, jnp.zeros_like(full))


def mix_kernel(spread, *refs):
    *parts, out = refs
    width = out.shape[1] // len(parts)
    for n, part in enumerate(parts):
        out[:, n * width : (n + 1) * width] = jnp.dot(spread[...], part[...], preferred_element_type=F32).astype(BF)


def mix(spread, parts):
    return pl.pallas_call(
        mix_kernel,
        out_shape=jax.ShapeDtypeStruct((512, 2048), BF),
        compiler_params=pltpu.CompilerParams(vmem_limit_bytes=16 << 20),
        name="mix",
    )(spread, *parts)


def half_kernel(order, rows, *refs):
    *rights, out, natural = refs
    for n, right in enumerate(rights):
        natural[pl.ds(pl.multiple_of(order[n] * 128, 128), 128), :] = right[...]
    total = jnp.dot(rows[...], natural[...], preferred_element_type=F32).astype(BF)
    for p in range(8):
        for m in range(out.shape[1]):
            for t in range(4):
                top = (p * 4 + t) * 16
                out[p, m, :, t * 128 : t * 128 + 128] = total[top : top + 16, m * 128 : m * 128 + 128]


def half_rotate(order, rows, rights):
    width = 512
    return pl.pallas_call(
        half_kernel,
        grid_spec=pltpu.PrefetchScalarGridSpec(
            num_scalar_prefetch=1,
            grid=(2048 // width,),
            in_specs=[pl.BlockSpec((512, 2048), lambda i, o: (0, 0))]
            + [pl.BlockSpec((128, width), lambda i, o: (0, i)) for _ in rights],
            out_specs=pl.BlockSpec((8, width // 128, 16, 512), lambda i, o: (0, i, 0, 0)),
            scratch_shapes=[pltpu.VMEM((2048, width), BF)],
        ),
        out_shape=jax.ShapeDtypeStruct((8, 16, 16, 512), BF),
        compiler_params=pltpu.CompilerParams(vmem_limit_bytes=HALF << 20),
        name="half",
    )(order, rows, *rights)


def final_kernel(order, *refs):
    *lefts, columns, out, rows = refs

    @pl.when(pl.program_id(0) == 0)
    def _():
        for n in range(len(lefts)):
            for chip in range(4):
                for p in range(2):
                    top = n * 128 + chip * 32 + p * 16
                    pair, place = order[2 * n] * 2 + p, order[2 * len(lefts) + (n // 4) * 4 + chip]
                    rows[top : top + 16, :] = columns[pair, place]

    left = jnp.concatenate([piece[...] for piece in lefts], axis=0)
    total = lax.dot_general(left, rows[...], (((0,), (0,)), ((), ())), preferred_element_type=F32).astype(BF)
    for t in range(4):
        out[t] = total[:, t * 128 : t * 128 + 128]


def final_rotate(order, lefts, columns):
    height = 512
    return pl.pallas_call(
        final_kernel,
        grid_spec=pltpu.PrefetchScalarGridSpec(
            num_scalar_prefetch=1,
            grid=(2048 // height,),
            in_specs=[pl.BlockSpec((128, height), lambda i, o: (0, i)) for _ in lefts]
            + [pl.BlockSpec((8, 16, 16, 512), lambda i, o: (0, 0, 0, 0))],
            out_specs=pl.BlockSpec((4, height, 128), lambda i, o: (0, i, 0)),
            scratch_shapes=[pltpu.VMEM((2048, 512), BF)],
        ),
        out_shape=jax.ShapeDtypeStruct((4, 2048, 128), BF),
        compiler_params=pltpu.CompilerParams(vmem_limit_bytes=FINAL << 20),
        name="final",
    )(order, *lefts, columns)


def after(*values):
    return lax.optimization_barrier(values)


def shards(operators, left_rot, right_rot, integrals, pair_index, target_index):
    core = lax.axis_index("core")
    y, xl, z = lax.axis_index("y"), lax.axis_index("xl"), lax.axis_index("z")

    near = [right_rot] + [shift(right_rot, dz=dz) for dz in (1, -1, 2)]
    there = shift(right_rot, dx=1)
    rights = near + [there, shift(there, dz=1), shift(there, dz=-1), shift(near[3], dx=1)]
    left_rot, there = after(left_rot, there)
    quarter = lax.dynamic_slice_in_dim(left_rot, y * 32, 32, 0)
    strip = jnp.concatenate([quarter, shift(quarter, dz=1), shift(quarter, dz=-1), shift(quarter, dz=2)])
    pieces = operators.reshape(4, 8, 16, 2048).transpose(1, 0, 2, 3)
    pieces = lax.all_to_all(pieces, PAIR, 0, 0, tiled=True).reshape(512, 2048)
    spread = spread_coupling(integrals, pair_index, target_index)
    lefts = [strip, shift(strip, dy=1), shift(strip, dy=-1), shift(strip, dy=2)]
    rights += [swap_core(right) for right in rights]

    rows = mix(spread, [pieces])

    def along_z(xl, core):
        way = 1 - 2 * core
        return [(xl * 4 + chip % 4) * 2 + core for chip in (z, z + 4 - way, z + 4 + way, z + 2)]

    places = along_z(xl, core) + along_z(1 - xl, core) + along_z(xl, 1 - core) + along_z(1 - xl, 1 - core)
    half = half_rotate(jnp.stack(places), rows, rights)
    across = shift(strip, dx=1)
    *lefts, across, half = after(*lefts, across, half)
    columns = lax.all_to_all(half.reshape(128, 16, 512), AXES, 0, 0, tiled=True)
    lefts += [across, shift(lefts[1], dx=1), shift(across, dy=-1), shift(lefts[3], dx=1)]
    lefts += [swap_core(left) for left in lefts]
    return final_rotate(jnp.stack(left_order(y, core) + places), lefts, columns.reshape(8, 16, 16, 512))


def left_order(y, core):
    order = []
    for side in (core, 1 - core):
        way = 1 - 2 * side
        for _ in range(2):
            for row in (y, (y + 4 - way) % 4, (y + 4 + way) % 4, (y + 2) % 4):
                order += [row, row]
    return order


def solution(mesh):
    fine = Mesh(mesh.devices.reshape(4, 2, 2, 4, 2), AXES)
    in_specs = (P(PAIR, MAT, None), P(MAT, None), P(MAT, None), P(), P(), P())
    out_specs = P(PAIR, None, MAT)
    return jax.shard_map(shards, mesh=fine, in_specs=in_specs, out_specs=out_specs, check_vma=False)
```

time: 184 us -> 149 us (0.81)
  blocking collectives: 48.5 us -> 0 us
  starting transfers between devices: 7.65 us -> 43.4 us
  Pallas kernels: 0 us -> 20.8 us
  matrix products: 23.5 us -> 4.58 us
  between operations: 13.5 us -> 0.36 us
  local copies, waits for them, and re-layouts: 18.3 us -> 7.48 us
    ppermute x0 -> x33, waiting for transfers between devices: none -> 70.3 us  [send(): return lax.ppermute(value, AXES, moves)]
    all_to_all x1 -> x0, blocking collectives: 48.5 us -> none  [shards(): columns = lax.all_to_all(blocks, AXES, 0, 0, tiled=True)]
    all_gather x2 -> x0, waiting for transfers between devices: 36.2 us -> none  [the longest x1 18.8 us: shards(): right = lax.all_gather(right_rot, MAT, axis=0, tiled=True)]
    all_to_all x1, waiting for transfers between devices: 32.3 us -> 0.01 us  [shards(): pieces = lax.all_to_all(pieces, PAIR, 0, 0, tiled=True).reshape(512, 2048)]
    ppermute x0 -> x33, starting transfers between devices: none -> 31.8 us  [send(): return lax.ppermute(value, AXES, moves)]
    pallas_call x0 -> x3, Pallas kernels: none -> 20.8 us  [the longest x1 9.88 us: half_rotate(): pl.pallas_call(half_kernel, grid_spec=pltpu.PrefetchScalarGridSpec(num_sc...]
    dot_general x4 -> x3, matrix products: 23.5 us -> 4.58 us  [the longest x1 3.84 us: spread_coupling(): jnp.dot(selector(target_index, npairs), integrals, precision=lax.Precisio...]
    mul x1 -> x0, local copies, waits for them, and re-layouts: 7.81 us -> none  [shards(): coupling[:, None, :, None]]
  transfers between devices with their start and end apart: 3 -> 35, of which waited for: 3 -> 12; matrix products, arithmetic and copies ran while one was open for 17% -> 7% of each run, Pallas kernels for 0% -> 7%
where the time goes in v2:
time: 149 us
  waiting for transfers between devices  70.3 us (47%)
  starting transfers between devices  43.4 us (29%)
  Pallas kernels  20.8 us (14%)
  local copies, waits for them, and re-layouts  7.48 us (5%)
  matrix products  4.58 us (3%)
  other arithmetic  1.75 us (1%)
    ppermute x33, waiting for transfers between devices, send(): return lax.ppermute(value, AXES, moves)  70.3 us
    ppermute x33, starting transfers between devices, send(): return lax.ppermute(value, AXES, moves)  31.8 us
    pallas_call x1, Pallas kernels, half_rotate(): pl.pallas_call(half_kernel, grid_spec=pltpu.PrefetchScalarGridSpec(num_sc...  9.88 us
    pallas_call x1, Pallas kernels, final_rotate(): pl.pallas_call(final_kernel, grid_spec=pltpu.PrefetchScalarGridSpec(num_s...  9.71 us
    all_to_all x1, starting transfers between devices, shards(): pieces = lax.all_to_all(pieces, PAIR, 0, 0, tiled=True).reshape(512, 2048)  6.49 us
    all_to_all x1, starting transfers between devices, shards(): columns = lax.all_to_all(half.reshape(128, 16, 512), AXES, 0, 0, tiled=True)  5.09 us
    dot_general x1, matrix products, spread_coupling(): jnp.dot(selector(target_index, npairs), integrals, precision=lax.Precisio...  3.84 us
    reshape x1, local copies, waits for them, and re-layouts, shards(): pieces = operators.reshape(4, 8, 16, 2048).transpose(1, 0, 2, 3)  3.16 us
  transfers between devices with their start and end apart: 35, of which 12 were waited for; matrix products, arithmetic and copies ran while one was open for 7% of the time, Pallas kernels for 7%

profile of v2, /device:TPU:1, one launch (start us, length us, event | category | flops | bytes accessed | tf_op | source)
XLA Modules:
  0.0 148.7 jit_solution(4335068866891130376)
XLA Ops:
  0.0 3.3 %collective-permute-start = (bf16[128,2048]{1,0:T(8,128)(2,1)}, bf16[128,2048]{1,0:T(8,128)(2,1)S(1)}, u32[]{:S(2)}, u32[]{:S(2)}) collective-permute-start(bf16[128,2048]{1,0:T(8,128)(2,1)} %refs_0_.1), channel_id=1, source_target_pairs={{0,8},{1,25},{2,10},{3,27},{4,12},{5,29},{6,14},{7,31},{32,40},{33... | collective-permute-start | bytes 1572872 | tf_op jit(solution)/shard_map/ppermute | solution.py:29
  3.3 3.6 %collective-permute-start.10 = (bf16[128,2048]{1,0:T(8,128)(2,1)}, bf16[128,2048]{1,0:T(8,128)(2,1)}, u32[]{:S(2)}, u32[]{:S(2)}) collective-permute-start(bf16[128,2048]{1,0:T(8,128)(2,1)} %refs_0_.1), channel_id=1, source_target_pairs={{0,4},{1,5},{2,6},{3,7},{4,0},{5,1},{6,2},{7,3},{32,36},{33,37},{3... | collective-permute-start | bytes 1572872 | tf_op jit(solution)/shard_map/ppermute | solution.py:29
  8.4 1.7 %collective-permute-start.14 = (bf16[128,2048]{1,0:T(8,128)(2,1)}, bf16[128,2048]{1,0:T(8,128)(2,1)}, u32[]{:S(2)}, u32[]{:S(2)}) collective-permute-start(bf16[128,2048]{1,0:T(8,128)(2,1)} %refs_0_.1), channel_id=1, source_target_pairs={{0,1},{1,0},{2,3},{3,2},{4,5},{5,4},{6,7},{7,6},{32,33},{33,32},{3... | collective-permute-start | bytes 1572872 | tf_op jit(solution)/shard_map/ppermute | solution.py:29
  10.1 3.2 %copy.9 = bf16[4,8,16,2048]{3,2,0,1:T(8,128)(2,1)} copy(bf16[4,8,16,2048]{3,2,1,0:T(8,128)(2,1)} %bitcast.36) | data formatting | bytes 4194304 | tf_op jit(solution)/shard_map/reshape | solution.py:156
  13.3 6.5 %all-to-all-start = ((bf16[8,4,16,2048]{3,2,1,0:T(8,128)(2,1)}), bf16[8,4,16,2048]{3,2,1,0:T(8,128)(2,1)S(1)}, u32[]{:S(2)}, u32[]{:S(2)}) async-start(bf16[8,4,16,2048]{3,2,1,0:T(8,128)(2,1)} %bitcast.35), calls=%async_computation | async-start | bytes 4194304 | tf_op jit(solution)/shard_map/all_to_all | solution.py:157
  21.3 10.3 %collective-permute-done.8.refs_1_ = bf16[128,2048]{1,0:T(8,128)(2,1)} collective-permute-done((bf16[128,2048]{1,0:T(8,128)(2,1)}, bf16[128,2048]{1,0:T(8,128)(2,1)}, u32[]{:S(2)}, u32[]{:S(2)}) %collective-permute-start.8) | collective-permute-done | bytes 524320 | tf_op jit(solution)/shard_map/ppermute | solution.py:29
  32.3 2.3 %collective-permute-start.1 = (bf16[32,2048]{1,0:T(8,128)(2,1)S(1)}, bf16[32,2048]{1,0:T(8,128)(2,1)S(1)}, u32[]{:S(2)}, u32[]{:S(2)}) collective-permute-start(bf16[32,2048]{1,0:T(8,128)(2,1)S(1)} %constant_dynamic-slice_fusion), channel_id=1, source_target_pairs={{0,2},{1,7},{2,4},{3,1},{4,6},{5,3},{6,0},{7,5},{32,34},{33,39},{3... | collective-permute-start | bytes 393224 | tf_op jit(solution)/shard_map/ppermute | solution.py:29
  34.6 9.8 %collective-permute-done.1 = bf16[32,2048]{1,0:T(8,128)(2,1)S(1)} collective-permute-done((bf16[32,2048]{1,0:T(8,128)(2,1)S(1)}, bf16[32,2048]{1,0:T(8,128)(2,1)S(1)}, u32[]{:S(2)}, u32[]{:S(2)}) %collective-permute-start.1) | collective-permute-done | bytes 131104 | tf_op jit(solution)/shard_map/ppermute | solution.py:29
  44.6 5.2 %collective-permute-done.2 = bf16[32,2048]{1,0:T(8,128)(2,1)S(1)} collective-permute-done((bf16[32,2048]{1,0:T(8,128)(2,1)S(1)}, bf16[32,2048]{1,0:T(8,128)(2,1)S(1)}, u32[]{:S(2)}, u32[]{:S(2)}) %collective-permute-start.2) | collective-permute-done | bytes 131104 | tf_op jit(solution)/shard_map/ppermute | solution.py:29
  50.5 5.6 %collective-permute-done.3 = bf16[32,2048]{1,0:T(8,128)(2,1)} collective-permute-done((bf16[32,2048]{1,0:T(8,128)(2,1)S(1)}, bf16[32,2048]{1,0:T(8,128)(2,1)}, u32[]{:S(2)}, u32[]{:S(2)}) %collective-permute-start.3) | collective-permute-done | bytes 131104 | tf_op jit(solution)/shard_map/ppermute | solution.py:29
  57.2 3.8 %fusion.3 = f32[32,1024]{1,0:T(8,128)S(1)} fusion(f32[1024,1024]{1,0:T(8,128)} %param.9, s32[32]{0:T(128)S(1)} %copy-done.10), kind=kOutput, calls=%fused_computation.12 | convolution fusion | flops 402685952 | bytes 4325504 | tf_op jit(solution)/shard_map/dot_general | solution.py:50
  61.1 1.7 %pad_maximum_fusion.refs_0_ = bf16[128,2048]{1,0:T(8,128)(2,1)} fusion(bf16[32,2048]{1,0:T(8,128)(2,1)} %collective-permute-done.3, bf16[32,2048]{1,0:T(8,128)(2,1)S(1)} %collective-permute-done.2, bf16[32,2048]{1,0:T(8,128)(2,1)S(1)} %collective-permute-done.1, bf16[32,2048]{1,0:T(8,128)(2,1)S(1)} %constant_dynamic-slice_fusion), kind=kLoop, calls=%fused_computation.6 | loop fusion | flops 2097152 | bytes 1048576 | tf_op jit(solution)/shard_map/concatenate | solution.py:155
  62.8 2.7 %collective-permute-start.4 = (bf16[128,2048]{1,0:T(8,128)(2,1)}, bf16[128,2048]{1,0:T(8,128)(2,1)}, u32[]{:S(2)}, u32[]{:S(2)}) collective-permute-start(bf16[128,2048]{1,0:T(8,128)(2,1)} %pad_maximum_fusion.refs_0_), channel_id=1, source_target_pairs={{0,32},{1,97},{2,34},{3,99},{4,36},{5,101},{6,38},{7,103},{32,64},... | collective-permute-start | bytes 1572872 | tf_op jit(solution)/shard_map/ppermute | solution.py:29
  65.6 1.6 %collective-permute-start.6 = (bf16[128,2048]{1,0:T(8,128)(2,1)}, bf16[128,2048]{1,0:T(8,128)(2,1)}, u32[]{:S(2)}, u32[]{:S(2)}) collective-permute-start(bf16[128,2048]{1,0:T(8,128)(2,1)} %pad_maximum_fusion.refs_0_), channel_id=1, source_target_pairs={{0,64},{1,65},{2,66},{3,67},{4,68},{5,69},{6,70},{7,71},{32,96},{3... | collective-permute-start | bytes 1572872 | tf_op jit(solution)/shard_map/ppermute | solution.py:29
  72.3 9.9 %half.1 = bf16[8,16,16,512]{3,2,1,0:T(8,128)(2,1)} custom-call(s32[16]{0:T(128)} %stack.137.order, bf16[512,2048]{1,0:T(8,128)(2,1)} %copy-done.1, bf16[128,2048]{1,0:T(8,128)(2,1)} %refs_0_.1, bf16[128,2048]{1,0:T(8,128)(2,1)} %collective-permute-done.8.refs_1_, bf16[128,2048]{1,0:T(8,128)(2,1)} %collective-permute-done.9.refs_2_, ...), custom_call_target="tpu_custom_call" | custom-call | tf_op jit(solution)/shard_map/half/pallas_call | solution.py:90
  82.2 5.5 %collective-permute-done.4.refs_1_ = bf16[128,2048]{1,0:T(8,128)(2,1)} collective-permute-done((bf16[128,2048]{1,0:T(8,128)(2,1)}, bf16[128,2048]{1,0:T(8,128)(2,1)}, u32[]{:S(2)}, u32[]{:S(2)}) %collective-permute-start.4) | collective-permute-done | bytes 524320 | tf_op jit(solution)/shard_map/ppermute | solution.py:29
  87.7 3.2 %collective-permute-done.6.refs_3_ = bf16[128,2048]{1,0:T(8,128)(2,1)} collective-permute-done((bf16[128,2048]{1,0:T(8,128)(2,1)}, bf16[128,2048]{1,0:T(8,128)(2,1)}, u32[]{:S(2)}, u32[]{:S(2)}) %collective-permute-start.6) | collective-permute-done | bytes 524320 | tf_op jit(solution)/shard_map/ppermute | solution.py:29
  90.9 5.1 %all-to-all-start.1 = ((bf16[128,16,512]{2,1,0:T(8,128)(2,1)}), bf16[128,16,512]{2,1,0:T(8,128)(2,1)S(1)}, u32[]{:S(2)}, u32[]{:S(2)}) async-start(bf16[128,16,512]{2,1,0:T(8,128)(2,1)} %bitcast.33), calls=%async_computation.1 | async-start | bytes 4194304 | tf_op jit(solution)/shard_map/all_to_all | solution.py:172
  96.0 2.7 %collective-permute-start.22 = (bf16[128,2048]{1,0:T(8,128)(2,1)}, bf16[128,2048]{1,0:T(8,128)(2,1)S(1)}, u32[]{:S(2)}, u32[]{:S(2)}) collective-permute-start(bf16[128,2048]{1,0:T(8,128)(2,1)} %collective-permute-done.4.refs_1_), channel_id=1, source_target_pairs={{0,8},{1,25},{2,10},{3,27},{4,12},{5,29},{6,14},{7,31},{32,40},{33... | collective-permute-start | bytes 1572872 | tf_op jit(solution)/shard_map/ppermute | solution.py:29
  100.4 1.9 %collective-permute-start.25 = (bf16[128,2048]{1,0:T(8,128)(2,1)}, bf16[128,2048]{1,0:T(8,128)(2,1)}, u32[]{:S(2)}, u32[]{:S(2)}) collective-permute-start(bf16[128,2048]{1,0:T(8,128)(2,1)} %pad_maximum_fusion.refs_0_), channel_id=1, source_target_pairs={{0,1},{1,0},{2,3},{3,2},{4,5},{5,4},{6,7},{7,6},{32,33},{33,32},{3... | collective-permute-start | bytes 1572872 | tf_op jit(solution)/shard_map/ppermute | solution.py:29
  102.3 23.8 %collective-permute-done.22.refs_5_ = bf16[128,2048]{1,0:T(8,128)(2,1)S(1)} collective-permute-done((bf16[128,2048]{1,0:T(8,128)(2,1)}, bf16[128,2048]{1,0:T(8,128)(2,1)S(1)}, u32[]{:S(2)}, u32[]{:S(2)}) %collective-permute-start.22) | collective-permute-done | bytes 524320 | tf_op jit(solution)/shard_map/ppermute | solution.py:29
  127.8 4.0 %collective-permute-done.24.refs_7_ = bf16[128,2048]{1,0:T(8,128)(2,1)} collective-permute-done((bf16[128,2048]{1,0:T(8,128)(2,1)}, bf16[128,2048]{1,0:T(8,128)(2,1)}, u32[]{:S(2)}, u32[]{:S(2)}) %collective-permute-start.24) | collective-permute-done | bytes 524320 | tf_op jit(solution)/shard_map/ppermute | solution.py:29
  131.8 1.6 %collective-permute-start.29 = (bf16[128,2048]{1,0:T(8,128)(2,1)}, bf16[128,2048]{1,0:T(8,128)(2,1)}, u32[]{:S(2)}, u32[]{:S(2)}) collective-permute-start(bf16[128,2048]{1,0:T(8,128)(2,1)} %collective-permute-done.7.refs_4_), channel_id=1, source_target_pairs={{0,1},{1,0},{2,3},{3,2},{4,5},{5,4},{6,7},{7,6},{32,33},{33,32},{3... | collective-permute-start | bytes 1572872 | tf_op jit(solution)/shard_map/ppermute | solution.py:29
  138.9 9.7 %final.1 = bf16[4,2048,128]{2,1,0:T(8,128)(2,1)} custom-call(s32[48]{0:T(128)} %stack.136.order, bf16[128,2048]{1,0:T(8,128)(2,1)} %pad_maximum_fusion.refs_0_, bf16[128,2048]{1,0:T(8,128)(2,1)} %collective-permute-done.4.refs_1_, bf16[128,2048]{1,0:T(8,128)(2,1)} %collective-permute-done.5.refs_2_, bf16[128,2048]{1,0:T(8,128)(2,1)} %collective-permute-done.6.refs_3_, ...), custom_call_target="tpu_custom_call" | custom-call | tf_op jit(solution)/shard_map/final/pallas_call | solution.py:126
  (84 shorter events, 19.6 us)
Async XLA Ops:
  0.0 19.8 %collective-permute-start = (bf16[128,2048]{1,0:T(8,128)(2,1)}, bf16[128,2048]{1,0:T(8,128)(2,1)S(1)}, u32[]{:S(2)}, u32[]{:S(2)}) collective-permute-start(bf16[128,2048]{1,0:T(8,128)(2,1)} %refs_0_.1), channel_id=1, source_target_pairs={{0,8},{1,25},{2,10},{3,27},{4,12},{5,29},{6,14},{7,31},{32,40},{33... | collective-permute-start | bytes 1572872 | tf_op jit(solution)/shard_map/ppermute | solution.py:29
  3.3 16.6 %collective-permute-start.10 = (bf16[128,2048]{1,0:T(8,128)(2,1)}, bf16[128,2048]{1,0:T(8,128)(2,1)}, u32[]{:S(2)}, u32[]{:S(2)}) collective-permute-start(bf16[128,2048]{1,0:T(8,128)(2,1)} %refs_0_.1), channel_id=1, source_target_pairs={{0,4},{1,5},{2,6},{3,7},{4,0},{5,1},{6,2},{7,3},{32,36},{33,37},{3... | collective-permute-start | bytes 1572872 | tf_op jit(solution)/shard_map/ppermute | solution.py:29
  6.9 24.7 %collective-permute-start.8 = (bf16[128,2048]{1,0:T(8,128)(2,1)}, bf16[128,2048]{1,0:T(8,128)(2,1)}, u32[]{:S(2)}, u32[]{:S(2)}) collective-permute-start(bf16[128,2048]{1,0:T(8,128)(2,1)} %refs_0_.1), channel_id=1, source_target_pairs={{0,2},{1,7},{2,4},{3,1},{4,6},{5,3},{6,0},{7,5},{32,34},{33,39},{3... | collective-permute-start | bytes 1572872 | tf_op jit(solution)/shard_map/ppermute | solution.py:29
  7.3 24.2 %collective-permute-start.9 = (bf16[128,2048]{1,0:T(8,128)(2,1)}, bf16[128,2048]{1,0:T(8,128)(2,1)}, u32[]{:S(2)}, u32[]{:S(2)}) collective-permute-start(bf16[128,2048]{1,0:T(8,128)(2,1)} %refs_0_.1), channel_id=1, source_target_pairs={{0,6},{1,3},{2,0},{3,5},{4,2},{5,7},{6,4},{7,1},{32,38},{33,35},{3... | collective-permute-start | bytes 1572872 | tf_op jit(solution)/shard_map/ppermute | solution.py:29
  8.4 23.9 %collective-permute-start.14 = (bf16[128,2048]{1,0:T(8,128)(2,1)}, bf16[128,2048]{1,0:T(8,128)(2,1)}, u32[]{:S(2)}, u32[]{:S(2)}) collective-permute-start(bf16[128,2048]{1,0:T(8,128)(2,1)} %refs_0_.1), channel_id=1, source_target_pairs={{0,1},{1,0},{2,3},{3,2},{4,5},{5,4},{6,7},{7,6},{32,33},{33,32},{3... | collective-permute-start | bytes 1572872 | tf_op jit(solution)/shard_map/ppermute | solution.py:29
  13.3 56.4 %all-to-all-start = ((bf16[8,4,16,2048]{3,2,1,0:T(8,128)(2,1)}), bf16[8,4,16,2048]{3,2,1,0:T(8,128)(2,1)S(1)}, u32[]{:S(2)}, u32[]{:S(2)}) async-start(bf16[8,4,16,2048]{3,2,1,0:T(8,128)(2,1)} %bitcast.35), calls=%async_computation | async-start | bytes 4194304 | tf_op jit(solution)/shard_map/all_to_all | solution.py:157
  19.8 36.4 %collective-permute-start.11 = (bf16[128,2048]{1,0:T(8,128)(2,1)S(1)}, bf16[128,2048]{1,0:T(8,128)(2,1)}, u32[]{:S(2)}, u32[]{:S(2)}) collective-permute-start(bf16[128,2048]{1,0:T(8,128)(2,1)S(1)} %collective-permute-done.refs_4_), channel_id=1, source_target_pairs={{0,2},{1,7},{2,4},{3,1},{4,6},{5,3},{6,0},{7,5},{32,34},{33,39},{3... | collective-permute-start | bytes 1572872 | tf_op jit(solution)/shard_map/ppermute | solution.py:29
  19.9 36.7 %collective-permute-start.12 = (bf16[128,2048]{1,0:T(8,128)(2,1)S(1)}, bf16[128,2048]{1,0:T(8,128)(2,1)}, u32[]{:S(2)}, u32[]{:S(2)}) collective-permute-start(bf16[128,2048]{1,0:T(8,128)(2,1)S(1)} %collective-permute-done.refs_4_), channel_id=1, source_target_pairs={{0,6},{1,3},{2,0},{3,5},{4,2},{5,7},{6,4},{7,1},{32,38},{33,35},{3... | collective-permute-start | bytes 1572872 | tf_op jit(solution)/shard_map/ppermute | solution.py:29
  31.6 25.1 %collective-permute-start.18 = (bf16[128,2048]{1,0:T(8,128)(2,1)S(1)}, bf16[128,2048]{1,0:T(8,128)(2,1)}, u32[]{:S(2)}, u32[]{:S(2)}) collective-permute-start(bf16[128,2048]{1,0:T(8,128)(2,1)S(1)} %collective-permute-done.refs_4_), channel_id=1, source_target_pairs={{0,1},{1,0},{2,3},{3,2},{4,5},{5,4},{6,7},{7,6},{32,33},{33,32},{3... | collective-permute-start | bytes 1572872 | tf_op jit(solution)/shard_map/ppermute | solution.py:29
  31.6 25.5 %collective-permute-start.13 = (bf16[128,2048]{1,0:T(8,128)(2,1)}, bf16[128,2048]{1,0:T(8,128)(2,1)}, u32[]{:S(2)}, u32[]{:S(2)}) collective-permute-start(bf16[128,2048]{1,0:T(8,128)(2,1)} %collective-permute-done.10.refs_3_), channel_id=1, source_target_pairs={{0,8},{1,25},{2,10},{3,27},{4,12},{5,29},{6,14},{7,31},{32,40},{33... | collective-permute-start | bytes 1572872 | tf_op jit(solution)/shard_map/ppermute | solution.py:29
  32.3 12.1 %collective-permute-start.1 = (bf16[32,2048]{1,0:T(8,128)(2,1)S(1)}, bf16[32,2048]{1,0:T(8,128)(2,1)S(1)}, u32[]{:S(2)}, u32[]{:S(2)}) collective-permute-start(bf16[32,2048]{1,0:T(8,128)(2,1)S(1)} %constant_dynamic-slice_fusion), channel_id=1, source_target_pairs={{0,2},{1,7},{2,4},{3,1},{4,6},{5,3},{6,0},{7,5},{32,34},{33,39},{3... | collective-permute-start | bytes 393224 | tf_op jit(solution)/shard_map/ppermute | solution.py:29
  56.2 9.4 %collective-permute-start.15 = (bf16[128,2048]{1,0:T(8,128)(2,1)}, bf16[128,2048]{1,0:T(8,128)(2,1)S(1)}, u32[]{:S(2)}, u32[]{:S(2)}) collective-permute-start(bf16[128,2048]{1,0:T(8,128)(2,1)} %collective-permute-done.8.refs_1_), channel_id=1, source_target_pairs={{0,1},{1,0},{2,3},{3,2},{4,5},{5,4},{6,7},{7,6},{32,33},{33,32},{3... | collective-permute-start | bytes 1572872 | tf_op jit(solution)/shard_map/ppermute | solution.py:29
  56.7 10.5 %collective-permute-start.19 = (bf16[128,2048]{1,0:T(8,128)(2,1)}, bf16[128,2048]{1,0:T(8,128)(2,1)S(1)}, u32[]{:S(2)}, u32[]{:S(2)}) collective-permute-start(bf16[128,2048]{1,0:T(8,128)(2,1)} %collective-permute-done.11.refs_5_), channel_id=1, source_target_pairs={{0,1},{1,0},{2,3},{3,2},{4,5},{5,4},{6,7},{7,6},{32,33},{33,32},{3... | collective-permute-start | bytes 1572872 | tf_op jit(solution)/shard_map/ppermute | solution.py:29
  57.1 11.3 %collective-permute-start.20 = (bf16[128,2048]{1,0:T(8,128)(2,1)}, bf16[128,2048]{1,0:T(8,128)(2,1)S(1)}, u32[]{:S(2)}, u32[]{:S(2)}) collective-permute-start(bf16[128,2048]{1,0:T(8,128)(2,1)} %collective-permute-done.12.refs_6_), channel_id=1, source_target_pairs={{0,1},{1,0},{2,3},{3,2},{4,5},{5,4},{6,7},{7,6},{32,33},{33,32},{3... | collective-permute-start | bytes 1572872 | tf_op jit(solution)/shard_map/ppermute | solution.py:29
  62.8 24.8 %collective-permute-start.4 = (bf16[128,2048]{1,0:T(8,128)(2,1)}, bf16[128,2048]{1,0:T(8,128)(2,1)}, u32[]{:S(2)}, u32[]{:S(2)}) collective-permute-start(bf16[128,2048]{1,0:T(8,128)(2,1)} %pad_maximum_fusion.refs_0_), channel_id=1, source_target_pairs={{0,32},{1,97},{2,34},{3,99},{4,36},{5,101},{6,38},{7,103},{32,64},... | collective-permute-start | bytes 1572872 | tf_op jit(solution)/shard_map/ppermute | solution.py:29
  65.6 22.1 %collective-permute-start.5 = (bf16[128,2048]{1,0:T(8,128)(2,1)}, bf16[128,2048]{1,0:T(8,128)(2,1)}, u32[]{:S(2)}, u32[]{:S(2)}) collective-permute-start(bf16[128,2048]{1,0:T(8,128)(2,1)} %pad_maximum_fusion.refs_0_), channel_id=1, source_target_pairs={{0,96},{1,33},{2,98},{3,35},{4,100},{5,37},{6,102},{7,39},{32,0},{... | collective-permute-start | bytes 1572872 | tf_op jit(solution)/shard_map/ppermute | solution.py:29
  65.6 25.3 %collective-permute-start.6 = (bf16[128,2048]{1,0:T(8,128)(2,1)}, bf16[128,2048]{1,0:T(8,128)(2,1)}, u32[]{:S(2)}, u32[]{:S(2)}) collective-permute-start(bf16[128,2048]{1,0:T(8,128)(2,1)} %pad_maximum_fusion.refs_0_), channel_id=1, source_target_pairs={{0,64},{1,65},{2,66},{3,67},{4,68},{5,69},{6,70},{7,71},{32,96},{3... | collective-permute-start | bytes 1572872 | tf_op jit(solution)/shard_map/ppermute | solution.py:29
  67.2 23.7 %collective-permute-start.7 = (bf16[128,2048]{1,0:T(8,128)(2,1)}, bf16[128,2048]{1,0:T(8,128)(2,1)}, u32[]{:S(2)}, u32[]{:S(2)}) collective-permute-start(bf16[128,2048]{1,0:T(8,128)(2,1)} %pad_maximum_fusion.refs_0_), channel_id=1, source_target_pairs={{0,8},{1,25},{2,10},{3,27},{4,12},{5,29},{6,14},{7,31},{32,40},{33... | collective-permute-start | bytes 1572872 | tf_op jit(solution)/shard_map/ppermute | solution.py:29
  90.9 46.6 %all-to-all-start.1 = ((bf16[128,16,512]{2,1,0:T(8,128)(2,1)}), bf16[128,16,512]{2,1,0:T(8,128)(2,1)S(1)}, u32[]{:S(2)}, u32[]{:S(2)}) async-start(bf16[128,16,512]{2,1,0:T(8,128)(2,1)} %bitcast.33), calls=%async_computation.1 | async-start | bytes 4194304 | tf_op jit(solution)/shard_map/all_to_all | solution.py:172
  96.0 30.2 %collective-permute-start.22 = (bf16[128,2048]{1,0:T(8,128)(2,1)}, bf16[128,2048]{1,0:T(8,128)(2,1)S(1)}, u32[]{:S(2)}, u32[]{:S(2)}) collective-permute-start(bf16[128,2048]{1,0:T(8,128)(2,1)} %collective-permute-done.4.refs_1_), channel_id=1, source_target_pairs={{0,8},{1,25},{2,10},{3,27},{4,12},{5,29},{6,14},{7,31},{32,40},{33... | collective-permute-start | bytes 1572872 | tf_op jit(solution)/shard_map/ppermute | solution.py:29
  98.7 29.0 %collective-permute-start.23 = (bf16[128,2048]{1,0:T(8,128)(2,1)}, bf16[128,2048]{1,0:T(8,128)(2,1)}, u32[]{:S(2)}, u32[]{:S(2)}) collective-permute-start(bf16[128,2048]{1,0:T(8,128)(2,1)} %collective-permute-done.7.refs_4_), channel_id=1, source_target_pairs={{0,96},{1,33},{2,98},{3,35},{4,100},{5,37},{6,102},{7,39},{32,0},{... | collective-permute-start | bytes 1572872 | tf_op jit(solution)/shard_map/ppermute | solution.py:29
  99.9 31.9 %collective-permute-start.24 = (bf16[128,2048]{1,0:T(8,128)(2,1)}, bf16[128,2048]{1,0:T(8,128)(2,1)}, u32[]{:S(2)}, u32[]{:S(2)}) collective-permute-start(bf16[128,2048]{1,0:T(8,128)(2,1)} %collective-permute-done.6.refs_3_), channel_id=1, source_target_pairs={{0,8},{1,25},{2,10},{3,27},{4,12},{5,29},{6,14},{7,31},{32,40},{33... | collective-permute-start | bytes 1572872 | tf_op jit(solution)/shard_map/ppermute | solution.py:29
  100.4 33.0 %collective-permute-start.25 = (bf16[128,2048]{1,0:T(8,128)(2,1)}, bf16[128,2048]{1,0:T(8,128)(2,1)}, u32[]{:S(2)}, u32[]{:S(2)}) collective-permute-start(bf16[128,2048]{1,0:T(8,128)(2,1)} %pad_maximum_fusion.refs_0_), channel_id=1, source_target_pairs={{0,1},{1,0},{2,3},{3,2},{4,5},{5,4},{6,7},{7,6},{32,33},{33,32},{3... | collective-permute-start | bytes 1572872 | tf_op jit(solution)/shard_map/ppermute | solution.py:29
  102.3 31.1 %collective-permute-start.26 = (bf16[128,2048]{1,0:T(8,128)(2,1)}, bf16[128,2048]{1,0:T(8,128)(2,1)}, u32[]{:S(2)}, u32[]{:S(2)}) collective-permute-start(bf16[128,2048]{1,0:T(8,128)(2,1)} %collective-permute-done.4.refs_1_), channel_id=1, source_target_pairs={{0,1},{1,0},{2,3},{3,2},{4,5},{5,4},{6,7},{7,6},{32,33},{33,32},{3... | collective-permute-start | bytes 1572872 | tf_op jit(solution)/shard_map/ppermute | solution.py:29
  (23 other events, 224.8 us)

commit v3 on v2

--- a/solution.py
+++ b/solution.py
@@ -149,17 +149,17 @@
 
     near = [right_rot] + [shift(right_rot, dz=dz) for dz in (1, -1, 2)]
     there = shift(right_rot, dx=1)
-    rights = near + [there, shift(there, dz=1), shift(there, dz=-1), shift(near[3], dx=1)]
-    left_rot, there = after(left_rot, there)
-    quarter = lax.dynamic_slice_in_dim(left_rot, y * 32, 32, 0)
-    strip = jnp.concatenate([quarter, shift(quarter, dz=1), shift(quarter, dz=-1), shift(quarter, dz=2)])
     pieces = operators.reshape(4, 8, 16, 2048).transpose(1, 0, 2, 3)
     pieces = lax.all_to_all(pieces, PAIR, 0, 0, tiled=True).reshape(512, 2048)
     spread = spread_coupling(integrals, pair_index, target_index)
-    lefts = [strip, shift(strip, dy=1), shift(strip, dy=-1), shift(strip, dy=2)]
+    left_rot, there, spread = after(left_rot, there, spread)
+    quarter = lax.dynamic_slice_in_dim(left_rot, y * 32, 32, 0)
+    strip = jnp.concatenate([quarter, shift(quarter, dz=1), shift(quarter, dz=-1), shift(quarter, dz=2)])
+    rights = near + [there, shift(there, dz=1), shift(there, dz=-1), shift(near[3], dx=1)]
     rights += [swap_core(right) for right in rights]
-
     rows = mix(spread, [pieces])
+    rows, strip, *rights = after(rows, strip, *rights)
+    lefts = [strip, shift(strip, dy=1), shift(strip, dy=-1)]
 
     def along_z(xl, core):
         way = 1 - 2 * core
@@ -167,10 +167,10 @@
 
     places = along_z(xl, core) + along_z(1 - xl, core) + along_z(xl, 1 - core) + along_z(1 - xl, 1 - core)
     half = half_rotate(jnp.stack(places), rows, rights)
-    across = shift(strip, dx=1)
-    *lefts, across, half = after(*lefts, across, half)
+    lefts.append(shift(lefts[1], dy=1))
+    lefts += [shift(left, dx=1) for left in lefts[:3]]
     columns = lax.all_to_all(half.reshape(128, 16, 512), AXES, 0, 0, tiled=True)
-    lefts += [across, shift(lefts[1], dx=1), shift(across, dy=-1), shift(lefts[3], dx=1)]
+    lefts.append(shift(lefts[3], dx=1))
     lefts += [swap_core(left) for left in lefts]
     return final_rotate(jnp.stack(left_order(y, core) + places), lefts, columns.reshape(8, 16, 16, 512))
 

time: 149 us -> 138 us (0.926)
  waiting for transfers between devices: 70.3 us -> 54.8 us
  starting transfers between devices: 43.4 us -> 49.4 us
    ppermute x33, waiting for transfers between devices: 70.3 us -> 54.8 us  [send(): return lax.ppermute(value, AXES, moves)]
    ppermute x33, starting transfers between devices: 31.8 us -> 39.2 us  [send(): return lax.ppermute(value, AXES, moves)]
    unnamed x24 -> x20, local copies, waits for them, and re-layouts: 3.03 us -> 1.68 us
  transfers between devices with their start and end apart: 35 -> 35, of which waited for: 12 -> 7; matrix products, arithmetic and copies ran while one was open for 7% -> 7% of each run, Pallas kernels for 7% -> 8%
where the time goes in v3:
time: 138 us; the launch traced here: 137 us
  waiting for transfers between devices  54.8 us (40%)
  starting transfers between devices  49.4 us (36%)
  Pallas kernels  20.9 us (15%)
  local copies, waits for them, and re-layouts  6.25 us (5%)
  matrix products  4.59 us (3%)
    ppermute x33, waiting for transfers between devices, send(): return lax.ppermute(value, AXES, moves)  54.8 us
    ppermute x33, starting transfers between devices, send(): return lax.ppermute(value, AXES, moves)  39.2 us
    pallas_call x1, Pallas kernels, half_rotate(): pl.pallas_call(half_kernel, grid_spec=pltpu.PrefetchScalarGridSpec(num_sc...  9.91 us
    pallas_call x1, Pallas kernels, final_rotate(): pl.pallas_call(final_kernel, grid_spec=pltpu.PrefetchScalarGridSpec(num_s...  9.7 us
    all_to_all x1, starting transfers between devices, shards(): pieces = lax.all_to_all(pieces, PAIR, 0, 0, tiled=True).reshape(512, 2048)  6.49 us
    dot_general x1, matrix products, spread_coupling(): jnp.dot(selector(target_index, npairs), integrals, precision=lax.Precisio...  3.84 us
    all_to_all x1, starting transfers between devices, shards(): columns = lax.all_to_all(half.reshape(128, 16, 512), AXES, 0, 0, tiled=True)  3.73 us
    reshape x1, local copies, waits for them, and re-layouts, shards(): pieces = operators.reshape(4, 8, 16, 2048).transpose(1, 0, 2, 3)  3.16 us
  transfers between devices with their start and end apart: 35, of which 7 were waited for; matrix products, arithmetic and copies ran while one was open for 7% of the time, Pallas kernels for 8%

profile of v3, /device:TPU:1, one launch (start us, length us, event | category | flops | bytes accessed | tf_op | source)
XLA Modules:
  0.0 137.2 jit_solution(2105894624646790269)
XLA Ops:
  0.0 3.3 %collective-permute-start = (bf16[128,2048]{1,0:T(8,128)(2,1)}, bf16[128,2048]{1,0:T(8,128)(2,1)}, u32[]{:S(2)}, u32[]{:S(2)}) collective-permute-start(bf16[128,2048]{1,0:T(8,128)(2,1)} %refs_0_), channel_id=1, source_target_pairs={{0,8},{1,25},{2,10},{3,27},{4,12},{5,29},{6,14},{7,31},{32,40},{33... | collective-permute-start | bytes 1572872 | tf_op jit(solution)/shard_map/ppermute | solution.py:29
  3.3 3.6 %collective-permute-start.6 = (bf16[128,2048]{1,0:T(8,128)(2,1)}, bf16[128,2048]{1,0:T(8,128)(2,1)}, u32[]{:S(2)}, u32[]{:S(2)}) collective-permute-start(bf16[128,2048]{1,0:T(8,128)(2,1)} %refs_0_), channel_id=1, source_target_pairs={{0,4},{1,5},{2,6},{3,7},{4,0},{5,1},{6,2},{7,3},{32,36},{33,37},{3... | collective-permute-start | bytes 1572872 | tf_op jit(solution)/shard_map/ppermute | solution.py:29
  8.4 1.7 %collective-permute-start.10 = (bf16[128,2048]{1,0:T(8,128)(2,1)}, bf16[128,2048]{1,0:T(8,128)(2,1)}, u32[]{:S(2)}, u32[]{:S(2)}) collective-permute-start(bf16[128,2048]{1,0:T(8,128)(2,1)} %refs_0_), channel_id=1, source_target_pairs={{0,1},{1,0},{2,3},{3,2},{4,5},{5,4},{6,7},{7,6},{32,33},{33,32},{3... | collective-permute-start | bytes 1572872 | tf_op jit(solution)/shard_map/ppermute | solution.py:29
  10.1 3.2 %copy.9 = bf16[4,8,16,2048]{3,2,0,1:T(8,128)(2,1)} copy(bf16[4,8,16,2048]{3,2,1,0:T(8,128)(2,1)} %bitcast.36) | data formatting | bytes 4194304 | tf_op jit(solution)/shard_map/reshape | solution.py:152
  13.3 6.5 %all-to-all-start = ((bf16[8,4,16,2048]{3,2,1,0:T(8,128)(2,1)}), bf16[8,4,16,2048]{3,2,1,0:T(8,128)(2,1)S(1)}, u32[]{:S(2)}, u32[]{:S(2)}) async-start(bf16[8,4,16,2048]{3,2,1,0:T(8,128)(2,1)} %bitcast.35), calls=%async_computation | async-start | bytes 4194304 | tf_op jit(solution)/shard_map/all_to_all | solution.py:153
  19.8 3.8 %fusion.3 = f32[32,1024]{1,0:T(8,128)S(1)} fusion(f32[1024,1024]{1,0:T(8,128)} %param.9, s32[32]{0:T(128)S(1)} %copy-done.8), kind=kOutput, calls=%fused_computation.12 | convolution fusion | flops 402685952 | bytes 4325504 | tf_op jit(solution)/shard_map/dot_general | solution.py:50
  24.6 1.4 %collective-permute-start.2 = (bf16[32,2048]{1,0:T(8,128)(2,1)S(1)}, bf16[32,2048]{1,0:T(8,128)(2,1)S(1)}, u32[]{:S(2)}, u32[]{:S(2)}) collective-permute-start(bf16[32,2048]{1,0:T(8,128)(2,1)S(1)} %constant_dynamic-slice_fusion), channel_id=1, source_target_pairs={{0,6},{1,3},{2,0},{3,5},{4,2},{5,7},{6,4},{7,1},{32,38},{33,35},{3... | collective-permute-start | bytes 393224 | tf_op jit(solution)/shard_map/ppermute | solution.py:29
  26.0 5.5 %collective-permute-done.4.refs_1_ = bf16[128,2048]{1,0:T(8,128)(2,1)} collective-permute-done((bf16[128,2048]{1,0:T(8,128)(2,1)}, bf16[128,2048]{1,0:T(8,128)(2,1)}, u32[]{:S(2)}, u32[]{:S(2)}) %collective-permute-start.4) | collective-permute-done | bytes 524320 | tf_op jit(solution)/shard_map/ppermute | solution.py:29
  32.5 1.9 %collective-permute-start.7 = (bf16[128,2048]{1,0:T(8,128)(2,1)}, bf16[128,2048]{1,0:T(8,128)(2,1)}, u32[]{:S(2)}, u32[]{:S(2)}) collective-permute-start(bf16[128,2048]{1,0:T(8,128)(2,1)} %collective-permute-done.refs_4_), channel_id=1, source_target_pairs={{0,2},{1,7},{2,4},{3,1},{4,6},{5,3},{6,0},{7,5},{32,34},{33,39},{3... | collective-permute-start | bytes 1572872 | tf_op jit(solution)/shard_map/ppermute | solution.py:29
  34.6 2.6 %collective-permute-start.14 = (bf16[128,2048]{1,0:T(8,128)(2,1)}, bf16[128,2048]{1,0:T(8,128)(2,1)}, u32[]{:S(2)}, u32[]{:S(2)}) collective-permute-start(bf16[128,2048]{1,0:T(8,128)(2,1)} %collective-permute-done.refs_4_), channel_id=1, source_target_pairs={{0,1},{1,0},{2,3},{3,2},{4,5},{5,4},{6,7},{7,6},{32,33},{33,32},{3... | collective-permute-start | bytes 1572872 | tf_op jit(solution)/shard_map/ppermute | solution.py:29
  39.1 9.2 %collective-permute-done.7.refs_5_ = bf16[128,2048]{1,0:T(8,128)(2,1)} collective-permute-done((bf16[128,2048]{1,0:T(8,128)(2,1)}, bf16[128,2048]{1,0:T(8,128)(2,1)}, u32[]{:S(2)}, u32[]{:S(2)}) %collective-permute-start.7) | collective-permute-done | bytes 524320 | tf_op jit(solution)/shard_map/ppermute | solution.py:29
  48.4 2.0 %collective-permute-start.11 = (bf16[128,2048]{1,0:T(8,128)(2,1)}, bf16[128,2048]{1,0:T(8,128)(2,1)}, u32[]{:S(2)}, u32[]{:S(2)}) collective-permute-start(bf16[128,2048]{1,0:T(8,128)(2,1)} %collective-permute-done.4.refs_1_), channel_id=1, source_target_pairs={{0,1},{1,0},{2,3},{3,2},{4,5},{5,4},{6,7},{7,6},{32,33},{33,32},{3... | collective-permute-start | bytes 1572872 | tf_op jit(solution)/shard_map/ppermute | solution.py:29
  50.9 2.9 %collective-permute-start.16 = (bf16[128,2048]{1,0:T(8,128)(2,1)}, bf16[128,2048]{1,0:T(8,128)(2,1)}, u32[]{:S(2)}, u32[]{:S(2)}) collective-permute-start(bf16[128,2048]{1,0:T(8,128)(2,1)} %collective-permute-done.8.refs_6_), channel_id=1, source_target_pairs={{0,1},{1,0},{2,3},{3,2},{4,5},{5,4},{6,7},{7,6},{32,33},{33,32},{3... | collective-permute-start | bytes 1572872 | tf_op jit(solution)/shard_map/ppermute | solution.py:29
  57.2 1.6 %collective-permute-start.18 = (bf16[128,2048]{1,0:T(8,128)(2,1)}, bf16[128,2048]{1,0:T(8,128)(2,1)S(1)}, u32[]{:S(2)}, u32[]{:S(2)}) collective-permute-start(bf16[128,2048]{1,0:T(8,128)(2,1)} %pad_maximum_fusion.refs_0_), channel_id=1, source_target_pairs={{0,32},{1,97},{2,34},{3,99},{4,36},{5,101},{6,38},{7,103},{32,64},... | collective-permute-start | bytes 1572872 | tf_op jit(solution)/shard_map/ppermute | solution.py:29
  59.4 9.9 %half.1 = bf16[8,16,16,512]{3,2,1,0:T(8,128)(2,1)} custom-call(s32[16]{0:T(128)} %stack.137.order, bf16[512,2048]{1,0:T(8,128)(2,1)} %copy-done.1, bf16[128,2048]{1,0:T(8,128)(2,1)} %refs_0_, bf16[128,2048]{1,0:T(8,128)(2,1)} %collective-permute-done.4.refs_1_, bf16[128,2048]{1,0:T(8,128)(2,1)} %collective-permute-done.5.refs_2_, ...), custom_call_target="tpu_custom_call" | custom-call | tf_op jit(solution)/shard_map/half/pallas_call | solution.py:90
  69.4 3.7 %all-to-all-start.1 = ((bf16[128,16,512]{2,1,0:T(8,128)(2,1)}), bf16[128,16,512]{2,1,0:T(8,128)(2,1)S(1)}, u32[]{:S(2)}, u32[]{:S(2)}) async-start(bf16[128,16,512]{2,1,0:T(8,128)(2,1)} %bitcast.33), calls=%async_computation.1 | async-start | bytes 4194304 | tf_op jit(solution)/shard_map/all_to_all | solution.py:172
  73.1 1.5 %collective-permute-start.19 = (bf16[128,2048]{1,0:T(8,128)(2,1)}, bf16[128,2048]{1,0:T(8,128)(2,1)S(1)}, u32[]{:S(2)}, u32[]{:S(2)}) collective-permute-start(bf16[128,2048]{1,0:T(8,128)(2,1)} %pad_maximum_fusion.refs_0_), channel_id=1, source_target_pairs={{0,96},{1,33},{2,98},{3,35},{4,100},{5,37},{6,102},{7,39},{32,0},{... | collective-permute-start | bytes 1572872 | tf_op jit(solution)/shard_map/ppermute | solution.py:29
  74.5 2.4 %collective-permute-start.21 = (bf16[128,2048]{1,0:T(8,128)(2,1)}, bf16[128,2048]{1,0:T(8,128)(2,1)}, u32[]{:S(2)}, u32[]{:S(2)}) collective-permute-start(bf16[128,2048]{1,0:T(8,128)(2,1)} %pad_maximum_fusion.refs_0_), channel_id=1, source_target_pairs={{0,8},{1,25},{2,10},{3,27},{4,12},{5,29},{6,14},{7,31},{32,40},{33... | collective-permute-start | bytes 1572872 | tf_op jit(solution)/shard_map/ppermute | solution.py:29
  78.5 1.4 %collective-permute-start.22 = (bf16[128,2048]{1,0:T(8,128)(2,1)S(1)}, bf16[128,2048]{1,0:T(8,128)(2,1)}, u32[]{:S(2)}, u32[]{:S(2)}) collective-permute-start(bf16[128,2048]{1,0:T(8,128)(2,1)S(1)} %collective-permute-done.18.refs_1_), channel_id=1, source_target_pairs={{0,8},{1,25},{2,10},{3,27},{4,12},{5,29},{6,14},{7,31},{32,40},{33... | collective-permute-start | bytes 1572872 | tf_op jit(solution)/shard_map/ppermute | solution.py:29
  79.9 29.9 %collective-permute-done.19.refs_2_ = bf16[128,2048]{1,0:T(8,128)(2,1)S(1)} collective-permute-done((bf16[128,2048]{1,0:T(8,128)(2,1)}, bf16[128,2048]{1,0:T(8,128)(2,1)S(1)}, u32[]{:S(2)}, u32[]{:S(2)}) %collective-permute-start.19) | collective-permute-done | bytes 524320 | tf_op jit(solution)/shard_map/ppermute | solution.py:29
  109.8 2.6 %collective-permute-start.23 = (bf16[128,2048]{1,0:T(8,128)(2,1)S(1)}, bf16[128,2048]{1,0:T(8,128)(2,1)}, u32[]{:S(2)}, u32[]{:S(2)}) collective-permute-start(bf16[128,2048]{1,0:T(8,128)(2,1)S(1)} %collective-permute-done.19.refs_2_), channel_id=1, source_target_pairs={{0,8},{1,25},{2,10},{3,27},{4,12},{5,29},{6,14},{7,31},{32,40},{33... | collective-permute-start | bytes 1572872 | tf_op jit(solution)/shard_map/ppermute | solution.py:29
  113.4 5.1 %collective-permute-done.23.refs_6_ = bf16[128,2048]{1,0:T(8,128)(2,1)} collective-permute-done((bf16[128,2048]{1,0:T(8,128)(2,1)S(1)}, bf16[128,2048]{1,0:T(8,128)(2,1)}, u32[]{:S(2)}, u32[]{:S(2)}) %collective-permute-start.23) | collective-permute-done | bytes 524320 | tf_op jit(solution)/shard_map/ppermute | solution.py:29
  120.5 3.7 %collective-permute-done.24.refs_7_ = bf16[128,2048]{1,0:T(8,128)(2,1)} collective-permute-done((bf16[128,2048]{1,0:T(8,128)(2,1)}, bf16[128,2048]{1,0:T(8,128)(2,1)}, u32[]{:S(2)}, u32[]{:S(2)}) %collective-permute-start.24) | collective-permute-done | bytes 524320 | tf_op jit(solution)/shard_map/ppermute | solution.py:29
  127.4 9.7 %final.1 = bf16[4,2048,128]{2,1,0:T(8,128)(2,1)} custom-call(s32[48]{0:T(128)} %stack.136.order, bf16[128,2048]{1,0:T(8,128)(2,1)} %pad_maximum_fusion.refs_0_, bf16[128,2048]{1,0:T(8,128)(2,1)} %copy-done.3, bf16[128,2048]{1,0:T(8,128)(2,1)} %copy-done.4, bf16[128,2048]{1,0:T(8,128)(2,1)} %collective-permute-done.20.refs_3_, ...), custom_call_target="tpu_custom_call" | custom-call | tf_op jit(solution)/shard_map/final/pallas_call | solution.py:126
  (80 shorter events, 17.7 us)
Async XLA Ops:
  0.0 24.4 %collective-permute-start = (bf16[128,2048]{1,0:T(8,128)(2,1)}, bf16[128,2048]{1,0:T(8,128)(2,1)}, u32[]{:S(2)}, u32[]{:S(2)}) collective-permute-start(bf16[128,2048]{1,0:T(8,128)(2,1)} %refs_0_), channel_id=1, source_target_pairs={{0,8},{1,25},{2,10},{3,27},{4,12},{5,29},{6,14},{7,31},{32,40},{33... | collective-permute-start | bytes 1572872 | tf_op jit(solution)/shard_map/ppermute | solution.py:29
  3.3 21.3 %collective-permute-start.6 = (bf16[128,2048]{1,0:T(8,128)(2,1)}, bf16[128,2048]{1,0:T(8,128)(2,1)}, u32[]{:S(2)}, u32[]{:S(2)}) collective-permute-start(bf16[128,2048]{1,0:T(8,128)(2,1)} %refs_0_), channel_id=1, source_target_pairs={{0,4},{1,5},{2,6},{3,7},{4,0},{5,1},{6,2},{7,3},{32,36},{33,37},{3... | collective-permute-start | bytes 1572872 | tf_op jit(solution)/shard_map/ppermute | solution.py:29
  6.9 24.7 %collective-permute-start.4 = (bf16[128,2048]{1,0:T(8,128)(2,1)}, bf16[128,2048]{1,0:T(8,128)(2,1)}, u32[]{:S(2)}, u32[]{:S(2)}) collective-permute-start(bf16[128,2048]{1,0:T(8,128)(2,1)} %refs_0_), channel_id=1, source_target_pairs={{0,2},{1,7},{2,4},{3,1},{4,6},{5,3},{6,0},{7,5},{32,34},{33,39},{3... | collective-permute-start | bytes 1572872 | tf_op jit(solution)/shard_map/ppermute | solution.py:29
  7.3 25.1 %collective-permute-start.5 = (bf16[128,2048]{1,0:T(8,128)(2,1)}, bf16[128,2048]{1,0:T(8,128)(2,1)}, u32[]{:S(2)}, u32[]{:S(2)}) collective-permute-start(bf16[128,2048]{1,0:T(8,128)(2,1)} %refs_0_), channel_id=1, source_target_pairs={{0,6},{1,3},{2,0},{3,5},{4,2},{5,7},{6,4},{7,1},{32,38},{33,35},{3... | collective-permute-start | bytes 1572872 | tf_op jit(solution)/shard_map/ppermute | solution.py:29
  8.4 25.9 %collective-permute-start.10 = (bf16[128,2048]{1,0:T(8,128)(2,1)}, bf16[128,2048]{1,0:T(8,128)(2,1)}, u32[]{:S(2)}, u32[]{:S(2)}) collective-permute-start(bf16[128,2048]{1,0:T(8,128)(2,1)} %refs_0_), channel_id=1, source_target_pairs={{0,1},{1,0},{2,3},{3,2},{4,5},{5,4},{6,7},{7,6},{32,33},{33,32},{3... | collective-permute-start | bytes 1572872 | tf_op jit(solution)/shard_map/ppermute | solution.py:29
  13.3 41.3 %all-to-all-start = ((bf16[8,4,16,2048]{3,2,1,0:T(8,128)(2,1)}), bf16[8,4,16,2048]{3,2,1,0:T(8,128)(2,1)S(1)}, u32[]{:S(2)}, u32[]{:S(2)}) async-start(bf16[8,4,16,2048]{3,2,1,0:T(8,128)(2,1)} %bitcast.35), calls=%async_computation | async-start | bytes 4194304 | tf_op jit(solution)/shard_map/all_to_all | solution.py:153
  24.5 10.1 %collective-permute-start.1 = (bf16[32,2048]{1,0:T(8,128)(2,1)S(1)}, bf16[32,2048]{1,0:T(8,128)(2,1)S(1)}, u32[]{:S(2)}, u32[]{:S(2)}) collective-permute-start(bf16[32,2048]{1,0:T(8,128)(2,1)S(1)} %constant_dynamic-slice_fusion), channel_id=1, source_target_pairs={{0,2},{1,7},{2,4},{3,1},{4,6},{5,3},{6,0},{7,5},{32,34},{33,39},{3... | collective-permute-start | bytes 393224 | tf_op jit(solution)/shard_map/ppermute | solution.py:29
  24.6 12.6 %collective-permute-start.2 = (bf16[32,2048]{1,0:T(8,128)(2,1)S(1)}, bf16[32,2048]{1,0:T(8,128)(2,1)S(1)}, u32[]{:S(2)}, u32[]{:S(2)}) collective-permute-start(bf16[32,2048]{1,0:T(8,128)(2,1)S(1)} %constant_dynamic-slice_fusion), channel_id=1, source_target_pairs={{0,6},{1,3},{2,0},{3,5},{4,2},{5,7},{6,4},{7,1},{32,38},{33,35},{3... | collective-permute-start | bytes 393224 | tf_op jit(solution)/shard_map/ppermute | solution.py:29
  32.5 15.9 %collective-permute-start.7 = (bf16[128,2048]{1,0:T(8,128)(2,1)}, bf16[128,2048]{1,0:T(8,128)(2,1)}, u32[]{:S(2)}, u32[]{:S(2)}) collective-permute-start(bf16[128,2048]{1,0:T(8,128)(2,1)} %collective-permute-done.refs_4_), channel_id=1, source_target_pairs={{0,2},{1,7},{2,4},{3,1},{4,6},{5,3},{6,0},{7,5},{32,34},{33,39},{3... | collective-permute-start | bytes 1572872 | tf_op jit(solution)/shard_map/ppermute | solution.py:29
  34.3 16.0 %collective-permute-start.8 = (bf16[128,2048]{1,0:T(8,128)(2,1)}, bf16[128,2048]{1,0:T(8,128)(2,1)}, u32[]{:S(2)}, u32[]{:S(2)}) collective-permute-start(bf16[128,2048]{1,0:T(8,128)(2,1)} %collective-permute-done.refs_4_), channel_id=1, source_target_pairs={{0,6},{1,3},{2,0},{3,5},{4,2},{5,7},{6,4},{7,1},{32,38},{33,35},{3... | collective-permute-start | bytes 1572872 | tf_op jit(solution)/shard_map/ppermute | solution.py:29
  34.6 15.8 %collective-permute-start.14 = (bf16[128,2048]{1,0:T(8,128)(2,1)}, bf16[128,2048]{1,0:T(8,128)(2,1)}, u32[]{:S(2)}, u32[]{:S(2)}) collective-permute-start(bf16[128,2048]{1,0:T(8,128)(2,1)} %collective-permute-done.refs_4_), channel_id=1, source_target_pairs={{0,1},{1,0},{2,3},{3,2},{4,5},{5,4},{6,7},{7,6},{32,33},{33,32},{3... | collective-permute-start | bytes 1572872 | tf_op jit(solution)/shard_map/ppermute | solution.py:29
  37.2 13.7 %collective-permute-start.9 = (bf16[128,2048]{1,0:T(8,128)(2,1)}, bf16[128,2048]{1,0:T(8,128)(2,1)}, u32[]{:S(2)}, u32[]{:S(2)}) collective-permute-start(bf16[128,2048]{1,0:T(8,128)(2,1)} %collective-permute-done.6.refs_3_), channel_id=1, source_target_pairs={{0,8},{1,25},{2,10},{3,27},{4,12},{5,29},{6,14},{7,31},{32,40},{33... | collective-permute-start | bytes 1572872 | tf_op jit(solution)/shard_map/ppermute | solution.py:29
  38.5 15.2 %collective-permute-start.13 = (bf16[128,2048]{1,0:T(8,128)(2,1)}, bf16[128,2048]{1,0:T(8,128)(2,1)}, u32[]{:S(2)}, u32[]{:S(2)}) collective-permute-start(bf16[128,2048]{1,0:T(8,128)(2,1)} %collective-permute-done.6.refs_3_), channel_id=1, source_target_pairs={{0,1},{1,0},{2,3},{3,2},{4,5},{5,4},{6,7},{7,6},{32,33},{33,32},{3... | collective-permute-start | bytes 1572872 | tf_op jit(solution)/shard_map/ppermute | solution.py:29
  48.4 8.8 %collective-permute-start.11 = (bf16[128,2048]{1,0:T(8,128)(2,1)}, bf16[128,2048]{1,0:T(8,128)(2,1)}, u32[]{:S(2)}, u32[]{:S(2)}) collective-permute-start(bf16[128,2048]{1,0:T(8,128)(2,1)} %collective-permute-done.4.refs_1_), channel_id=1, source_target_pairs={{0,1},{1,0},{2,3},{3,2},{4,5},{5,4},{6,7},{7,6},{32,33},{33,32},{3... | collective-permute-start | bytes 1572872 | tf_op jit(solution)/shard_map/ppermute | solution.py:29
  57.2 20.7 %collective-permute-start.18 = (bf16[128,2048]{1,0:T(8,128)(2,1)}, bf16[128,2048]{1,0:T(8,128)(2,1)S(1)}, u32[]{:S(2)}, u32[]{:S(2)}) collective-permute-start(bf16[128,2048]{1,0:T(8,128)(2,1)} %pad_maximum_fusion.refs_0_), channel_id=1, source_target_pairs={{0,32},{1,97},{2,34},{3,99},{4,36},{5,101},{6,38},{7,103},{32,64},... | collective-permute-start | bytes 1572872 | tf_op jit(solution)/shard_map/ppermute | solution.py:29
  69.4 56.7 %all-to-all-start.1 = ((bf16[128,16,512]{2,1,0:T(8,128)(2,1)}), bf16[128,16,512]{2,1,0:T(8,128)(2,1)S(1)}, u32[]{:S(2)}, u32[]{:S(2)}) async-start(bf16[128,16,512]{2,1,0:T(8,128)(2,1)} %bitcast.33), calls=%async_computation.1 | async-start | bytes 4194304 | tf_op jit(solution)/shard_map/all_to_all | solution.py:172
  73.1 36.7 %collective-permute-start.19 = (bf16[128,2048]{1,0:T(8,128)(2,1)}, bf16[128,2048]{1,0:T(8,128)(2,1)S(1)}, u32[]{:S(2)}, u32[]{:S(2)}) collective-permute-start(bf16[128,2048]{1,0:T(8,128)(2,1)} %pad_maximum_fusion.refs_0_), channel_id=1, source_target_pairs={{0,96},{1,33},{2,98},{3,35},{4,100},{5,37},{6,102},{7,39},{32,0},{... | collective-permute-start | bytes 1572872 | tf_op jit(solution)/shard_map/ppermute | solution.py:29
  74.5 37.8 %collective-permute-start.21 = (bf16[128,2048]{1,0:T(8,128)(2,1)}, bf16[128,2048]{1,0:T(8,128)(2,1)}, u32[]{:S(2)}, u32[]{:S(2)}) collective-permute-start(bf16[128,2048]{1,0:T(8,128)(2,1)} %pad_maximum_fusion.refs_0_), channel_id=1, source_target_pairs={{0,8},{1,25},{2,10},{3,27},{4,12},{5,29},{6,14},{7,31},{32,40},{33... | collective-permute-start | bytes 1572872 | tf_op jit(solution)/shard_map/ppermute | solution.py:29
  76.9 35.4 %collective-permute-start.25 = (bf16[128,2048]{1,0:T(8,128)(2,1)}, bf16[128,2048]{1,0:T(8,128)(2,1)S(1)}, u32[]{:S(2)}, u32[]{:S(2)}) collective-permute-start(bf16[128,2048]{1,0:T(8,128)(2,1)} %pad_maximum_fusion.refs_0_), channel_id=1, source_target_pairs={{0,1},{1,0},{2,3},{3,2},{4,5},{5,4},{6,7},{7,6},{32,33},{33,32},{3... | collective-permute-start | bytes 1572872 | tf_op jit(solution)/shard_map/ppermute | solution.py:29
  77.9 34.9 %collective-permute-start.20 = (bf16[128,2048]{1,0:T(8,128)(2,1)S(1)}, bf16[128,2048]{1,0:T(8,128)(2,1)}, u32[]{:S(2)}, u32[]{:S(2)}) collective-permute-start(bf16[128,2048]{1,0:T(8,128)(2,1)S(1)} %collective-permute-done.18.refs_1_), channel_id=1, source_target_pairs={{0,32},{1,97},{2,34},{3,99},{4,36},{5,101},{6,38},{7,103},{32,64},... | collective-permute-start | bytes 1572872 | tf_op jit(solution)/shard_map/ppermute | solution.py:29
  78.5 34.8 %collective-permute-start.22 = (bf16[128,2048]{1,0:T(8,128)(2,1)S(1)}, bf16[128,2048]{1,0:T(8,128)(2,1)}, u32[]{:S(2)}, u32[]{:S(2)}) collective-permute-start(bf16[128,2048]{1,0:T(8,128)(2,1)S(1)} %collective-permute-done.18.refs_1_), channel_id=1, source_target_pairs={{0,8},{1,25},{2,10},{3,27},{4,12},{5,29},{6,14},{7,31},{32,40},{33... | collective-permute-start | bytes 1572872 | tf_op jit(solution)/shard_map/ppermute | solution.py:29
  109.8 8.7 %collective-permute-start.23 = (bf16[128,2048]{1,0:T(8,128)(2,1)S(1)}, bf16[128,2048]{1,0:T(8,128)(2,1)}, u32[]{:S(2)}, u32[]{:S(2)}) collective-permute-start(bf16[128,2048]{1,0:T(8,128)(2,1)S(1)} %collective-permute-done.19.refs_2_), channel_id=1, source_target_pairs={{0,8},{1,25},{2,10},{3,27},{4,12},{5,29},{6,14},{7,31},{32,40},{33... | collective-permute-start | bytes 1572872 | tf_op jit(solution)/shard_map/ppermute | solution.py:29
  112.9 11.3 %collective-permute-start.24 = (bf16[128,2048]{1,0:T(8,128)(2,1)}, bf16[128,2048]{1,0:T(8,128)(2,1)}, u32[]{:S(2)}, u32[]{:S(2)}) collective-permute-start(bf16[128,2048]{1,0:T(8,128)(2,1)} %collective-permute-done.20.refs_3_), channel_id=1, source_target_pairs={{0,8},{1,25},{2,10},{3,27},{4,12},{5,29},{6,14},{7,31},{32,40},{33... | collective-permute-start | bytes 1572872 | tf_op jit(solution)/shard_map/ppermute | solution.py:29
  113.4 12.6 %collective-permute-start.29 = (bf16[128,2048]{1,0:T(8,128)(2,1)}, bf16[128,2048]{1,0:T(8,128)(2,1)}, u32[]{:S(2)}, u32[]{:S(2)}) collective-permute-start(bf16[128,2048]{1,0:T(8,128)(2,1)} %collective-permute-done.21.refs_4_), channel_id=1, source_target_pairs={{0,1},{1,0},{2,3},{3,2},{4,5},{5,4},{6,7},{7,6},{32,33},{33,32},{3... | collective-permute-start | bytes 1572872 | tf_op jit(solution)/shard_map/ppermute | solution.py:29
  (21 other events, 177.3 us)

commit v4 on v3

--- a/solution.py
+++ b/solution.py
@@ -77,34 +77,34 @@
     *rights, out, natural = refs
     for n, right in enumerate(rights):
         natural[pl.ds(pl.multiple_of(order[n] * 128, 128), 128), :] = right[...]
-    total = jnp.dot(rows[...], natural[...], preferred_element_type=F32).astype(BF)
+    total = jnp.dot(rows[...].reshape(256, 2048), natural[...], preferred_element_type=F32).astype(BF)
     for p in range(8):
         for m in range(out.shape[1]):
-            for t in range(4):
-                top = (p * 4 + t) * 16
+            for t in range(2):
+                top = (p * 2 + t) * 16
                 out[p, m, :, t * 128 : t * 128 + 128] = total[top : top + 16, m * 128 : m * 128 + 128]
 
 
-def half_rotate(order, rows, rights):
+def half_rotate(order, rows, rights, part):
     width = 512
     return pl.pallas_call(
         half_kernel,
         grid_spec=pltpu.PrefetchScalarGridSpec(
             num_scalar_prefetch=1,
             grid=(2048 // width,),
-            in_specs=[pl.BlockSpec((512, 2048), lambda i, o: (0, 0))]
+            in_specs=[pl.BlockSpec((8, 2, 16, 2048), lambda i, o: (0, part, 0, 0))]
             + [pl.BlockSpec((128, width), lambda i, o: (0, i)) for _ in rights],
-            out_specs=pl.BlockSpec((8, width // 128, 16, 512), lambda i, o: (0, i, 0, 0)),
+            out_specs=pl.BlockSpec((8, width // 128, 16, 256), lambda i, o: (0, i, 0, 0)),
             scratch_shapes=[pltpu.VMEM((2048, width), BF)],
         ),
-        out_shape=jax.ShapeDtypeStruct((8, 16, 16, 512), BF),
+        out_shape=jax.ShapeDtypeStruct((8, 16, 16, 256), BF),
         compiler_params=pltpu.CompilerParams(vmem_limit_bytes=HALF << 20),
         name="half",
     )(order, rows, *rights)
 
 
 def final_kernel(order, *refs):
-    *lefts, columns, out, rows = refs
+    lefts, (columns, *_, out, rows) = refs[:16], refs[16:]
 
     @pl.when(pl.program_id(0) == 0)
     def _():
@@ -117,11 +117,11 @@
 
     left = jnp.concatenate([piece[...] for piece in lefts], axis=0)
     total = lax.dot_general(left, rows[...], (((0,), (0,)), ((), ())), preferred_element_type=F32).astype(BF)
-    for t in range(4):
+    for t in range(2):
         out[t] = total[:, t * 128 : t * 128 + 128]
 
 
-def final_rotate(order, lefts, columns):
+def final_rotate(order, lefts, columns, part, begun=()):
     height = 512
     return pl.pallas_call(
         final_kernel,
@@ -129,14 +129,17 @@
             num_scalar_prefetch=1,
             grid=(2048 // height,),
             in_specs=[pl.BlockSpec((128, height), lambda i, o: (0, i)) for _ in lefts]
-            + [pl.BlockSpec((8, 16, 16, 512), lambda i, o: (0, 0, 0, 0))],
-            out_specs=pl.BlockSpec((4, height, 128), lambda i, o: (0, i, 0)),
-            scratch_shapes=[pltpu.VMEM((2048, 512), BF)],
+            + [pl.BlockSpec((8, 16, 16, 256), lambda i, o: (0, 0, 0, 0))]
+            + [pl.BlockSpec(memory_space=pl.ANY) for _ in begun],
+            out_specs=pl.BlockSpec((2, height, 128), lambda i, o: (part, i, 0)),
+            scratch_shapes=[pltpu.VMEM((2048, 256), BF)],
         ),
         out_shape=jax.ShapeDtypeStruct((4, 2048, 128), BF),
+        input_output_aliases={18: 0} if begun else {},
         compiler_params=pltpu.CompilerParams(vmem_limit_bytes=FINAL << 20),
+        cost_estimate=pl.CostEstimate(flops=2 * 256 * 2048 * 2048, bytes_accessed=10 << 20, transcendentals=0),
         name="final",
-    )(order, *lefts, columns)
+    )(order, *lefts, columns, *begun)
 
 
 def after(*values):
@@ -158,21 +161,30 @@
     rights = near + [there, shift(there, dz=1), shift(there, dz=-1), shift(near[3], dx=1)]
     rights += [swap_core(right) for right in rights]
     rows = mix(spread, [pieces])
-    rows, strip, *rights = after(rows, strip, *rights)
+    rows, strip, *rights = after(rows.reshape(8, 4, 16, 2048), strip, *rights)
     lefts = [strip, shift(strip, dy=1), shift(strip, dy=-1)]
+    across = [shift(strip, dx=1), shift(strip, dx=1, dy=1)]
 
     def along_z(xl, core):
         way = 1 - 2 * core
         return [(xl * 4 + chip % 4) * 2 + core for chip in (z, z + 4 - way, z + 4 + way, z + 2)]
 
     places = along_z(xl, core) + along_z(1 - xl, core) + along_z(xl, 1 - core) + along_z(1 - xl, 1 - core)
-    half = half_rotate(jnp.stack(places), rows, rights)
+    def exchange(half):
+        return lax.all_to_all(half.reshape(128, 16, 256), AXES, 0, 0, tiled=True).reshape(8, 16, 16, 256)
+
+    places = jnp.stack(places)
+    first = exchange(half_rotate(places, rows, rights, 0))
+    rows, *lefts, across[0], across[1] = after(rows, *lefts, *across)
+    half = half_rotate(places, rows, rights, 1)
+    half, *lefts, across[0], across[1] = after(half, *lefts, *across)
+    second = exchange(half)
     lefts.append(shift(lefts[1], dy=1))
-    lefts += [shift(left, dx=1) for left in lefts[:3]]
-    columns = lax.all_to_all(half.reshape(128, 16, 512), AXES, 0, 0, tiled=True)
-    lefts.append(shift(lefts[3], dx=1))
+    lefts += [across[0], across[1], shift(lefts[2], dx=1), shift(across[1], dy=1)]
     lefts += [swap_core(left) for left in lefts]
-    return final_rotate(jnp.stack(left_order(y, core) + places), lefts, columns.reshape(8, 16, 16, 512))
+    order = jnp.concatenate([jnp.stack(left_order(y, core)), places])
+    begun = final_rotate(order, lefts, first, 0)
+    return final_rotate(order, lefts, second, 1, (begun,))
 
 
 def left_order(y, core):

time: 138 us -> 129 us (0.935)
  waiting for transfers between devices: 54.8 us -> 27.1 us
  Pallas kernels: 20.9 us -> 32.1 us
  starting transfers between devices: 49.4 us -> 56.9 us
    ppermute x33, waiting for transfers between devices: 54.8 us -> 18.8 us  [send(): return lax.ppermute(value, AXES, moves)]
    all_to_all x1 -> x2, waiting for transfers between devices: 0.01 us -> 8.29 us  [exchange(): lax.all_to_all(half.reshape(128, 16, 256), AXES, 0, 0, tiled=True)]
    all_to_all x1 -> x2, starting transfers between devices: 3.73 us -> 11.8 us  [exchange(): lax.all_to_all(half.reshape(128, 16, 256), AXES, 0, 0, tiled=True)]
    pallas_call x1 -> x2, Pallas kernels: 9.91 us -> 15.6 us  [half_rotate(): pl.pallas_call(half_kernel, grid_spec=pltpu.PrefetchScalarGridSpec(num_sc...]
    pallas_call x1 -> x2, Pallas kernels: 9.7 us -> 15.2 us  [final_rotate(): pl.pallas_call(final_kernel, grid_spec=pltpu.PrefetchScalarGridSpec(num_s...]
  transfers between devices with their start and end apart: 35 -> 36, of which waited for: 7 -> 10; matrix products, arithmetic and copies ran while one was open for 7% -> 8% of each run, Pallas kernels for 8% -> 19%
where the time goes in v4:
time: 129 us
  starting transfers between devices  56.9 us (44%)
  Pallas kernels  32.1 us (25%)
  waiting for transfers between devices  27.1 us (21%)
  local copies, waits for them, and re-layouts  6.78 us (5%)
  matrix products  4.59 us (4%)
    ppermute x33, starting transfers between devices, send(): return lax.ppermute(value, AXES, moves)  39.3 us
    ppermute x33, waiting for transfers between devices, send(): return lax.ppermute(value, AXES, moves)  18.8 us
    pallas_call x2, Pallas kernels, half_rotate(): pl.pallas_call(half_kernel, grid_spec=pltpu.PrefetchScalarGridSpec(num_sc...  15.6 us
    pallas_call x2, Pallas kernels, final_rotate(): pl.pallas_call(final_kernel, grid_spec=pltpu.PrefetchScalarGridSpec(num_s...  15.2 us
    all_to_all x2, starting transfers between devices, exchange(): lax.all_to_all(half.reshape(128, 16, 256), AXES, 0, 0, tiled=True)  11.8 us
    all_to_all x2, waiting for transfers between devices, exchange(): lax.all_to_all(half.reshape(128, 16, 256), AXES, 0, 0, tiled=True)  8.29 us
    all_to_all x1, starting transfers between devices, shards(): pieces = lax.all_to_all(pieces, PAIR, 0, 0, tiled=True).reshape(512, 2048)  5.8 us
    dot_general x1, matrix products, spread_coupling(): jnp.dot(selector(target_index, npairs), integrals, precision=lax.Precisio...  3.84 us
  transfers between devices with their start and end apart: 36, of which 10 were waited for; matrix products, arithmetic and copies ran while one was open for 8% of the time, Pallas kernels for 19%

profile of v4, /device:TPU:1, one launch (start us, length us, event | category | flops | bytes accessed | tf_op | source)
XLA Modules:
  0.0 128.8 jit_solution(3688775256614127349)
XLA Ops:
  0.0 4.4 %collective-permute-start.6 = (bf16[128,2048]{1,0:T(8,128)(2,1)}, bf16[128,2048]{1,0:T(8,128)(2,1)}, u32[]{:S(2)}, u32[]{:S(2)}) collective-permute-start(bf16[128,2048]{1,0:T(8,128)(2,1)} %refs_0_.1), channel_id=1, source_target_pairs={{0,4},{1,5},{2,6},{3,7},{4,0},{5,1},{6,2},{7,3},{32,36},{33,37},{3... | collective-permute-start | bytes 1572872 | tf_op jit(solution)/shard_map/ppermute | solution.py:29
  7.1 2.5 %collective-permute-start = (bf16[128,2048]{1,0:T(8,128)(2,1)}, bf16[128,2048]{1,0:T(8,128)(2,1)}, u32[]{:S(2)}, u32[]{:S(2)}) collective-permute-start(bf16[128,2048]{1,0:T(8,128)(2,1)} %refs_0_.1), channel_id=1, source_target_pairs={{0,8},{1,25},{2,10},{3,27},{4,12},{5,29},{6,14},{7,31},{32,40},{33... | collective-permute-start | bytes 1572872 | tf_op jit(solution)/shard_map/ppermute | solution.py:29
  9.6 3.2 %copy.10 = bf16[4,8,16,2048]{3,2,0,1:T(8,128)(2,1)} copy(bf16[4,8,16,2048]{3,2,1,0:T(8,128)(2,1)} %bitcast.43) | data formatting | bytes 4194304 | tf_op jit(solution)/shard_map/reshape | solution.py:155
  12.8 5.8 %all-to-all-start = ((bf16[8,4,16,2048]{3,2,1,0:T(8,128)(2,1)}), bf16[8,4,16,2048]{3,2,1,0:T(8,128)(2,1)S(1)}, u32[]{:S(2)}, u32[]{:S(2)}) async-start(bf16[8,4,16,2048]{3,2,1,0:T(8,128)(2,1)} %bitcast.38), calls=%async_computation | async-start | bytes 4194304 | tf_op jit(solution)/shard_map/all_to_all | solution.py:156
  18.6 3.8 %fusion.3 = f32[32,1024]{1,0:T(8,128)S(1)} fusion(f32[1024,1024]{1,0:T(8,128)} %param.9, s32[32]{0:T(128)S(1)} %copy-done.6), kind=kOutput, calls=%fused_computation.12 | convolution fusion | flops 402685952 | bytes 4325504 | tf_op jit(solution)/shard_map/dot_general | solution.py:50
  25.6 3.4 %collective-permute-done.5.refs_2_ = bf16[128,2048]{1,0:T(8,128)(2,1)} collective-permute-done((bf16[128,2048]{1,0:T(8,128)(2,1)}, bf16[128,2048]{1,0:T(8,128)(2,1)}, u32[]{:S(2)}, u32[]{:S(2)}) %collective-permute-start.5) | collective-permute-done | bytes 524320 | tf_op jit(solution)/shard_map/ppermute | solution.py:29
  29.1 2.0 %collective-permute-start.13 = (bf16[128,2048]{1,0:T(8,128)(2,1)}, bf16[128,2048]{1,0:T(8,128)(2,1)}, u32[]{:S(2)}, u32[]{:S(2)}) collective-permute-start(bf16[128,2048]{1,0:T(8,128)(2,1)} %collective-permute-done.6.refs_3_), channel_id=1, source_target_pairs={{0,1},{1,0},{2,3},{3,2},{4,5},{5,4},{6,7},{7,6},{32,33},{33,32},{3... | collective-permute-start | bytes 1572872 | tf_op jit(solution)/shard_map/ppermute | solution.py:29
  31.1 2.6 %collective-permute-start.9 = (bf16[128,2048]{1,0:T(8,128)(2,1)}, bf16[128,2048]{1,0:T(8,128)(2,1)}, u32[]{:S(2)}, u32[]{:S(2)}) collective-permute-start(bf16[128,2048]{1,0:T(8,128)(2,1)} %collective-permute-done.6.refs_3_), channel_id=1, source_target_pairs={{0,8},{1,25},{2,10},{3,27},{4,12},{5,29},{6,14},{7,31},{32,40},{33... | collective-permute-start | bytes 1572872 | tf_op jit(solution)/shard_map/ppermute | solution.py:29
  34.6 2.5 %collective-permute-start.7 = (bf16[128,2048]{1,0:T(8,128)(2,1)}, bf16[128,2048]{1,0:T(8,128)(2,1)}, u32[]{:S(2)}, u32[]{:S(2)}) collective-permute-start(bf16[128,2048]{1,0:T(8,128)(2,1)} %collective-permute-done.refs_4_), channel_id=1, source_target_pairs={{0,2},{1,7},{2,4},{3,1},{4,6},{5,3},{6,0},{7,5},{32,34},{33,39},{3... | collective-permute-start | bytes 1572872 | tf_op jit(solution)/shard_map/ppermute | solution.py:29
  37.7 10.5 %collective-permute-done.9.refs_7_ = bf16[128,2048]{1,0:T(8,128)(2,1)} collective-permute-done((bf16[128,2048]{1,0:T(8,128)(2,1)}, bf16[128,2048]{1,0:T(8,128)(2,1)}, u32[]{:S(2)}, u32[]{:S(2)}) %collective-permute-start.9) | collective-permute-done | bytes 524320 | tf_op jit(solution)/shard_map/ppermute | solution.py:29
  48.2 3.4 %collective-permute-start.11 = (bf16[128,2048]{1,0:T(8,128)(2,1)}, bf16[128,2048]{1,0:T(8,128)(2,1)}, u32[]{:S(2)}, u32[]{:S(2)}) collective-permute-start(bf16[128,2048]{1,0:T(8,128)(2,1)} %collective-permute-done.4.refs_1_), channel_id=1, source_target_pairs={{0,1},{1,0},{2,3},{3,2},{4,5},{5,4},{6,7},{7,6},{32,33},{33,32},{3... | collective-permute-start | bytes 1572872 | tf_op jit(solution)/shard_map/ppermute | solution.py:29
  55.7 2.5 %collective-permute-start.21 = (bf16[128,2048]{1,0:T(8,128)(2,1)}, bf16[128,2048]{1,0:T(8,128)(2,1)S(1)}, u32[]{:S(2)}, u32[]{:S(2)}) collective-permute-start(bf16[128,2048]{1,0:T(8,128)(2,1)} %pad_maximum_fusion.refs_0_), channel_id=1, source_target_pairs={{0,40},{1,121},{2,42},{3,123},{4,44},{5,125},{6,46},{7,127},{32,72... | collective-permute-start | bytes 1572872 | tf_op jit(solution)/shard_map/ppermute | solution.py:29
  58.6 2.7 %collective-permute-start.18 = (bf16[128,2048]{1,0:T(8,128)(2,1)}, bf16[128,2048]{1,0:T(8,128)(2,1)}, u32[]{:S(2)}, u32[]{:S(2)}) collective-permute-start(bf16[128,2048]{1,0:T(8,128)(2,1)} %pad_maximum_fusion.refs_0_), channel_id=1, source_target_pairs={{0,32},{1,97},{2,34},{3,99},{4,36},{5,101},{6,38},{7,103},{32,64},... | collective-permute-start | bytes 1572872 | tf_op jit(solution)/shard_map/ppermute | solution.py:29
  61.9 7.8 %half.3 = bf16[8,16,16,256]{3,2,1,0:T(8,128)(2,1)} custom-call(s32[16]{0:T(128)} %stack.117.order, bf16[8,4,16,2048]{3,2,1,0:T(8,128)(2,1)} %bitcast.35, bf16[128,2048]{1,0:T(8,128)(2,1)} %refs_0_.1, bf16[128,2048]{1,0:T(8,128)(2,1)} %collective-permute-done.4.refs_1_, bf16[128,2048]{1,0:T(8,128)(2,1)} %collective-permute-done.5.refs_2_, ...), custom_call_target="tpu_custom_call" | custom-call | tf_op jit(solution)/shard_map/half/pallas_call | solution.py:90
  69.7 7.2 %all-to-all-start.2 = ((bf16[128,16,256]{2,1,0:T(8,128)(2,1)}), bf16[128,16,256]{2,1,0:T(8,128)(2,1)S(1)}, u32[]{:S(2)}, u32[]{:S(2)}) async-start(bf16[128,16,256]{2,1,0:T(8,128)(2,1)} %bitcast.41), calls=%async_computation.2 | async-start | bytes 2097152 | tf_op jit(solution)/shard_map/all_to_all | solution.py:174
  76.9 2.5 %collective-permute-done.19.refs_2_ = bf16[128,2048]{1,0:T(8,128)(2,1)} collective-permute-done((bf16[128,2048]{1,0:T(8,128)(2,1)}, bf16[128,2048]{1,0:T(8,128)(2,1)}, u32[]{:S(2)}, u32[]{:S(2)}) %collective-permute-start.19) | collective-permute-done | bytes 524320 | tf_op jit(solution)/shard_map/ppermute | solution.py:29
  79.4 7.8 %half.2 = bf16[8,16,16,256]{3,2,1,0:T(8,128)(2,1)} custom-call(s32[16]{0:T(128)} %stack.117.order, bf16[8,4,16,2048]{3,2,1,0:T(8,128)(2,1)} %bitcast.36, bf16[128,2048]{1,0:T(8,128)(2,1)} %refs_0_.1, bf16[128,2048]{1,0:T(8,128)(2,1)} %collective-permute-done.4.refs_1_, bf16[128,2048]{1,0:T(8,128)(2,1)} %collective-permute-done.5.refs_2_, ...), custom_call_target="tpu_custom_call" | custom-call | tf_op jit(solution)/shard_map/half/pallas_call | solution.py:90
  88.9 1.9 %collective-permute-start.23 = (bf16[128,2048]{1,0:T(8,128)(2,1)}, bf16[128,2048]{1,0:T(8,128)(2,1)}, u32[]{:S(2)}, u32[]{:S(2)}) collective-permute-start(bf16[128,2048]{1,0:T(8,128)(2,1)} %collective-permute-done.19.refs_2_), channel_id=1, source_target_pairs={{0,8},{1,25},{2,10},{3,27},{4,12},{5,29},{6,14},{7,31},{32,40},{33... | collective-permute-start | bytes 1572872 | tf_op jit(solution)/shard_map/ppermute | solution.py:29
  91.3 4.7 %all-to-all-done.2 = bf16[128,16,256]{2,1,0:T(8,128)(2,1)S(1)} async-done(((bf16[128,16,256]{2,1,0:T(8,128)(2,1)}), bf16[128,16,256]{2,1,0:T(8,128)(2,1)S(1)}, u32[]{:S(2)}, u32[]{:S(2)}) %all-to-all-start.2) | async-done | bytes 1048608 | tf_op jit(solution)/shard_map/all_to_all | solution.py:174
  96.1 4.6 %all-to-all-start.1 = ((bf16[128,16,256]{2,1,0:T(8,128)(2,1)}), bf16[128,16,256]{2,1,0:T(8,128)(2,1)S(1)}, u32[]{:S(2)}, u32[]{:S(2)}) async-start(bf16[128,16,256]{2,1,0:T(8,128)(2,1)} %bitcast.40), calls=%async_computation.1 | async-start | bytes 2097152 | tf_op jit(solution)/shard_map/all_to_all | solution.py:174
  103.1 3.8 %collective-permute-start.32 = (bf16[128,2048]{1,0:T(8,128)(2,1)}, bf16[128,2048]{1,0:T(8,128)(2,1)}, u32[]{:S(2)}, u32[]{:S(2)}) collective-permute-start(bf16[128,2048]{1,0:T(8,128)(2,1)} %collective-permute-done.24.refs_7_), channel_id=1, source_target_pairs={{0,1},{1,0},{2,3},{3,2},{4,5},{5,4},{6,7},{7,6},{32,33},{33,32},{3... | collective-permute-start | bytes 1572872 | tf_op jit(solution)/shard_map/ppermute | solution.py:29
  108.8 7.6 %final.2.refs_17_ = bf16[4,2048,128]{2,1,0:T(8,128)(2,1)} custom-call(s32[48]{0:T(128)} %concatenate.7.order, bf16[128,2048]{1,0:T(8,128)(2,1)} %pad_maximum_fusion.refs_0_, bf16[128,2048]{1,0:T(8,128)(2,1)} %collective-permute-done.18.refs_1_, bf16[128,2048]{1,0:T(8,128)(2,1)} %collective-permute-done.19.refs_2_, ...), custom_call_target="tpu_custom_call" | custom-call | flops 2147483648 | bytes 10485760 | tf_op jit(solution)/shard_map/final/pallas_call | solution.py:126
  116.4 3.6 %all-to-all-done.1 = bf16[128,16,256]{2,1,0:T(8,128)(2,1)S(1)} async-done(((bf16[128,16,256]{2,1,0:T(8,128)(2,1)}), bf16[128,16,256]{2,1,0:T(8,128)(2,1)S(1)}, u32[]{:S(2)}, u32[]{:S(2)}) %all-to-all-start.1) | async-done | bytes 1048608 | tf_op jit(solution)/shard_map/all_to_all | solution.py:174
  121.0 7.6 %final.3 = bf16[4,2048,128]{2,1,0:T(8,128)(2,1)} custom-call(s32[48]{0:T(128)} %concatenate.7.order, bf16[128,2048]{1,0:T(8,128)(2,1)} %pad_maximum_fusion.refs_0_, bf16[128,2048]{1,0:T(8,128)(2,1)} %collective-permute-done.18.refs_1_, bf16[128,2048]{1,0:T(8,128)(2,1)} %collective-permute-done.19.refs_2_, ...), custom_call_target="tpu_custom_call", output_to_operand_aliasing={{}: (18, {})} | custom-call | flops 2147483648 | bytes 10485760 | tf_op jit(solution)/shard_map/final/pallas_call | solution.py:126
  (80 shorter events, 19.8 us)
Async XLA Ops:
  0.0 24.1 %collective-permute-start.6 = (bf16[128,2048]{1,0:T(8,128)(2,1)}, bf16[128,2048]{1,0:T(8,128)(2,1)}, u32[]{:S(2)}, u32[]{:S(2)}) collective-permute-start(bf16[128,2048]{1,0:T(8,128)(2,1)} %refs_0_.1), channel_id=1, source_target_pairs={{0,4},{1,5},{2,6},{3,7},{4,0},{5,1},{6,2},{7,3},{32,36},{33,37},{3... | collective-permute-start | bytes 1572872 | tf_op jit(solution)/shard_map/ppermute | solution.py:29
  4.4 24.6 %collective-permute-start.5 = (bf16[128,2048]{1,0:T(8,128)(2,1)}, bf16[128,2048]{1,0:T(8,128)(2,1)}, u32[]{:S(2)}, u32[]{:S(2)}) collective-permute-start(bf16[128,2048]{1,0:T(8,128)(2,1)} %refs_0_.1), channel_id=1, source_target_pairs={{0,6},{1,3},{2,0},{3,5},{4,2},{5,7},{6,4},{7,1},{32,38},{33,35},{3... | collective-permute-start | bytes 1572872 | tf_op jit(solution)/shard_map/ppermute | solution.py:29
  5.2 24.0 %collective-permute-start.4 = (bf16[128,2048]{1,0:T(8,128)(2,1)}, bf16[128,2048]{1,0:T(8,128)(2,1)}, u32[]{:S(2)}, u32[]{:S(2)}) collective-permute-start(bf16[128,2048]{1,0:T(8,128)(2,1)} %refs_0_.1), channel_id=1, source_target_pairs={{0,2},{1,7},{2,4},{3,1},{4,6},{5,3},{6,0},{7,5},{32,34},{33,39},{3... | collective-permute-start | bytes 1572872 | tf_op jit(solution)/shard_map/ppermute | solution.py:29
  7.1 16.1 %collective-permute-start = (bf16[128,2048]{1,0:T(8,128)(2,1)}, bf16[128,2048]{1,0:T(8,128)(2,1)}, u32[]{:S(2)}, u32[]{:S(2)}) collective-permute-start(bf16[128,2048]{1,0:T(8,128)(2,1)} %refs_0_.1), channel_id=1, source_target_pairs={{0,8},{1,25},{2,10},{3,27},{4,12},{5,29},{6,14},{7,31},{32,40},{33... | collective-permute-start | bytes 1572872 | tf_op jit(solution)/shard_map/ppermute | solution.py:29
  9.6 21.6 %collective-permute-start.10 = (bf16[128,2048]{1,0:T(8,128)(2,1)}, bf16[128,2048]{1,0:T(8,128)(2,1)}, u32[]{:S(2)}, u32[]{:S(2)}) collective-permute-start(bf16[128,2048]{1,0:T(8,128)(2,1)} %refs_0_.1), channel_id=1, source_target_pairs={{0,1},{1,0},{2,3},{3,2},{4,5},{5,4},{6,7},{7,6},{32,33},{33,32},{3... | collective-permute-start | bytes 1572872 | tf_op jit(solution)/shard_map/ppermute | solution.py:29
  12.8 40.3 %all-to-all-start = ((bf16[8,4,16,2048]{3,2,1,0:T(8,128)(2,1)}), bf16[8,4,16,2048]{3,2,1,0:T(8,128)(2,1)S(1)}, u32[]{:S(2)}, u32[]{:S(2)}) async-start(bf16[8,4,16,2048]{3,2,1,0:T(8,128)(2,1)} %bitcast.38), calls=%async_computation | async-start | bytes 4194304 | tf_op jit(solution)/shard_map/all_to_all | solution.py:156
  23.3 10.5 %collective-permute-start.3 = (bf16[32,2048]{1,0:T(8,128)(2,1)S(1)}, bf16[32,2048]{1,0:T(8,128)(2,1)S(1)}, u32[]{:S(2)}, u32[]{:S(2)}) collective-permute-start(bf16[32,2048]{1,0:T(8,128)(2,1)S(1)} %constant_dynamic-slice_fusion), channel_id=1, source_target_pairs={{0,4},{1,5},{2,6},{3,7},{4,0},{5,1},{6,2},{7,3},{32,36},{33,37},{3... | collective-permute-start | bytes 393224 | tf_op jit(solution)/shard_map/ppermute | solution.py:29
  24.1 9.6 %collective-permute-start.2 = (bf16[32,2048]{1,0:T(8,128)(2,1)S(1)}, bf16[32,2048]{1,0:T(8,128)(2,1)S(1)}, u32[]{:S(2)}, u32[]{:S(2)}) collective-permute-start(bf16[32,2048]{1,0:T(8,128)(2,1)S(1)} %constant_dynamic-slice_fusion), channel_id=1, source_target_pairs={{0,6},{1,3},{2,0},{3,5},{4,2},{5,7},{6,4},{7,1},{32,38},{33,35},{3... | collective-permute-start | bytes 393224 | tf_op jit(solution)/shard_map/ppermute | solution.py:29
  31.1 17.0 %collective-permute-start.9 = (bf16[128,2048]{1,0:T(8,128)(2,1)}, bf16[128,2048]{1,0:T(8,128)(2,1)}, u32[]{:S(2)}, u32[]{:S(2)}) collective-permute-start(bf16[128,2048]{1,0:T(8,128)(2,1)} %collective-permute-done.6.refs_3_), channel_id=1, source_target_pairs={{0,8},{1,25},{2,10},{3,27},{4,12},{5,29},{6,14},{7,31},{32,40},{33... | collective-permute-start | bytes 1572872 | tf_op jit(solution)/shard_map/ppermute | solution.py:29
  33.7 17.9 %collective-permute-start.12 = (bf16[128,2048]{1,0:T(8,128)(2,1)}, bf16[128,2048]{1,0:T(8,128)(2,1)}, u32[]{:S(2)}, u32[]{:S(2)}) collective-permute-start(bf16[128,2048]{1,0:T(8,128)(2,1)} %collective-permute-done.5.refs_2_), channel_id=1, source_target_pairs={{0,1},{1,0},{2,3},{3,2},{4,5},{5,4},{6,7},{7,6},{32,33},{33,32},{3... | collective-permute-start | bytes 1572872 | tf_op jit(solution)/shard_map/ppermute | solution.py:29
  33.7 17.9 %collective-permute-start.8 = (bf16[128,2048]{1,0:T(8,128)(2,1)}, bf16[128,2048]{1,0:T(8,128)(2,1)}, u32[]{:S(2)}, u32[]{:S(2)}) collective-permute-start(bf16[128,2048]{1,0:T(8,128)(2,1)} %collective-permute-done.refs_4_), channel_id=1, source_target_pairs={{0,6},{1,3},{2,0},{3,5},{4,2},{5,7},{6,4},{7,1},{32,38},{33,35},{3... | collective-permute-start | bytes 1572872 | tf_op jit(solution)/shard_map/ppermute | solution.py:29
  34.6 17.6 %collective-permute-start.7 = (bf16[128,2048]{1,0:T(8,128)(2,1)}, bf16[128,2048]{1,0:T(8,128)(2,1)}, u32[]{:S(2)}, u32[]{:S(2)}) collective-permute-start(bf16[128,2048]{1,0:T(8,128)(2,1)} %collective-permute-done.refs_4_), channel_id=1, source_target_pairs={{0,2},{1,7},{2,4},{3,1},{4,6},{5,3},{6,0},{7,5},{32,34},{33,39},{3... | collective-permute-start | bytes 1572872 | tf_op jit(solution)/shard_map/ppermute | solution.py:29
  37.1 18.6 %collective-permute-start.14 = (bf16[128,2048]{1,0:T(8,128)(2,1)}, bf16[128,2048]{1,0:T(8,128)(2,1)}, u32[]{:S(2)}, u32[]{:S(2)}) collective-permute-start(bf16[128,2048]{1,0:T(8,128)(2,1)} %collective-permute-done.refs_4_), channel_id=1, source_target_pairs={{0,1},{1,0},{2,3},{3,2},{4,5},{5,4},{6,7},{7,6},{32,33},{33,32},{3... | collective-permute-start | bytes 1572872 | tf_op jit(solution)/shard_map/ppermute | solution.py:29
  55.7 21.1 %collective-permute-start.21 = (bf16[128,2048]{1,0:T(8,128)(2,1)}, bf16[128,2048]{1,0:T(8,128)(2,1)S(1)}, u32[]{:S(2)}, u32[]{:S(2)}) collective-permute-start(bf16[128,2048]{1,0:T(8,128)(2,1)} %pad_maximum_fusion.refs_0_), channel_id=1, source_target_pairs={{0,40},{1,121},{2,42},{3,123},{4,44},{5,125},{6,46},{7,127},{32,72... | collective-permute-start | bytes 1572872 | tf_op jit(solution)/shard_map/ppermute | solution.py:29
  58.2 18.7 %collective-permute-start.20 = (bf16[128,2048]{1,0:T(8,128)(2,1)}, bf16[128,2048]{1,0:T(8,128)(2,1)}, u32[]{:S(2)}, u32[]{:S(2)}) collective-permute-start(bf16[128,2048]{1,0:T(8,128)(2,1)} %pad_maximum_fusion.refs_0_), channel_id=1, source_target_pairs={{0,8},{1,25},{2,10},{3,27},{4,12},{5,29},{6,14},{7,31},{32,40},{33... | collective-permute-start | bytes 1572872 | tf_op jit(solution)/shard_map/ppermute | solution.py:29
  58.6 20.8 %collective-permute-start.19 = (bf16[128,2048]{1,0:T(8,128)(2,1)}, bf16[128,2048]{1,0:T(8,128)(2,1)}, u32[]{:S(2)}, u32[]{:S(2)}) collective-permute-start(bf16[128,2048]{1,0:T(8,128)(2,1)} %pad_maximum_fusion.refs_0_), channel_id=1, source_target_pairs={{0,96},{1,33},{2,98},{3,35},{4,100},{5,37},{6,102},{7,39},{32,0},{... | collective-permute-start | bytes 1572872 | tf_op jit(solution)/shard_map/ppermute | solution.py:29
  58.6 20.8 %collective-permute-start.18 = (bf16[128,2048]{1,0:T(8,128)(2,1)}, bf16[128,2048]{1,0:T(8,128)(2,1)}, u32[]{:S(2)}, u32[]{:S(2)}) collective-permute-start(bf16[128,2048]{1,0:T(8,128)(2,1)} %pad_maximum_fusion.refs_0_), channel_id=1, source_target_pairs={{0,32},{1,97},{2,34},{3,99},{4,36},{5,101},{6,38},{7,103},{32,64},... | collective-permute-start | bytes 1572872 | tf_op jit(solution)/shard_map/ppermute | solution.py:29
  69.7 26.4 %all-to-all-start.2 = ((bf16[128,16,256]{2,1,0:T(8,128)(2,1)}), bf16[128,16,256]{2,1,0:T(8,128)(2,1)S(1)}, u32[]{:S(2)}, u32[]{:S(2)}) async-start(bf16[128,16,256]{2,1,0:T(8,128)(2,1)} %bitcast.41), calls=%async_computation.2 | async-start | bytes 2097152 | tf_op jit(solution)/shard_map/all_to_all | solution.py:174
  88.0 12.7 %collective-permute-start.29 = (bf16[128,2048]{1,0:T(8,128)(2,1)}, bf16[128,2048]{1,0:T(8,128)(2,1)}, u32[]{:S(2)}, u32[]{:S(2)}) collective-permute-start(bf16[128,2048]{1,0:T(8,128)(2,1)} %collective-permute-done.20.refs_4_), channel_id=1, source_target_pairs={{0,1},{1,0},{2,3},{3,2},{4,5},{5,4},{6,7},{7,6},{32,33},{33,32},{3... | collective-permute-start | bytes 1572872 | tf_op jit(solution)/shard_map/ppermute | solution.py:29
  88.1 13.9 %collective-permute-start.26 = (bf16[128,2048]{1,0:T(8,128)(2,1)}, bf16[128,2048]{1,0:T(8,128)(2,1)}, u32[]{:S(2)}, u32[]{:S(2)}) collective-permute-start(bf16[128,2048]{1,0:T(8,128)(2,1)} %collective-permute-done.18.refs_1_), channel_id=1, source_target_pairs={{0,1},{1,0},{2,3},{3,2},{4,5},{5,4},{6,7},{7,6},{32,33},{33,32},{3... | collective-permute-start | bytes 1572872 | tf_op jit(solution)/shard_map/ppermute | solution.py:29
  88.5 13.6 %collective-permute-start.22 = (bf16[128,2048]{1,0:T(8,128)(2,1)}, bf16[128,2048]{1,0:T(8,128)(2,1)}, u32[]{:S(2)}, u32[]{:S(2)}) collective-permute-start(bf16[128,2048]{1,0:T(8,128)(2,1)} %collective-permute-done.18.refs_1_), channel_id=1, source_target_pairs={{0,32},{1,97},{2,34},{3,99},{4,36},{5,101},{6,38},{7,103},{32,64},... | collective-permute-start | bytes 1572872 | tf_op jit(solution)/shard_map/ppermute | solution.py:29
  88.9 13.6 %collective-permute-start.23 = (bf16[128,2048]{1,0:T(8,128)(2,1)}, bf16[128,2048]{1,0:T(8,128)(2,1)}, u32[]{:S(2)}, u32[]{:S(2)}) collective-permute-start(bf16[128,2048]{1,0:T(8,128)(2,1)} %collective-permute-done.19.refs_2_), channel_id=1, source_target_pairs={{0,8},{1,25},{2,10},{3,27},{4,12},{5,29},{6,14},{7,31},{32,40},{33... | collective-permute-start | bytes 1572872 | tf_op jit(solution)/shard_map/ppermute | solution.py:29
  90.8 12.3 %collective-permute-start.24 = (bf16[128,2048]{1,0:T(8,128)(2,1)S(1)}, bf16[128,2048]{1,0:T(8,128)(2,1)}, u32[]{:S(2)}, u32[]{:S(2)}) collective-permute-start(bf16[128,2048]{1,0:T(8,128)(2,1)S(1)} %collective-permute-done.21.refs_5_), channel_id=1, source_target_pairs={{0,32},{1,97},{2,34},{3,99},{4,36},{5,101},{6,38},{7,103},{32,64},... | collective-permute-start | bytes 1572872 | tf_op jit(solution)/shard_map/ppermute | solution.py:29
  96.1 23.9 %all-to-all-start.1 = ((bf16[128,16,256]{2,1,0:T(8,128)(2,1)}), bf16[128,16,256]{2,1,0:T(8,128)(2,1)S(1)}, u32[]{:S(2)}, u32[]{:S(2)}) async-start(bf16[128,16,256]{2,1,0:T(8,128)(2,1)} %bitcast.40), calls=%async_computation.1 | async-start | bytes 2097152 | tf_op jit(solution)/shard_map/all_to_all | solution.py:174
  (20 other events, 143.3 us)

commit v5 on v4

--- a/solution.py
+++ b/solution.py
@@ -10,7 +10,8 @@
 MAT = ("xl", "z", "core")
 BF = jnp.bfloat16
 F32 = jnp.float32
-HALF, FINAL = 56, 56
+HALF, FINAL = 56, 16
+SLICES = 2
 
 
 def place(x, y, z, core):
@@ -74,28 +75,46 @@
 
 
 def half_kernel(order, rows, *refs):
-    *rights, out, natural = refs
-    for n, right in enumerate(rights):
-        natural[pl.ds(pl.multiple_of(order[n] * 128, 128), 128), :] = right[...]
-    total = jnp.dot(rows[...].reshape(256, 2048), natural[...], preferred_element_type=F32).astype(BF)
-    for p in range(8):
-        for m in range(out.shape[1]):
-            for t in range(2):
-                top = (p * 2 + t) * 16
-                out[p, m, :, t * 128 : t * 128 + 128] = total[top : top + 16, m * 128 : m * 128 + 128]
+    rights, (out, natural, arrived) = refs[:16], refs[16:]
+    width = 2048 // SLICES
+    copies = [
+        [
+            pltpu.make_async_copy(
+                right.at[:, part * width : (part + 1) * width],
+                natural.at[pl.ds(pl.multiple_of(order[n] * 128, 128), 128), part * width : (part + 1) * width],
+                arrived.at[part, n],
+            )
+            for n, right in enumerate(rights)
+        ]
+        for part in range(SLICES)
+    ]
+    for copy in sum(copies, []):
+        copy.start()
+    own = rows[...].reshape(256, 2048)
+    for part in range(SLICES):
+        for copy in copies[part]:
+            copy.wait()
+        for left in range(part * width, (part + 1) * width, 512):
+            total = jnp.dot(own, natural[:, left : left + 512], preferred_element_type=F32).astype(BF)
+            for p in range(8):
+                for m in range(4):
+                    for t in range(2):
+                        top = (p * 2 + t) * 16
+                        out[p, left // 128 + m, :, t * 128 : t * 128 + 128] = total[
+                            top : top + 16, m * 128 : m * 128 + 128
+                        ]
 
 
 def half_rotate(order, rows, rights, part):
-    width = 512
     return pl.pallas_call(
         half_kernel,
         grid_spec=pltpu.PrefetchScalarGridSpec(
             num_scalar_prefetch=1,
-            grid=(2048 // width,),
+            grid=(1,),
             in_specs=[pl.BlockSpec((8, 2, 16, 2048), lambda i, o: (0, part, 0, 0))]
-            + [pl.BlockSpec((128, width), lambda i, o: (0, i)) for _ in rights],
-            out_specs=pl.BlockSpec((8, width // 128, 16, 256), lambda i, o: (0, i, 0, 0)),
-            scratch_shapes=[pltpu.VMEM((2048, width), BF)],
+            + [pl.BlockSpec(memory_space=pl.ANY) for _ in rights],
+            out_specs=pl.BlockSpec((8, 16, 16, 256), lambda i, o: (0, 0, 0, 0)),
+            scratch_shapes=[pltpu.VMEM((2048, 2048), BF), pltpu.SemaphoreType.DMA((SLICES, 16))],
         ),
         out_shape=jax.ShapeDtypeStruct((8, 16, 16, 256), BF),
         compiler_params=pltpu.CompilerParams(vmem_limit_bytes=HALF << 20),
@@ -104,35 +123,53 @@
 
 
 def final_kernel(order, *refs):
-    lefts, (columns, *_, out, rows) = refs[:16], refs[16:]
-
-    @pl.when(pl.program_id(0) == 0)
-    def _():
-        for n in range(len(lefts)):
-            for chip in range(4):
-                for p in range(2):
-                    top = n * 128 + chip * 32 + p * 16
-                    pair, place = order[2 * n] * 2 + p, order[2 * len(lefts) + (n // 4) * 4 + chip]
-                    rows[top : top + 16, :] = columns[pair, place]
-
-    left = jnp.concatenate([piece[...] for piece in lefts], axis=0)
-    total = lax.dot_general(left, rows[...], (((0,), (0,)), ((), ())), preferred_element_type=F32).astype(BF)
-    for t in range(2):
-        out[t] = total[:, t * 128 : t * 128 + 128]
+    lefts, (columns, *_, out, rows, whole, arrived) = refs[:16], refs[16:]
+    width = 2048 // SLICES
+    copies = [
+        [
+            pltpu.make_async_copy(
+                left.at[:, part * width : (part + 1) * width],
+                whole.at[n * 128 : n * 128 + 128, part * width : (part + 1) * width],
+                arrived.at[part, n],
+            )
+            for n, left in enumerate(lefts)
+        ]
+        for part in range(SLICES)
+    ]
+    for copy in sum(copies, []):
+        copy.start()
+    for n in range(len(lefts)):
+        for chip in range(4):
+            for p in range(2):
+                top = n * 128 + chip * 32 + p * 16
+                pair, place = order[2 * n] * 2 + p, order[2 * len(lefts) + (n // 4) * 4 + chip]
+                rows[top : top + 16, :] = columns[pair, place]
+    for part in range(SLICES):
+        for copy in copies[part]:
+            copy.wait()
+        for top in range(part * width, (part + 1) * width, 512):
+            total = lax.dot_general(
+                whole[:, top : top + 512], rows[...], (((0,), (0,)), ((), ())), preferred_element_type=F32
+            ).astype(BF)
+            for t in range(2):
+                out[t, top : top + 512] = total[:, t * 128 : t * 128 + 128]
 
 
 def final_rotate(order, lefts, columns, part, begun=()):
-    height = 512
     return pl.pallas_call(
         final_kernel,
         grid_spec=pltpu.PrefetchScalarGridSpec(
             num_scalar_prefetch=1,
-            grid=(2048 // height,),
-            in_specs=[pl.BlockSpec((128, height), lambda i, o: (0, i)) for _ in lefts]
+            grid=(1,),
+            in_specs=[pl.BlockSpec(memory_space=pl.ANY) for _ in lefts]
             + [pl.BlockSpec((8, 16, 16, 256), lambda i, o: (0, 0, 0, 0))]
             + [pl.BlockSpec(memory_space=pl.ANY) for _ in begun],
-            out_specs=pl.BlockSpec((2, height, 128), lambda i, o: (part, i, 0)),
-            scratch_shapes=[pltpu.VMEM((2048, 256), BF)],
+            out_specs=pl.BlockSpec((2, 2048, 128), lambda i, o: (part, 0, 0)),
+            scratch_shapes=[
+                pltpu.VMEM((2048, 256), BF),
+                pltpu.VMEM((2048, 2048), BF),
+                pltpu.SemaphoreType.DMA((SLICES, 16)),
+            ],
         ),
         out_shape=jax.ShapeDtypeStruct((4, 2048, 128), BF),
         input_output_aliases={18: 0} if begun else {},

time: 129 us -> 129 us (level)
  local copies, waits for them, and re-layouts: 6.78 us -> 9.52 us
  Pallas kernels: 32.1 us -> 29.9 us
    unnamed x16 -> x22, local copies, waits for them, and re-layouts: 2.35 us -> 5.54 us
    pallas_call x2, Pallas kernels: 15.2 us -> 12.9 us  [final_rotate(): pl.pallas_call(final_kernel, grid_spec=pltpu.PrefetchScalarGridSpec(num_s...]
    ppermute x33, waiting for transfers between devices: 18.8 us -> 17.1 us  [send(): return lax.ppermute(value, AXES, moves)]
  transfers between devices with their start and end apart: 36 -> 36, of which waited for: 10 -> 9; matrix products, arithmetic and copies ran while one was open for 8% -> 7% of each run, Pallas kernels for 19% -> 18%
where the time goes in v5:
time: 129 us; the launch traced here: 128 us
  starting transfers between devices  56.9 us (44%)
  Pallas kernels  29.9 us (23%)
  waiting for transfers between devices  26.2 us (20%)
  local copies, waits for them, and re-layouts  9.52 us (7%)
  matrix products  5.4 us (4%)
    ppermute x33, starting transfers between devices, send(): return lax.ppermute(value, AXES, moves)  39.2 us
    ppermute x33, waiting for transfers between devices, send(): return lax.ppermute(value, AXES, moves)  17.1 us
    pallas_call x2, Pallas kernels, half_rotate(): pl.pallas_call(half_kernel, grid_spec=pltpu.PrefetchScalarGridSpec(num_sc...  15.7 us
    pallas_call x2, Pallas kernels, final_rotate(): pl.pallas_call(final_kernel, grid_spec=pltpu.PrefetchScalarGridSpec(num_s...  12.9 us
    all_to_all x2, starting transfers between devices, exchange(): lax.all_to_all(half.reshape(128, 16, 256), AXES, 0, 0, tiled=True)  11.9 us
    all_to_all x2, waiting for transfers between devices, exchange(): lax.all_to_all(half.reshape(128, 16, 256), AXES, 0, 0, tiled=True)  9.04 us
    all_to_all x1, starting transfers between devices, shards(): pieces = lax.all_to_all(pieces, PAIR, 0, 0, tiled=True).reshape(512, 2048)  5.8 us
    unnamed x22, local copies, waits for them, and re-layouts  5.54 us
  transfers between devices with their start and end apart: 36, of which 9 were waited for; matrix products, arithmetic and copies ran while one was open for 7% of the time, Pallas kernels for 18%

profile of v5, /device:TPU:1, one launch (start us, length us, event | category | flops | bytes accessed | tf_op | source)
XLA Modules:
  0.0 128.3 jit_solution(3987213461181300022)
XLA Ops:
  0.0 4.4 %collective-permute-start.6 = (bf16[128,2048]{1,0:T(8,128)(2,1)}, bf16[128,2048]{1,0:T(8,128)(2,1)S(1)}, u32[]{:S(2)}, u32[]{:S(2)}) collective-permute-start(bf16[128,2048]{1,0:T(8,128)(2,1)} %refs_0_.1), channel_id=1, source_target_pairs={{0,4},{1,5},{2,6},{3,7},{4,0},{5,1},{6,2},{7,3},{32,36},{33,37},{3... | collective-permute-start | bytes 1572872 | tf_op jit(solution)/shard_map/ppermute | solution.py:30
  5.2 1.9 %collective-permute-start.4 = (bf16[128,2048]{1,0:T(8,128)(2,1)}, bf16[128,2048]{1,0:T(8,128)(2,1)}, u32[]{:S(2)}, u32[]{:S(2)}) collective-permute-start(bf16[128,2048]{1,0:T(8,128)(2,1)} %refs_0_.1), channel_id=1, source_target_pairs={{0,2},{1,7},{2,4},{3,1},{4,6},{5,3},{6,0},{7,5},{32,34},{33,39},{3... | collective-permute-start | bytes 1572872 | tf_op jit(solution)/shard_map/ppermute | solution.py:30
  7.1 2.5 %collective-permute-start = (bf16[128,2048]{1,0:T(8,128)(2,1)}, bf16[128,2048]{1,0:T(8,128)(2,1)}, u32[]{:S(2)}, u32[]{:S(2)}) collective-permute-start(bf16[128,2048]{1,0:T(8,128)(2,1)} %refs_0_.1), channel_id=1, source_target_pairs={{0,8},{1,25},{2,10},{3,27},{4,12},{5,29},{6,14},{7,31},{32,40},{33... | collective-permute-start | bytes 1572872 | tf_op jit(solution)/shard_map/ppermute | solution.py:30
  9.6 3.2 %copy.10 = bf16[4,8,16,2048]{3,2,0,1:T(8,128)(2,1)} copy(bf16[4,8,16,2048]{3,2,1,0:T(8,128)(2,1)} %bitcast.43) | data formatting | bytes 4194304 | tf_op jit(solution)/shard_map/reshape | solution.py:192
  12.8 5.8 %all-to-all-start = ((bf16[8,4,16,2048]{3,2,1,0:T(8,128)(2,1)}), bf16[8,4,16,2048]{3,2,1,0:T(8,128)(2,1)S(1)}, u32[]{:S(2)}, u32[]{:S(2)}) async-start(bf16[8,4,16,2048]{3,2,1,0:T(8,128)(2,1)} %bitcast.40), calls=%async_computation | async-start | bytes 4194304 | tf_op jit(solution)/shard_map/all_to_all | solution.py:193
  18.6 3.8 %fusion.3 = f32[32,1024]{1,0:T(8,128)S(1)} fusion(f32[1024,1024]{1,0:T(8,128)} %param.9, s32[32]{0:T(128)S(1)} %copy-done.9), kind=kOutput, calls=%fused_computation.12 | convolution fusion | flops 402685952 | bytes 4325504 | tf_op jit(solution)/shard_map/dot_general | solution.py:51
  26.4 2.0 %collective-permute-done.5.refs_2_ = bf16[128,2048]{1,0:T(8,128)(2,1)} collective-permute-done((bf16[128,2048]{1,0:T(8,128)(2,1)}, bf16[128,2048]{1,0:T(8,128)(2,1)}, u32[]{:S(2)}, u32[]{:S(2)}) %collective-permute-start.5) | collective-permute-done | bytes 524320 | tf_op jit(solution)/shard_map/ppermute | solution.py:30
  30.8 2.6 %collective-permute-start.9 = (bf16[128,2048]{1,0:T(8,128)(2,1)S(1)}, bf16[128,2048]{1,0:T(8,128)(2,1)}, u32[]{:S(2)}, u32[]{:S(2)}) collective-permute-start(bf16[128,2048]{1,0:T(8,128)(2,1)S(1)} %collective-permute-done.6.refs_3_), channel_id=1, source_target_pairs={{0,8},{1,25},{2,10},{3,27},{4,12},{5,29},{6,14},{7,31},{32,40},{33... | collective-permute-start | bytes 1572872 | tf_op jit(solution)/shard_map/ppermute | solution.py:30
  34.4 2.7 %collective-permute-start.7 = (bf16[128,2048]{1,0:T(8,128)(2,1)}, bf16[128,2048]{1,0:T(8,128)(2,1)}, u32[]{:S(2)}, u32[]{:S(2)}) collective-permute-start(bf16[128,2048]{1,0:T(8,128)(2,1)} %collective-permute-done.refs_4_), channel_id=1, source_target_pairs={{0,2},{1,7},{2,4},{3,1},{4,6},{5,3},{6,0},{7,5},{32,34},{33,39},{3... | collective-permute-start | bytes 1572872 | tf_op jit(solution)/shard_map/ppermute | solution.py:30
  37.8 10.3 %collective-permute-done.9.refs_7_ = bf16[128,2048]{1,0:T(8,128)(2,1)} collective-permute-done((bf16[128,2048]{1,0:T(8,128)(2,1)S(1)}, bf16[128,2048]{1,0:T(8,128)(2,1)}, u32[]{:S(2)}, u32[]{:S(2)}) %collective-permute-start.9) | collective-permute-done | bytes 524320 | tf_op jit(solution)/shard_map/ppermute | solution.py:30
  48.1 3.5 %collective-permute-start.11 = (bf16[128,2048]{1,0:T(8,128)(2,1)}, bf16[128,2048]{1,0:T(8,128)(2,1)}, u32[]{:S(2)}, u32[]{:S(2)}) collective-permute-start(bf16[128,2048]{1,0:T(8,128)(2,1)} %collective-permute-done.4.refs_1_), channel_id=1, source_target_pairs={{0,1},{1,0},{2,3},{3,2},{4,5},{5,4},{6,7},{7,6},{32,33},{33,32},{3... | collective-permute-start | bytes 1572872 | tf_op jit(solution)/shard_map/ppermute | solution.py:30
  56.1 2.5 %collective-permute-start.21 = (bf16[128,2048]{1,0:T(8,128)(2,1)S(1)}, bf16[128,2048]{1,0:T(8,128)(2,1)}, u32[]{:S(2)}, u32[]{:S(2)}) collective-permute-start(bf16[128,2048]{1,0:T(8,128)(2,1)S(1)} %pad_maximum_fusion.refs_0_), channel_id=1, source_target_pairs={{0,40},{1,121},{2,42},{3,123},{4,44},{5,125},{6,46},{7,127},{32,72... | collective-permute-start | bytes 1572872 | tf_op jit(solution)/shard_map/ppermute | solution.py:30
  59.0 2.7 %collective-permute-start.18 = (bf16[128,2048]{1,0:T(8,128)(2,1)S(1)}, bf16[128,2048]{1,0:T(8,128)(2,1)}, u32[]{:S(2)}, u32[]{:S(2)}) collective-permute-start(bf16[128,2048]{1,0:T(8,128)(2,1)S(1)} %pad_maximum_fusion.refs_0_), channel_id=1, source_target_pairs={{0,32},{1,97},{2,34},{3,99},{4,36},{5,101},{6,38},{7,103},{32,64},... | collective-permute-start | bytes 1572872 | tf_op jit(solution)/shard_map/ppermute | solution.py:30
  62.4 7.8 %half.3 = bf16[8,16,16,256]{3,2,1,0:T(8,128)(2,1)} custom-call(s32[16]{0:T(128)} %stack.117.order, bf16[8,4,16,2048]{3,2,1,0:T(8,128)(2,1)} %bitcast.35, bf16[128,2048]{1,0:T(8,128)(2,1)} %refs_0_.1, bf16[128,2048]{1,0:T(8,128)(2,1)} %collective-permute-done.4.refs_1_, bf16[128,2048]{1,0:T(8,128)(2,1)} %collective-permute-done.5.refs_2_, ...), custom_call_target="tpu_custom_call" | custom-call | tf_op jit(solution)/shard_map/half/pallas_call | solution.py:109
  70.2 7.3 %all-to-all-start.2 = ((bf16[128,16,256]{2,1,0:T(8,128)(2,1)}), bf16[128,16,256]{2,1,0:T(8,128)(2,1)S(1)}, u32[]{:S(2)}, u32[]{:S(2)}) async-start(bf16[128,16,256]{2,1,0:T(8,128)(2,1)} %bitcast.42), calls=%async_computation.2 | async-start | bytes 2097152 | tf_op jit(solution)/shard_map/all_to_all | solution.py:211
  77.5 1.9 %collective-permute-done.19.refs_2_ = bf16[128,2048]{1,0:T(8,128)(2,1)} collective-permute-done((bf16[128,2048]{1,0:T(8,128)(2,1)S(1)}, bf16[128,2048]{1,0:T(8,128)(2,1)}, u32[]{:S(2)}, u32[]{:S(2)}) %collective-permute-start.19) | collective-permute-done | bytes 524320 | tf_op jit(solution)/shard_map/ppermute | solution.py:30
  79.4 7.8 %half.2 = bf16[8,16,16,256]{3,2,1,0:T(8,128)(2,1)} custom-call(s32[16]{0:T(128)} %stack.117.order, bf16[8,4,16,2048]{3,2,1,0:T(8,128)(2,1)} %bitcast.36, bf16[128,2048]{1,0:T(8,128)(2,1)} %refs_0_.1, bf16[128,2048]{1,0:T(8,128)(2,1)} %collective-permute-done.4.refs_1_, bf16[128,2048]{1,0:T(8,128)(2,1)} %collective-permute-done.5.refs_2_, ...), custom_call_target="tpu_custom_call" | custom-call | tf_op jit(solution)/shard_map/half/pallas_call | solution.py:109
  89.1 2.4 %collective-permute-start.23 = (bf16[128,2048]{1,0:T(8,128)(2,1)}, bf16[128,2048]{1,0:T(8,128)(2,1)}, u32[]{:S(2)}, u32[]{:S(2)}) collective-permute-start(bf16[128,2048]{1,0:T(8,128)(2,1)} %collective-permute-done.19.refs_2_), channel_id=1, source_target_pairs={{0,8},{1,25},{2,10},{3,27},{4,12},{5,29},{6,14},{7,31},{32,40},{33... | collective-permute-start | bytes 1572872 | tf_op jit(solution)/shard_map/ppermute | solution.py:30
  92.8 3.9 %all-to-all-done.2 = bf16[128,16,256]{2,1,0:T(8,128)(2,1)S(1)} async-done(((bf16[128,16,256]{2,1,0:T(8,128)(2,1)}), bf16[128,16,256]{2,1,0:T(8,128)(2,1)S(1)}, u32[]{:S(2)}, u32[]{:S(2)}) %all-to-all-start.2) | async-done | bytes 1048608 | tf_op jit(solution)/shard_map/all_to_all | solution.py:211
  96.7 4.6 %all-to-all-start.1 = ((bf16[128,16,256]{2,1,0:T(8,128)(2,1)}), bf16[128,16,256]{2,1,0:T(8,128)(2,1)S(1)}, u32[]{:S(2)}, u32[]{:S(2)}) async-start(bf16[128,16,256]{2,1,0:T(8,128)(2,1)} %bitcast.41), calls=%async_computation.1 | async-start | bytes 2097152 | tf_op jit(solution)/shard_map/all_to_all | solution.py:211
  103.6 2.5 %collective-permute-start.32 = (bf16[128,2048]{1,0:T(8,128)(2,1)}, bf16[128,2048]{1,0:T(8,128)(2,1)}, u32[]{:S(2)}, u32[]{:S(2)}) collective-permute-start(bf16[128,2048]{1,0:T(8,128)(2,1)} %collective-permute-done.24.refs_7_), channel_id=1, source_target_pairs={{0,1},{1,0},{2,3},{3,2},{4,5},{5,4},{6,7},{7,6},{32,33},{33,32},{3... | collective-permute-start | bytes 1572872 | tf_op jit(solution)/shard_map/ppermute | solution.py:30
  109.0 6.5 %final.2.refs_17_ = bf16[4,2048,128]{2,1,0:T(8,128)(2,1)} custom-call(s32[48]{0:T(128)S(1)} %concatenate.7.order, bf16[128,2048]{1,0:T(8,128)(2,1)S(1)} %pad_maximum_fusion.refs_0_, bf16[128,2048]{1,0:T(8,128)(2,1)} %collective-permute-done.18.refs_1_, bf16[128,2048]{1,0:T(8,128)(2,1)} %collective-permute-done.19.refs_2_, ...), custom_call_target="tpu_custom_call" | custom-call | flops 2147483648 | bytes 10485760 | tf_op jit(solution)/shard_map/final/pallas_call | solution.py:159
  115.5 5.1 %all-to-all-done.1 = bf16[128,16,256]{2,1,0:T(8,128)(2,1)S(1)} async-done(((bf16[128,16,256]{2,1,0:T(8,128)(2,1)}), bf16[128,16,256]{2,1,0:T(8,128)(2,1)S(1)}, u32[]{:S(2)}, u32[]{:S(2)}) %all-to-all-start.1) | async-done | bytes 1048608 | tf_op jit(solution)/shard_map/all_to_all | solution.py:211
  121.7 6.5 %final.3 = bf16[4,2048,128]{2,1,0:T(8,128)(2,1)} custom-call(s32[48]{0:T(128)S(1)} %concatenate.7.order, bf16[128,2048]{1,0:T(8,128)(2,1)S(1)} %pad_maximum_fusion.refs_0_, bf16[128,2048]{1,0:T(8,128)(2,1)} %collective-permute-done.18.refs_1_, bf16[128,2048]{1,0:T(8,128)(2,1)} %collective-permute-done.19.refs_2_, ...), custom_call_target="tpu_custom_call", output_to_operand_aliasing={{}: (18, {})} | custom-call | flops 2147483648 | bytes 10485760 | tf_op jit(solution)/shard_map/final/pallas_call | solution.py:159
  (86 shorter events, 23.7 us)
Async XLA Ops:
  0.0 24.9 %collective-permute-start.6 = (bf16[128,2048]{1,0:T(8,128)(2,1)}, bf16[128,2048]{1,0:T(8,128)(2,1)S(1)}, u32[]{:S(2)}, u32[]{:S(2)}) collective-permute-start(bf16[128,2048]{1,0:T(8,128)(2,1)} %refs_0_.1), channel_id=1, source_target_pairs={{0,4},{1,5},{2,6},{3,7},{4,0},{5,1},{6,2},{7,3},{32,36},{33,37},{3... | collective-permute-start | bytes 1572872 | tf_op jit(solution)/shard_map/ppermute | solution.py:30
  4.4 23.9 %collective-permute-start.5 = (bf16[128,2048]{1,0:T(8,128)(2,1)}, bf16[128,2048]{1,0:T(8,128)(2,1)}, u32[]{:S(2)}, u32[]{:S(2)}) collective-permute-start(bf16[128,2048]{1,0:T(8,128)(2,1)} %refs_0_.1), channel_id=1, source_target_pairs={{0,6},{1,3},{2,0},{3,5},{4,2},{5,7},{6,4},{7,1},{32,38},{33,35},{3... | collective-permute-start | bytes 1572872 | tf_op jit(solution)/shard_map/ppermute | solution.py:30
  5.2 24.0 %collective-permute-start.4 = (bf16[128,2048]{1,0:T(8,128)(2,1)}, bf16[128,2048]{1,0:T(8,128)(2,1)}, u32[]{:S(2)}, u32[]{:S(2)}) collective-permute-start(bf16[128,2048]{1,0:T(8,128)(2,1)} %refs_0_.1), channel_id=1, source_target_pairs={{0,2},{1,7},{2,4},{3,1},{4,6},{5,3},{6,0},{7,5},{32,34},{33,39},{3... | collective-permute-start | bytes 1572872 | tf_op jit(solution)/shard_map/ppermute | solution.py:30
  7.1 16.9 %collective-permute-start = (bf16[128,2048]{1,0:T(8,128)(2,1)}, bf16[128,2048]{1,0:T(8,128)(2,1)}, u32[]{:S(2)}, u32[]{:S(2)}) collective-permute-start(bf16[128,2048]{1,0:T(8,128)(2,1)} %refs_0_.1), channel_id=1, source_target_pairs={{0,8},{1,25},{2,10},{3,27},{4,12},{5,29},{6,14},{7,31},{32,40},{33... | collective-permute-start | bytes 1572872 | tf_op jit(solution)/shard_map/ppermute | solution.py:30
  9.6 21.2 %collective-permute-start.10 = (bf16[128,2048]{1,0:T(8,128)(2,1)}, bf16[128,2048]{1,0:T(8,128)(2,1)}, u32[]{:S(2)}, u32[]{:S(2)}) collective-permute-start(bf16[128,2048]{1,0:T(8,128)(2,1)} %refs_0_.1), channel_id=1, source_target_pairs={{0,1},{1,0},{2,3},{3,2},{4,5},{5,4},{6,7},{7,6},{32,33},{33,32},{3... | collective-permute-start | bytes 1572872 | tf_op jit(solution)/shard_map/ppermute | solution.py:30
  12.8 39.7 %all-to-all-start = ((bf16[8,4,16,2048]{3,2,1,0:T(8,128)(2,1)}), bf16[8,4,16,2048]{3,2,1,0:T(8,128)(2,1)S(1)}, u32[]{:S(2)}, u32[]{:S(2)}) async-start(bf16[8,4,16,2048]{3,2,1,0:T(8,128)(2,1)} %bitcast.40), calls=%async_computation | async-start | bytes 4194304 | tf_op jit(solution)/shard_map/all_to_all | solution.py:193
  24.0 9.3 %collective-permute-start.3 = (bf16[32,2048]{1,0:T(8,128)(2,1)S(1)}, bf16[32,2048]{1,0:T(8,128)(2,1)S(1)}, u32[]{:S(2)}, u32[]{:S(2)}) collective-permute-start(bf16[32,2048]{1,0:T(8,128)(2,1)S(1)} %constant_dynamic-slice_fusion), channel_id=1, source_target_pairs={{0,4},{1,5},{2,6},{3,7},{4,0},{5,1},{6,2},{7,3},{32,36},{33,37},{3... | collective-permute-start | bytes 393224 | tf_op jit(solution)/shard_map/ppermute | solution.py:30
  24.9 8.4 %collective-permute-start.2 = (bf16[32,2048]{1,0:T(8,128)(2,1)S(1)}, bf16[32,2048]{1,0:T(8,128)(2,1)S(1)}, u32[]{:S(2)}, u32[]{:S(2)}) collective-permute-start(bf16[32,2048]{1,0:T(8,128)(2,1)S(1)} %constant_dynamic-slice_fusion), channel_id=1, source_target_pairs={{0,6},{1,3},{2,0},{3,5},{4,2},{5,7},{6,4},{7,1},{32,38},{33,35},{3... | collective-permute-start | bytes 393224 | tf_op jit(solution)/shard_map/ppermute | solution.py:30
  30.8 17.3 %collective-permute-start.9 = (bf16[128,2048]{1,0:T(8,128)(2,1)S(1)}, bf16[128,2048]{1,0:T(8,128)(2,1)}, u32[]{:S(2)}, u32[]{:S(2)}) collective-permute-start(bf16[128,2048]{1,0:T(8,128)(2,1)S(1)} %collective-permute-done.6.refs_3_), channel_id=1, source_target_pairs={{0,8},{1,25},{2,10},{3,27},{4,12},{5,29},{6,14},{7,31},{32,40},{33... | collective-permute-start | bytes 1572872 | tf_op jit(solution)/shard_map/ppermute | solution.py:30
  33.4 18.2 %collective-permute-start.12 = (bf16[128,2048]{1,0:T(8,128)(2,1)}, bf16[128,2048]{1,0:T(8,128)(2,1)S(1)}, u32[]{:S(2)}, u32[]{:S(2)}) collective-permute-start(bf16[128,2048]{1,0:T(8,128)(2,1)} %collective-permute-done.5.refs_2_), channel_id=1, source_target_pairs={{0,1},{1,0},{2,3},{3,2},{4,5},{5,4},{6,7},{7,6},{32,33},{33,32},{3... | collective-permute-start | bytes 1572872 | tf_op jit(solution)/shard_map/ppermute | solution.py:30
  33.4 18.3 %collective-permute-start.8 = (bf16[128,2048]{1,0:T(8,128)(2,1)}, bf16[128,2048]{1,0:T(8,128)(2,1)}, u32[]{:S(2)}, u32[]{:S(2)}) collective-permute-start(bf16[128,2048]{1,0:T(8,128)(2,1)} %collective-permute-done.refs_4_), channel_id=1, source_target_pairs={{0,6},{1,3},{2,0},{3,5},{4,2},{5,7},{6,4},{7,1},{32,38},{33,35},{3... | collective-permute-start | bytes 1572872 | tf_op jit(solution)/shard_map/ppermute | solution.py:30
  34.4 17.7 %collective-permute-start.7 = (bf16[128,2048]{1,0:T(8,128)(2,1)}, bf16[128,2048]{1,0:T(8,128)(2,1)}, u32[]{:S(2)}, u32[]{:S(2)}) collective-permute-start(bf16[128,2048]{1,0:T(8,128)(2,1)} %collective-permute-done.refs_4_), channel_id=1, source_target_pairs={{0,2},{1,7},{2,4},{3,1},{4,6},{5,3},{6,0},{7,5},{32,34},{33,39},{3... | collective-permute-start | bytes 1572872 | tf_op jit(solution)/shard_map/ppermute | solution.py:30
  37.1 19.0 %collective-permute-start.14 = (bf16[128,2048]{1,0:T(8,128)(2,1)}, bf16[128,2048]{1,0:T(8,128)(2,1)}, u32[]{:S(2)}, u32[]{:S(2)}) collective-permute-start(bf16[128,2048]{1,0:T(8,128)(2,1)} %collective-permute-done.refs_4_), channel_id=1, source_target_pairs={{0,1},{1,0},{2,3},{3,2},{4,5},{5,4},{6,7},{7,6},{32,33},{33,32},{3... | collective-permute-start | bytes 1572872 | tf_op jit(solution)/shard_map/ppermute | solution.py:30
  56.1 21.4 %collective-permute-start.21 = (bf16[128,2048]{1,0:T(8,128)(2,1)S(1)}, bf16[128,2048]{1,0:T(8,128)(2,1)}, u32[]{:S(2)}, u32[]{:S(2)}) collective-permute-start(bf16[128,2048]{1,0:T(8,128)(2,1)S(1)} %pad_maximum_fusion.refs_0_), channel_id=1, source_target_pairs={{0,40},{1,121},{2,42},{3,123},{4,44},{5,125},{6,46},{7,127},{32,72... | collective-permute-start | bytes 1572872 | tf_op jit(solution)/shard_map/ppermute | solution.py:30
  58.6 18.9 %collective-permute-start.20 = (bf16[128,2048]{1,0:T(8,128)(2,1)S(1)}, bf16[128,2048]{1,0:T(8,128)(2,1)}, u32[]{:S(2)}, u32[]{:S(2)}) collective-permute-start(bf16[128,2048]{1,0:T(8,128)(2,1)S(1)} %pad_maximum_fusion.refs_0_), channel_id=1, source_target_pairs={{0,8},{1,25},{2,10},{3,27},{4,12},{5,29},{6,14},{7,31},{32,40},{33... | collective-permute-start | bytes 1572872 | tf_op jit(solution)/shard_map/ppermute | solution.py:30
  59.0 20.4 %collective-permute-start.19 = (bf16[128,2048]{1,0:T(8,128)(2,1)S(1)}, bf16[128,2048]{1,0:T(8,128)(2,1)}, u32[]{:S(2)}, u32[]{:S(2)}) collective-permute-start(bf16[128,2048]{1,0:T(8,128)(2,1)S(1)} %pad_maximum_fusion.refs_0_), channel_id=1, source_target_pairs={{0,96},{1,33},{2,98},{3,35},{4,100},{5,37},{6,102},{7,39},{32,0},{... | collective-permute-start | bytes 1572872 | tf_op jit(solution)/shard_map/ppermute | solution.py:30
  59.0 20.4 %collective-permute-start.18 = (bf16[128,2048]{1,0:T(8,128)(2,1)S(1)}, bf16[128,2048]{1,0:T(8,128)(2,1)}, u32[]{:S(2)}, u32[]{:S(2)}) collective-permute-start(bf16[128,2048]{1,0:T(8,128)(2,1)S(1)} %pad_maximum_fusion.refs_0_), channel_id=1, source_target_pairs={{0,32},{1,97},{2,34},{3,99},{4,36},{5,101},{6,38},{7,103},{32,64},... | collective-permute-start | bytes 1572872 | tf_op jit(solution)/shard_map/ppermute | solution.py:30
  70.2 26.5 %all-to-all-start.2 = ((bf16[128,16,256]{2,1,0:T(8,128)(2,1)}), bf16[128,16,256]{2,1,0:T(8,128)(2,1)S(1)}, u32[]{:S(2)}, u32[]{:S(2)}) async-start(bf16[128,16,256]{2,1,0:T(8,128)(2,1)} %bitcast.42), calls=%async_computation.2 | async-start | bytes 2097152 | tf_op jit(solution)/shard_map/all_to_all | solution.py:211
  88.2 13.1 %collective-permute-start.29 = (bf16[128,2048]{1,0:T(8,128)(2,1)}, bf16[128,2048]{1,0:T(8,128)(2,1)}, u32[]{:S(2)}, u32[]{:S(2)}) collective-permute-start(bf16[128,2048]{1,0:T(8,128)(2,1)} %collective-permute-done.20.refs_4_), channel_id=1, source_target_pairs={{0,1},{1,0},{2,3},{3,2},{4,5},{5,4},{6,7},{7,6},{32,33},{33,32},{3... | collective-permute-start | bytes 1572872 | tf_op jit(solution)/shard_map/ppermute | solution.py:30
  88.3 14.3 %collective-permute-start.26 = (bf16[128,2048]{1,0:T(8,128)(2,1)}, bf16[128,2048]{1,0:T(8,128)(2,1)}, u32[]{:S(2)}, u32[]{:S(2)}) collective-permute-start(bf16[128,2048]{1,0:T(8,128)(2,1)} %collective-permute-done.18.refs_1_), channel_id=1, source_target_pairs={{0,1},{1,0},{2,3},{3,2},{4,5},{5,4},{6,7},{7,6},{32,33},{33,32},{3... | collective-permute-start | bytes 1572872 | tf_op jit(solution)/shard_map/ppermute | solution.py:30
  88.7 14.0 %collective-permute-start.22 = (bf16[128,2048]{1,0:T(8,128)(2,1)}, bf16[128,2048]{1,0:T(8,128)(2,1)}, u32[]{:S(2)}, u32[]{:S(2)}) collective-permute-start(bf16[128,2048]{1,0:T(8,128)(2,1)} %collective-permute-done.18.refs_1_), channel_id=1, source_target_pairs={{0,32},{1,97},{2,34},{3,99},{4,36},{5,101},{6,38},{7,103},{32,64},... | collective-permute-start | bytes 1572872 | tf_op jit(solution)/shard_map/ppermute | solution.py:30
  89.1 14.0 %collective-permute-start.23 = (bf16[128,2048]{1,0:T(8,128)(2,1)}, bf16[128,2048]{1,0:T(8,128)(2,1)}, u32[]{:S(2)}, u32[]{:S(2)}) collective-permute-start(bf16[128,2048]{1,0:T(8,128)(2,1)} %collective-permute-done.19.refs_2_), channel_id=1, source_target_pairs={{0,8},{1,25},{2,10},{3,27},{4,12},{5,29},{6,14},{7,31},{32,40},{33... | collective-permute-start | bytes 1572872 | tf_op jit(solution)/shard_map/ppermute | solution.py:30
  92.3 11.4 %collective-permute-start.24 = (bf16[128,2048]{1,0:T(8,128)(2,1)}, bf16[128,2048]{1,0:T(8,128)(2,1)}, u32[]{:S(2)}, u32[]{:S(2)}) collective-permute-start(bf16[128,2048]{1,0:T(8,128)(2,1)} %collective-permute-done.21.refs_5_), channel_id=1, source_target_pairs={{0,32},{1,97},{2,34},{3,99},{4,36},{5,101},{6,38},{7,103},{32,64},... | collective-permute-start | bytes 1572872 | tf_op jit(solution)/shard_map/ppermute | solution.py:30
  96.7 23.9 %all-to-all-start.1 = ((bf16[128,16,256]{2,1,0:T(8,128)(2,1)}), bf16[128,16,256]{2,1,0:T(8,128)(2,1)S(1)}, u32[]{:S(2)}, u32[]{:S(2)}) async-start(bf16[128,16,256]{2,1,0:T(8,128)(2,1)} %bitcast.41), calls=%async_computation.1 | async-start | bytes 2097152 | tf_op jit(solution)/shard_map/all_to_all | solution.py:211
  (23 other events, 140.8 us)

commit v6 on v5

--- a/solution.py
+++ b/solution.py
@@ -11,7 +11,7 @@
 BF = jnp.bfloat16
 F32 = jnp.float32
 HALF, FINAL = 56, 16
-SLICES = 2
+SLICES = 1
 
 
 def place(x, y, z, core):

time: 129 us -> 131 us (1.016)
  Pallas kernels: 29.9 us -> 33.1 us
  waiting for transfers between devices: 26.2 us -> 23.7 us
    pallas_call x2, Pallas kernels: 15.7 us -> 17.5 us  [half_rotate(): pl.pallas_call(half_kernel, grid_spec=pltpu.PrefetchScalarGridSpec(num_sc...]
    all_to_all x2, waiting for transfers between devices: 9.04 us -> 7.5 us  [exchange(): lax.all_to_all(half.reshape(128, 16, 256), AXES, 0, 0, tiled=True)]
    pallas_call x2, Pallas kernels: 12.9 us -> 14.3 us  [final_rotate(): pl.pallas_call(final_kernel, grid_spec=pltpu.PrefetchScalarGridSpec(num_s...]
  transfers between devices with their start and end apart: 36 -> 36, of which waited for: 9 -> 9; matrix products, arithmetic and copies ran while one was open for 7% -> 7% of each run, Pallas kernels for 18% -> 20%
where the time goes in v6:
time: 131 us; the launch traced here: 130 us
  starting transfers between devices  57.7 us (44%)
  Pallas kernels  33.1 us (25%)
  waiting for transfers between devices  23.7 us (18%)
  local copies, waits for them, and re-layouts  9.52 us (7%)
  matrix products  5.4 us (4%)
    ppermute x33, starting transfers between devices, send(): return lax.ppermute(value, AXES, moves)  40 us
    pallas_call x2, Pallas kernels, half_rotate(): pl.pallas_call(half_kernel, grid_spec=pltpu.PrefetchScalarGridSpec(num_sc...  17.5 us
    ppermute x33, waiting for transfers between devices, send(): return lax.ppermute(value, AXES, moves)  16.2 us
    pallas_call x2, Pallas kernels, final_rotate(): pl.pallas_call(final_kernel, grid_spec=pltpu.PrefetchScalarGridSpec(num_s...  14.3 us
    all_to_all x2, starting transfers between devices, exchange(): lax.all_to_all(half.reshape(128, 16, 256), AXES, 0, 0, tiled=True)  11.9 us
    all_to_all x2, waiting for transfers between devices, exchange(): lax.all_to_all(half.reshape(128, 16, 256), AXES, 0, 0, tiled=True)  7.5 us
    all_to_all x1, starting transfers between devices, shards(): pieces = lax.all_to_all(pieces, PAIR, 0, 0, tiled=True).reshape(512, 2048)  5.8 us
    unnamed x22, local copies, waits for them, and re-layouts  5.54 us
  transfers between devices with their start and end apart: 36, of which 9 were waited for; matrix products, arithmetic and copies ran while one was open for 7% of the time, Pallas kernels for 20%

profile of v6, /device:TPU:1, one launch (start us, length us, event | category | flops | bytes accessed | tf_op | source)
XLA Modules:
  0.0 129.9 jit_solution(13323044405626602915)
XLA Ops:
  0.0 4.4 %collective-permute-start.6 = (bf16[128,2048]{1,0:T(8,128)(2,1)}, bf16[128,2048]{1,0:T(8,128)(2,1)S(1)}, u32[]{:S(2)}, u32[]{:S(2)}) collective-permute-start(bf16[128,2048]{1,0:T(8,128)(2,1)} %refs_0_.1), channel_id=1, source_target_pairs={{0,4},{1,5},{2,6},{3,7},{4,0},{5,1},{6,2},{7,3},{32,36},{33,37},{3... | collective-permute-start | bytes 1572872 | tf_op jit(solution)/shard_map/ppermute | solution.py:30
  5.2 1.9 %collective-permute-start.4 = (bf16[128,2048]{1,0:T(8,128)(2,1)}, bf16[128,2048]{1,0:T(8,128)(2,1)}, u32[]{:S(2)}, u32[]{:S(2)}) collective-permute-start(bf16[128,2048]{1,0:T(8,128)(2,1)} %refs_0_.1), channel_id=1, source_target_pairs={{0,2},{1,7},{2,4},{3,1},{4,6},{5,3},{6,0},{7,5},{32,34},{33,39},{3... | collective-permute-start | bytes 1572872 | tf_op jit(solution)/shard_map/ppermute | solution.py:30
  7.1 2.5 %collective-permute-start = (bf16[128,2048]{1,0:T(8,128)(2,1)}, bf16[128,2048]{1,0:T(8,128)(2,1)}, u32[]{:S(2)}, u32[]{:S(2)}) collective-permute-start(bf16[128,2048]{1,0:T(8,128)(2,1)} %refs_0_.1), channel_id=1, source_target_pairs={{0,8},{1,25},{2,10},{3,27},{4,12},{5,29},{6,14},{7,31},{32,40},{33... | collective-permute-start | bytes 1572872 | tf_op jit(solution)/shard_map/ppermute | solution.py:30
  9.6 3.2 %copy.10 = bf16[4,8,16,2048]{3,2,0,1:T(8,128)(2,1)} copy(bf16[4,8,16,2048]{3,2,1,0:T(8,128)(2,1)} %bitcast.43) | data formatting | bytes 4194304 | tf_op jit(solution)/shard_map/reshape | solution.py:192
  12.8 5.8 %all-to-all-start = ((bf16[8,4,16,2048]{3,2,1,0:T(8,128)(2,1)}), bf16[8,4,16,2048]{3,2,1,0:T(8,128)(2,1)S(1)}, u32[]{:S(2)}, u32[]{:S(2)}) async-start(bf16[8,4,16,2048]{3,2,1,0:T(8,128)(2,1)} %bitcast.40), calls=%async_computation | async-start | bytes 4194304 | tf_op jit(solution)/shard_map/all_to_all | solution.py:193
  18.6 3.8 %fusion.3 = f32[32,1024]{1,0:T(8,128)S(1)} fusion(f32[1024,1024]{1,0:T(8,128)} %param.9, s32[32]{0:T(128)S(1)} %copy-done.9), kind=kOutput, calls=%fused_computation.12 | convolution fusion | flops 402685952 | bytes 4325504 | tf_op jit(solution)/shard_map/dot_general | solution.py:51
  26.4 2.0 %collective-permute-done.5.refs_2_ = bf16[128,2048]{1,0:T(8,128)(2,1)} collective-permute-done((bf16[128,2048]{1,0:T(8,128)(2,1)}, bf16[128,2048]{1,0:T(8,128)(2,1)}, u32[]{:S(2)}, u32[]{:S(2)}) %collective-permute-start.5) | collective-permute-done | bytes 524320 | tf_op jit(solution)/shard_map/ppermute | solution.py:30
  29.1 1.6 %collective-permute-start.13 = (bf16[128,2048]{1,0:T(8,128)(2,1)S(1)}, bf16[128,2048]{1,0:T(8,128)(2,1)S(1)}, u32[]{:S(2)}, u32[]{:S(2)}) collective-permute-start(bf16[128,2048]{1,0:T(8,128)(2,1)S(1)} %collective-permute-done.6.refs_3_), channel_id=1, source_target_pairs={{0,1},{1,0},{2,3},{3,2},{4,5},{5,4},{6,7},{7,6},{32,33},{33,32},{3... | collective-permute-start | bytes 1572872 | tf_op jit(solution)/shard_map/ppermute | solution.py:30
  30.8 2.6 %collective-permute-start.9 = (bf16[128,2048]{1,0:T(8,128)(2,1)S(1)}, bf16[128,2048]{1,0:T(8,128)(2,1)}, u32[]{:S(2)}, u32[]{:S(2)}) collective-permute-start(bf16[128,2048]{1,0:T(8,128)(2,1)S(1)} %collective-permute-done.6.refs_3_), channel_id=1, source_target_pairs={{0,8},{1,25},{2,10},{3,27},{4,12},{5,29},{6,14},{7,31},{32,40},{33... | collective-permute-start | bytes 1572872 | tf_op jit(solution)/shard_map/ppermute | solution.py:30
  34.4 2.7 %collective-permute-start.7 = (bf16[128,2048]{1,0:T(8,128)(2,1)}, bf16[128,2048]{1,0:T(8,128)(2,1)}, u32[]{:S(2)}, u32[]{:S(2)}) collective-permute-start(bf16[128,2048]{1,0:T(8,128)(2,1)} %collective-permute-done.refs_4_), channel_id=1, source_target_pairs={{0,2},{1,7},{2,4},{3,1},{4,6},{5,3},{6,0},{7,5},{32,34},{33,39},{3... | collective-permute-start | bytes 1572872 | tf_op jit(solution)/shard_map/ppermute | solution.py:30
  37.8 10.3 %collective-permute-done.9.refs_7_ = bf16[128,2048]{1,0:T(8,128)(2,1)} collective-permute-done((bf16[128,2048]{1,0:T(8,128)(2,1)S(1)}, bf16[128,2048]{1,0:T(8,128)(2,1)}, u32[]{:S(2)}, u32[]{:S(2)}) %collective-permute-start.9) | collective-permute-done | bytes 524320 | tf_op jit(solution)/shard_map/ppermute | solution.py:30
  48.1 3.5 %collective-permute-start.11 = (bf16[128,2048]{1,0:T(8,128)(2,1)}, bf16[128,2048]{1,0:T(8,128)(2,1)}, u32[]{:S(2)}, u32[]{:S(2)}) collective-permute-start(bf16[128,2048]{1,0:T(8,128)(2,1)} %collective-permute-done.4.refs_1_), channel_id=1, source_target_pairs={{0,1},{1,0},{2,3},{3,2},{4,5},{5,4},{6,7},{7,6},{32,33},{33,32},{3... | collective-permute-start | bytes 1572872 | tf_op jit(solution)/shard_map/ppermute | solution.py:30
  56.1 2.5 %collective-permute-start.21 = (bf16[128,2048]{1,0:T(8,128)(2,1)S(1)}, bf16[128,2048]{1,0:T(8,128)(2,1)}, u32[]{:S(2)}, u32[]{:S(2)}) collective-permute-start(bf16[128,2048]{1,0:T(8,128)(2,1)S(1)} %pad_maximum_fusion.refs_0_), channel_id=1, source_target_pairs={{0,40},{1,121},{2,42},{3,123},{4,44},{5,125},{6,46},{7,127},{32,72... | collective-permute-start | bytes 1572872 | tf_op jit(solution)/shard_map/ppermute | solution.py:30
  59.0 2.7 %collective-permute-start.18 = (bf16[128,2048]{1,0:T(8,128)(2,1)S(1)}, bf16[128,2048]{1,0:T(8,128)(2,1)}, u32[]{:S(2)}, u32[]{:S(2)}) collective-permute-start(bf16[128,2048]{1,0:T(8,128)(2,1)S(1)} %pad_maximum_fusion.refs_0_), channel_id=1, source_target_pairs={{0,32},{1,97},{2,34},{3,99},{4,36},{5,101},{6,38},{7,103},{32,64},... | collective-permute-start | bytes 1572872 | tf_op jit(solution)/shard_map/ppermute | solution.py:30
  62.4 8.7 %half.3 = bf16[8,16,16,256]{3,2,1,0:T(8,128)(2,1)} custom-call(s32[16]{0:T(128)} %stack.117.order, bf16[8,4,16,2048]{3,2,1,0:T(8,128)(2,1)} %bitcast.35, bf16[128,2048]{1,0:T(8,128)(2,1)} %refs_0_.1, bf16[128,2048]{1,0:T(8,128)(2,1)} %collective-permute-done.4.refs_1_, bf16[128,2048]{1,0:T(8,128)(2,1)} %collective-permute-done.5.refs_2_, ...), custom_call_target="tpu_custom_call" | custom-call | tf_op jit(solution)/shard_map/half/pallas_call | solution.py:109
  71.1 7.3 %all-to-all-start.2 = ((bf16[128,16,256]{2,1,0:T(8,128)(2,1)}), bf16[128,16,256]{2,1,0:T(8,128)(2,1)S(1)}, u32[]{:S(2)}, u32[]{:S(2)}) async-start(bf16[128,16,256]{2,1,0:T(8,128)(2,1)} %bitcast.42), calls=%async_computation.2 | async-start | bytes 2097152 | tf_op jit(solution)/shard_map/all_to_all | solution.py:211
  79.4 8.7 %half.2 = bf16[8,16,16,256]{3,2,1,0:T(8,128)(2,1)} custom-call(s32[16]{0:T(128)} %stack.117.order, bf16[8,4,16,2048]{3,2,1,0:T(8,128)(2,1)} %bitcast.36, bf16[128,2048]{1,0:T(8,128)(2,1)} %refs_0_.1, bf16[128,2048]{1,0:T(8,128)(2,1)} %collective-permute-done.4.refs_1_, bf16[128,2048]{1,0:T(8,128)(2,1)} %collective-permute-done.5.refs_2_, ...), custom_call_target="tpu_custom_call" | custom-call | tf_op jit(solution)/shard_map/half/pallas_call | solution.py:109
  90.8 2.4 %collective-permute-start.23 = (bf16[128,2048]{1,0:T(8,128)(2,1)}, bf16[128,2048]{1,0:T(8,128)(2,1)}, u32[]{:S(2)}, u32[]{:S(2)}) collective-permute-start(bf16[128,2048]{1,0:T(8,128)(2,1)} %collective-permute-done.19.refs_2_), channel_id=1, source_target_pairs={{0,8},{1,25},{2,10},{3,27},{4,12},{5,29},{6,14},{7,31},{32,40},{33... | collective-permute-start | bytes 1572872 | tf_op jit(solution)/shard_map/ppermute | solution.py:30
  94.6 3.0 %all-to-all-done.2 = bf16[128,16,256]{2,1,0:T(8,128)(2,1)S(1)} async-done(((bf16[128,16,256]{2,1,0:T(8,128)(2,1)}), bf16[128,16,256]{2,1,0:T(8,128)(2,1)S(1)}, u32[]{:S(2)}, u32[]{:S(2)}) %all-to-all-start.2) | async-done | bytes 1048608 | tf_op jit(solution)/shard_map/all_to_all | solution.py:211
  97.6 4.6 %all-to-all-start.1 = ((bf16[128,16,256]{2,1,0:T(8,128)(2,1)}), bf16[128,16,256]{2,1,0:T(8,128)(2,1)S(1)}, u32[]{:S(2)}, u32[]{:S(2)}) async-start(bf16[128,16,256]{2,1,0:T(8,128)(2,1)} %bitcast.41), calls=%async_computation.1 | async-start | bytes 2097152 | tf_op jit(solution)/shard_map/all_to_all | solution.py:211
  104.5 2.4 %collective-permute-start.32 = (bf16[128,2048]{1,0:T(8,128)(2,1)}, bf16[128,2048]{1,0:T(8,128)(2,1)}, u32[]{:S(2)}, u32[]{:S(2)}) collective-permute-start(bf16[128,2048]{1,0:T(8,128)(2,1)} %collective-permute-done.24.refs_7_), channel_id=1, source_target_pairs={{0,1},{1,0},{2,3},{3,2},{4,5},{5,4},{6,7},{7,6},{32,33},{33,32},{3... | collective-permute-start | bytes 1572872 | tf_op jit(solution)/shard_map/ppermute | solution.py:30
  109.9 7.2 %final.2.refs_17_ = bf16[4,2048,128]{2,1,0:T(8,128)(2,1)} custom-call(s32[48]{0:T(128)S(1)} %concatenate.7.order, bf16[128,2048]{1,0:T(8,128)(2,1)S(1)} %pad_maximum_fusion.refs_0_, bf16[128,2048]{1,0:T(8,128)(2,1)} %collective-permute-done.18.refs_1_, bf16[128,2048]{1,0:T(8,128)(2,1)} %collective-permute-done.19.refs_2_, ...), custom_call_target="tpu_custom_call" | custom-call | flops 2147483648 | bytes 10485760 | tf_op jit(solution)/shard_map/final/pallas_call | solution.py:159
  117.0 4.5 %all-to-all-done.1 = bf16[128,16,256]{2,1,0:T(8,128)(2,1)S(1)} async-done(((bf16[128,16,256]{2,1,0:T(8,128)(2,1)}), bf16[128,16,256]{2,1,0:T(8,128)(2,1)S(1)}, u32[]{:S(2)}, u32[]{:S(2)}) %all-to-all-start.1) | async-done | bytes 1048608 | tf_op jit(solution)/shard_map/all_to_all | solution.py:211
  122.6 7.2 %final.3 = bf16[4,2048,128]{2,1,0:T(8,128)(2,1)} custom-call(s32[48]{0:T(128)S(1)} %concatenate.7.order, bf16[128,2048]{1,0:T(8,128)(2,1)S(1)} %pad_maximum_fusion.refs_0_, bf16[128,2048]{1,0:T(8,128)(2,1)} %collective-permute-done.18.refs_1_, bf16[128,2048]{1,0:T(8,128)(2,1)} %collective-permute-done.19.refs_2_, ...), custom_call_target="tpu_custom_call", output_to_operand_aliasing={{}: (18, {})} | custom-call | flops 2147483648 | bytes 10485760 | tf_op jit(solution)/shard_map/final/pallas_call | solution.py:159
  (86 shorter events, 23.8 us)
Async XLA Ops:
  0.0 24.9 %collective-permute-start.6 = (bf16[128,2048]{1,0:T(8,128)(2,1)}, bf16[128,2048]{1,0:T(8,128)(2,1)S(1)}, u32[]{:S(2)}, u32[]{:S(2)}) collective-permute-start(bf16[128,2048]{1,0:T(8,128)(2,1)} %refs_0_.1), channel_id=1, source_target_pairs={{0,4},{1,5},{2,6},{3,7},{4,0},{5,1},{6,2},{7,3},{32,36},{33,37},{3... | collective-permute-start | bytes 1572872 | tf_op jit(solution)/shard_map/ppermute | solution.py:30
  4.4 23.9 %collective-permute-start.5 = (bf16[128,2048]{1,0:T(8,128)(2,1)}, bf16[128,2048]{1,0:T(8,128)(2,1)}, u32[]{:S(2)}, u32[]{:S(2)}) collective-permute-start(bf16[128,2048]{1,0:T(8,128)(2,1)} %refs_0_.1), channel_id=1, source_target_pairs={{0,6},{1,3},{2,0},{3,5},{4,2},{5,7},{6,4},{7,1},{32,38},{33,35},{3... | collective-permute-start | bytes 1572872 | tf_op jit(solution)/shard_map/ppermute | solution.py:30
  5.2 24.0 %collective-permute-start.4 = (bf16[128,2048]{1,0:T(8,128)(2,1)}, bf16[128,2048]{1,0:T(8,128)(2,1)}, u32[]{:S(2)}, u32[]{:S(2)}) collective-permute-start(bf16[128,2048]{1,0:T(8,128)(2,1)} %refs_0_.1), channel_id=1, source_target_pairs={{0,2},{1,7},{2,4},{3,1},{4,6},{5,3},{6,0},{7,5},{32,34},{33,39},{3... | collective-permute-start | bytes 1572872 | tf_op jit(solution)/shard_map/ppermute | solution.py:30
  7.1 16.9 %collective-permute-start = (bf16[128,2048]{1,0:T(8,128)(2,1)}, bf16[128,2048]{1,0:T(8,128)(2,1)}, u32[]{:S(2)}, u32[]{:S(2)}) collective-permute-start(bf16[128,2048]{1,0:T(8,128)(2,1)} %refs_0_.1), channel_id=1, source_target_pairs={{0,8},{1,25},{2,10},{3,27},{4,12},{5,29},{6,14},{7,31},{32,40},{33... | collective-permute-start | bytes 1572872 | tf_op jit(solution)/shard_map/ppermute | solution.py:30
  9.6 21.2 %collective-permute-start.10 = (bf16[128,2048]{1,0:T(8,128)(2,1)}, bf16[128,2048]{1,0:T(8,128)(2,1)}, u32[]{:S(2)}, u32[]{:S(2)}) collective-permute-start(bf16[128,2048]{1,0:T(8,128)(2,1)} %refs_0_.1), channel_id=1, source_target_pairs={{0,1},{1,0},{2,3},{3,2},{4,5},{5,4},{6,7},{7,6},{32,33},{33,32},{3... | collective-permute-start | bytes 1572872 | tf_op jit(solution)/shard_map/ppermute | solution.py:30
  12.8 39.7 %all-to-all-start = ((bf16[8,4,16,2048]{3,2,1,0:T(8,128)(2,1)}), bf16[8,4,16,2048]{3,2,1,0:T(8,128)(2,1)S(1)}, u32[]{:S(2)}, u32[]{:S(2)}) async-start(bf16[8,4,16,2048]{3,2,1,0:T(8,128)(2,1)} %bitcast.40), calls=%async_computation | async-start | bytes 4194304 | tf_op jit(solution)/shard_map/all_to_all | solution.py:193
  24.0 9.3 %collective-permute-start.3 = (bf16[32,2048]{1,0:T(8,128)(2,1)S(1)}, bf16[32,2048]{1,0:T(8,128)(2,1)S(1)}, u32[]{:S(2)}, u32[]{:S(2)}) collective-permute-start(bf16[32,2048]{1,0:T(8,128)(2,1)S(1)} %constant_dynamic-slice_fusion), channel_id=1, source_target_pairs={{0,4},{1,5},{2,6},{3,7},{4,0},{5,1},{6,2},{7,3},{32,36},{33,37},{3... | collective-permute-start | bytes 393224 | tf_op jit(solution)/shard_map/ppermute | solution.py:30
  24.9 8.4 %collective-permute-start.2 = (bf16[32,2048]{1,0:T(8,128)(2,1)S(1)}, bf16[32,2048]{1,0:T(8,128)(2,1)S(1)}, u32[]{:S(2)}, u32[]{:S(2)}) collective-permute-start(bf16[32,2048]{1,0:T(8,128)(2,1)S(1)} %constant_dynamic-slice_fusion), channel_id=1, source_target_pairs={{0,6},{1,3},{2,0},{3,5},{4,2},{5,7},{6,4},{7,1},{32,38},{33,35},{3... | collective-permute-start | bytes 393224 | tf_op jit(solution)/shard_map/ppermute | solution.py:30
  30.8 17.3 %collective-permute-start.9 = (bf16[128,2048]{1,0:T(8,128)(2,1)S(1)}, bf16[128,2048]{1,0:T(8,128)(2,1)}, u32[]{:S(2)}, u32[]{:S(2)}) collective-permute-start(bf16[128,2048]{1,0:T(8,128)(2,1)S(1)} %collective-permute-done.6.refs_3_), channel_id=1, source_target_pairs={{0,8},{1,25},{2,10},{3,27},{4,12},{5,29},{6,14},{7,31},{32,40},{33... | collective-permute-start | bytes 1572872 | tf_op jit(solution)/shard_map/ppermute | solution.py:30
  33.4 18.2 %collective-permute-start.12 = (bf16[128,2048]{1,0:T(8,128)(2,1)}, bf16[128,2048]{1,0:T(8,128)(2,1)S(1)}, u32[]{:S(2)}, u32[]{:S(2)}) collective-permute-start(bf16[128,2048]{1,0:T(8,128)(2,1)} %collective-permute-done.5.refs_2_), channel_id=1, source_target_pairs={{0,1},{1,0},{2,3},{3,2},{4,5},{5,4},{6,7},{7,6},{32,33},{33,32},{3... | collective-permute-start | bytes 1572872 | tf_op jit(solution)/shard_map/ppermute | solution.py:30
  33.4 18.3 %collective-permute-start.8 = (bf16[128,2048]{1,0:T(8,128)(2,1)}, bf16[128,2048]{1,0:T(8,128)(2,1)}, u32[]{:S(2)}, u32[]{:S(2)}) collective-permute-start(bf16[128,2048]{1,0:T(8,128)(2,1)} %collective-permute-done.refs_4_), channel_id=1, source_target_pairs={{0,6},{1,3},{2,0},{3,5},{4,2},{5,7},{6,4},{7,1},{32,38},{33,35},{3... | collective-permute-start | bytes 1572872 | tf_op jit(solution)/shard_map/ppermute | solution.py:30
  34.4 17.7 %collective-permute-start.7 = (bf16[128,2048]{1,0:T(8,128)(2,1)}, bf16[128,2048]{1,0:T(8,128)(2,1)}, u32[]{:S(2)}, u32[]{:S(2)}) collective-permute-start(bf16[128,2048]{1,0:T(8,128)(2,1)} %collective-permute-done.refs_4_), channel_id=1, source_target_pairs={{0,2},{1,7},{2,4},{3,1},{4,6},{5,3},{6,0},{7,5},{32,34},{33,39},{3... | collective-permute-start | bytes 1572872 | tf_op jit(solution)/shard_map/ppermute | solution.py:30
  37.1 19.0 %collective-permute-start.14 = (bf16[128,2048]{1,0:T(8,128)(2,1)}, bf16[128,2048]{1,0:T(8,128)(2,1)}, u32[]{:S(2)}, u32[]{:S(2)}) collective-permute-start(bf16[128,2048]{1,0:T(8,128)(2,1)} %collective-permute-done.refs_4_), channel_id=1, source_target_pairs={{0,1},{1,0},{2,3},{3,2},{4,5},{5,4},{6,7},{7,6},{32,33},{33,32},{3... | collective-permute-start | bytes 1572872 | tf_op jit(solution)/shard_map/ppermute | solution.py:30
  56.1 22.3 %collective-permute-start.21 = (bf16[128,2048]{1,0:T(8,128)(2,1)S(1)}, bf16[128,2048]{1,0:T(8,128)(2,1)}, u32[]{:S(2)}, u32[]{:S(2)}) collective-permute-start(bf16[128,2048]{1,0:T(8,128)(2,1)S(1)} %pad_maximum_fusion.refs_0_), channel_id=1, source_target_pairs={{0,40},{1,121},{2,42},{3,123},{4,44},{5,125},{6,46},{7,127},{32,72... | collective-permute-start | bytes 1572872 | tf_op jit(solution)/shard_map/ppermute | solution.py:30
  58.6 19.8 %collective-permute-start.20 = (bf16[128,2048]{1,0:T(8,128)(2,1)S(1)}, bf16[128,2048]{1,0:T(8,128)(2,1)}, u32[]{:S(2)}, u32[]{:S(2)}) collective-permute-start(bf16[128,2048]{1,0:T(8,128)(2,1)S(1)} %pad_maximum_fusion.refs_0_), channel_id=1, source_target_pairs={{0,8},{1,25},{2,10},{3,27},{4,12},{5,29},{6,14},{7,31},{32,40},{33... | collective-permute-start | bytes 1572872 | tf_op jit(solution)/shard_map/ppermute | solution.py:30
  59.0 20.4 %collective-permute-start.19 = (bf16[128,2048]{1,0:T(8,128)(2,1)S(1)}, bf16[128,2048]{1,0:T(8,128)(2,1)}, u32[]{:S(2)}, u32[]{:S(2)}) collective-permute-start(bf16[128,2048]{1,0:T(8,128)(2,1)S(1)} %pad_maximum_fusion.refs_0_), channel_id=1, source_target_pairs={{0,96},{1,33},{2,98},{3,35},{4,100},{5,37},{6,102},{7,39},{32,0},{... | collective-permute-start | bytes 1572872 | tf_op jit(solution)/shard_map/ppermute | solution.py:30
  59.0 20.4 %collective-permute-start.18 = (bf16[128,2048]{1,0:T(8,128)(2,1)S(1)}, bf16[128,2048]{1,0:T(8,128)(2,1)}, u32[]{:S(2)}, u32[]{:S(2)}) collective-permute-start(bf16[128,2048]{1,0:T(8,128)(2,1)S(1)} %pad_maximum_fusion.refs_0_), channel_id=1, source_target_pairs={{0,32},{1,97},{2,34},{3,99},{4,36},{5,101},{6,38},{7,103},{32,64},... | collective-permute-start | bytes 1572872 | tf_op jit(solution)/shard_map/ppermute | solution.py:30
  71.1 26.5 %all-to-all-start.2 = ((bf16[128,16,256]{2,1,0:T(8,128)(2,1)}), bf16[128,16,256]{2,1,0:T(8,128)(2,1)S(1)}, u32[]{:S(2)}, u32[]{:S(2)}) async-start(bf16[128,16,256]{2,1,0:T(8,128)(2,1)} %bitcast.42), calls=%async_computation.2 | async-start | bytes 2097152 | tf_op jit(solution)/shard_map/all_to_all | solution.py:211
  89.1 13.1 %collective-permute-start.29 = (bf16[128,2048]{1,0:T(8,128)(2,1)}, bf16[128,2048]{1,0:T(8,128)(2,1)}, u32[]{:S(2)}, u32[]{:S(2)}) collective-permute-start(bf16[128,2048]{1,0:T(8,128)(2,1)} %collective-permute-done.20.refs_4_), channel_id=1, source_target_pairs={{0,1},{1,0},{2,3},{3,2},{4,5},{5,4},{6,7},{7,6},{32,33},{33,32},{3... | collective-permute-start | bytes 1572872 | tf_op jit(solution)/shard_map/ppermute | solution.py:30
  89.2 14.3 %collective-permute-start.26 = (bf16[128,2048]{1,0:T(8,128)(2,1)}, bf16[128,2048]{1,0:T(8,128)(2,1)}, u32[]{:S(2)}, u32[]{:S(2)}) collective-permute-start(bf16[128,2048]{1,0:T(8,128)(2,1)} %collective-permute-done.18.refs_1_), channel_id=1, source_target_pairs={{0,1},{1,0},{2,3},{3,2},{4,5},{5,4},{6,7},{7,6},{32,33},{33,32},{3... | collective-permute-start | bytes 1572872 | tf_op jit(solution)/shard_map/ppermute | solution.py:30
  89.6 14.0 %collective-permute-start.22 = (bf16[128,2048]{1,0:T(8,128)(2,1)}, bf16[128,2048]{1,0:T(8,128)(2,1)}, u32[]{:S(2)}, u32[]{:S(2)}) collective-permute-start(bf16[128,2048]{1,0:T(8,128)(2,1)} %collective-permute-done.18.refs_1_), channel_id=1, source_target_pairs={{0,32},{1,97},{2,34},{3,99},{4,36},{5,101},{6,38},{7,103},{32,64},... | collective-permute-start | bytes 1572872 | tf_op jit(solution)/shard_map/ppermute | solution.py:30
  90.8 13.2 %collective-permute-start.23 = (bf16[128,2048]{1,0:T(8,128)(2,1)}, bf16[128,2048]{1,0:T(8,128)(2,1)}, u32[]{:S(2)}, u32[]{:S(2)}) collective-permute-start(bf16[128,2048]{1,0:T(8,128)(2,1)} %collective-permute-done.19.refs_2_), channel_id=1, source_target_pairs={{0,8},{1,25},{2,10},{3,27},{4,12},{5,29},{6,14},{7,31},{32,40},{33... | collective-permute-start | bytes 1572872 | tf_op jit(solution)/shard_map/ppermute | solution.py:30
  94.1 10.5 %collective-permute-start.24 = (bf16[128,2048]{1,0:T(8,128)(2,1)}, bf16[128,2048]{1,0:T(8,128)(2,1)}, u32[]{:S(2)}, u32[]{:S(2)}) collective-permute-start(bf16[128,2048]{1,0:T(8,128)(2,1)} %collective-permute-done.21.refs_5_), channel_id=1, source_target_pairs={{0,32},{1,97},{2,34},{3,99},{4,36},{5,101},{6,38},{7,103},{32,64},... | collective-permute-start | bytes 1572872 | tf_op jit(solution)/shard_map/ppermute | solution.py:30
  97.6 23.9 %all-to-all-start.1 = ((bf16[128,16,256]{2,1,0:T(8,128)(2,1)}), bf16[128,16,256]{2,1,0:T(8,128)(2,1)S(1)}, u32[]{:S(2)}, u32[]{:S(2)}) async-start(bf16[128,16,256]{2,1,0:T(8,128)(2,1)} %bitcast.41), calls=%async_computation.1 | async-start | bytes 2097152 | tf_op jit(solution)/shard_map/all_to_all | solution.py:211
  (23 other events, 141.5 us)
